TPU v7x, 32 devices: a whole 2x2x4 slice. The times are simulated.
32 devices in a mesh: dp: 8 (over z, x), tensor: 4 (over y, core).
Axes of the slice: x: 2, y: 2, z: 4, core: 2. Of those that a mesh axis runs over, the one named last changes fastest.
Arguments:
- gate_act: bfloat16 [1024, 26624], P('dp', 'tensor'), may hold values from -8 to 8
- up_act: bfloat16 [1024, 26624], P('dp', 'tensor'), may hold values from -6 to 6
- down_codes: bfloat16 [26624, 16384], P('tensor', 'dp'), may hold values from -4 to 4
- down_scales: float32 [208, 128], P('tensor', 'dp'), may hold values from 0.0024514517 to 0.024514517
- grad_out: bfloat16 [1024, 16384], P('tensor', 'dp'), may hold values from -6 to 6
Outputs:
- layer_output: bfloat16 [1024, 16384], P('tensor', 'dp')
- gate_grad: bfloat16 [1024, 26624], P('dp', 'tensor')
- up_grad: bfloat16 [1024, 26624], P('dp', 'tensor')
All inputs are finite; a program needn't handle non-finite values.
Results may differ from a plain program's by a relative error of at most 0.027.
Values may be sent and summed in bfloat16 or wider, within the bound.
No kernel may reach another device: no remote copies, remote signals or barrier semaphores. Data moves between devices by JAX's collectives and lax.ppermute only.
A program may use at most 192 MiB of HBM per device.

v0:
```python
import math

import jax
import jax.numpy as jnp
from jax import lax
from jax.sharding import PartitionSpec as P

BLOCK = 128


def from_partner(value, axis, stride):
    return lax.ppermute(value, axis, [(i, i ^ 1 << stride) for i in range(lax.axis_size(axis))])


def sylvester(matrix_order):
    indices = jnp.arange(matrix_order, dtype=jnp.int32)
    common_bits = indices[:, None] & indices[None, :]
    parity = jnp.zeros((matrix_order, matrix_order), jnp.int32)
    for section_bit in range(max(matrix_order.bit_length() - 1, 0)):
        parity = parity + (common_bits >> section_bit & 1)
    return (1 - 2 * (parity % 2)).astype(jnp.float32)


def dequantize(code_block, scale_block):
    row_count, col_count = code_block.shape
    expanded = code_block.astype(jnp.float32).reshape(
        row_count // BLOCK, BLOCK, col_count // BLOCK, BLOCK
    )
    return (
        (expanded * scale_block[:, None, :, None])
        .reshape(row_count, col_count)
        .astype(jnp.bfloat16)
    )


def local_mix(values, group_size):
    row_count, col_count = values.shape
    shaped = values.reshape(row_count, col_count // BLOCK, BLOCK)
    mixed_values = jnp.einsum(
        "rbc,dc->rbd", shaped, sylvester(BLOCK), precision=lax.Precision.HIGHEST
    )
    return (mixed_values / math.sqrt(group_size * BLOCK)).reshape(row_count, col_count)


def rotate_pairs(values):
    group_size = lax.axis_size("tensor")
    position = lax.axis_index("tensor")
    current = values.astype(jnp.float32)
    for section_bit in range(group_size.bit_length() - 1):
        partner = from_partner(current.astype(jnp.bfloat16), "tensor", section_bit).astype(
            current.dtype
        )
        upper_half = position >> section_bit & 1 == 1
        current = jnp.where(upper_half, partner - current, current + partner)
    return local_mix(current, group_size).astype(jnp.bfloat16)


def rotate(values):
    return rotate_pairs(values)


def on_device(gate_act, up_act, down_codes, down_scales, grad_out):
    gate_wide = gate_act.astype(jnp.float32)
    up_wide = up_act.astype(jnp.float32)
    sigmoid_gate = jax.nn.sigmoid(gate_wide)
    silu_gate = gate_wide * sigmoid_gate
    hidden = (silu_gate * up_wide).astype(jnp.bfloat16)
    rotated = rotate(hidden)
    weight = dequantize(down_codes, down_scales)
    partial_value = jnp.dot(
        lax.all_gather(rotated, "dp", axis=0, tiled=True),
        weight,
        preferred_element_type=jnp.float32,
    )
    layer_output = lax.psum_scatter(
        partial_value.astype(jnp.bfloat16), "tensor", scatter_dimension=0, tiled=True
    )
    grad_rows = lax.all_gather(grad_out, "tensor", axis=0, tiled=True)
    grad_rotated = lax.psum_scatter(
        lax.dot_general(
            grad_rows, weight, (((1,), (1,)), ((), ())), preferred_element_type=jnp.float32
        ).astype(jnp.bfloat16),
        "dp",
        scatter_dimension=0,
        tiled=True,
    )
    grad_hidden = rotate(grad_rotated).astype(jnp.float32)
    up_grad = (grad_hidden * silu_gate).astype(jnp.bfloat16)
    gate_grad = (
        grad_hidden * up_wide * sigmoid_gate * (1.0 + gate_wide * (1.0 - sigmoid_gate))
    ).astype(jnp.bfloat16)
    return (layer_output, gate_grad, up_grad)


def solution(mesh):
    return jax.shard_map(
        on_device,
        mesh=mesh,
        in_specs=(
            P("dp", "tensor"),
            P("dp", "tensor"),
            P("tensor", "dp"),
            P("tensor", "dp"),
            P("tensor", "dp"),
        ),
        out_specs=(P("tensor", "dp"), P("dp", "tensor"), P("dp", "tensor")),
        check_vma=False,
    )
```

profile of v0, /device:TPU:0, one launch (start us, length us, event | category | flops | bytes accessed | tf_op | source)
XLA Modules:
  0.0 751.3 jit_solution(5088303032109234207)
XLA Ops:
  8.7 38.0 %all-gather.5.cloned.1.call-done = bf16[1024,2048]{1,0:T(8,128)(2,1)} async-done(((bf16[256,2048]{1,0:T(8,128)(2,1)}), bf16[1024,2048]{1,0:T(8,128)(2,1)}) %all-gather.5.cloned.1.call-update) | async-done | bytes 4194320 | tf_op jit(solution)/shard_map/all_gather | solution.py:78
  46.8 17.4 %mul.41 = f32[52,128,16,128]{3,2,1,0:T(8,128)} broadcast(f32[52,16]{1,0:T(8,128)S(1)} %copy.18), dimensions={0,2} | broadcast | bytes 54529280 | tf_op jit(solution)/shard_map/mul | solution.py:30
  64.2 52.7 %convert_bitcast_fusion = bf16[1024,6656]{0,1:T(8,128)(2,1)} fusion(bf16[1024,2048]{1,0:T(8,128)(2,1)} %all-gather.5.cloned.1.call-done, f32[832,8,16,128]{3,2,1,0:T(8,128)} %bitcast.30, bf16[6656,2048]{1,0:T(8,128)(2,1)} %param.7), kind=kOutput, calls=%fused_computation.2 | convolution fusion | flops 27964997632 | bytes 99614720 | tf_op jit(solution)/shard_map/dot_general | solution.py:80
  116.8 17.5 %copy.24 = bf16[1024,6656]{1,0:T(8,128)(2,1)} copy(bf16[1024,6656]{0,1:T(8,128)(2,1)} %convert_bitcast_fusion) | data formatting | bytes 27262976
  134.6 221.7 %reduce-scatter.7.cloned.1.call-done = bf16[128,6656]{1,0:T(8,128)(2,1)} async-done(((bf16[1024,6656]{1,0:T(8,128)(2,1)}), bf16[128,6656]{1,0:T(8,128)(2,1)}) %reduce-scatter.7.cloned.1.call-update) | async-done | bytes 1703952
  356.3 3.0 copy.25
  359.4 3.6 collective-permute-done.2
  363.0 1.8 fusion.14
  364.8 1.5 collective-permute-start.3
  366.3 3.8 copy.15
  370.1 3.8 copy.16
  373.8 30.5 %collective-permute-done.3 = bf16[128,6656]{0,1:T(8,128)(2,1)} collective-permute-done((bf16[128,6656]{0,1:T(8,128)(2,1)}, bf16[128,6656]{0,1:T(8,128)(2,1)}, u32[]{:S(2)}, u32[]{:S(2)}) %collective-permute-start.3) | collective-permute-done | bytes 1703968 | tf_op jit(solution)/shard_map/ppermute | solution.py:12
  404.4 2.4 fusion.5
  406.8 3.4 multiply_convert_fusion
  410.3 2.2 fusion.9
  412.5 3.6 collective-permute-done
  416.8 1.6 collective-permute-start.1
  418.3 37.8 %collective-permute-done.1 = bf16[128,6656]{0,1:T(8,128)(2,1)S(1)} collective-permute-done((bf16[128,6656]{0,1:T(8,128)(2,1)S(1)}, bf16[128,6656]{0,1:T(8,128)(2,1)S(1)}, u32[]{:S(2)}, u32[]{:S(2)}) %collective-permute-start.1) | collective-permute-done | bytes 1703968 | tf_op jit(solution)/shard_map/ppermute | solution.py:12
  457.1 4.3 multiply_convert_fusion.1
  461.7 188.4 %all-gather.3.cloned.1.call-done = bf16[1024,6656]{0,1:T(8,128)(2,1)} async-done(((bf16[128,6656]{0,1:T(8,128)(2,1)}), bf16[1024,6656]{0,1:T(8,128)(2,1)}) %all-gather.3.cloned.1.call-update) | async-done | bytes 13631504 | tf_op jit(solution)/shard_map/all_gather | solution.py:71
  650.1 51.8 %convolution_convert_fusion = bf16[1024,2048]{1,0:T(8,128)(2,1)} fusion(bf16[1024,6656]{0,1:T(8,128)(2,1)} %all-gather.3.cloned.1.call-done, f32[832,8,16,128]{3,2,1,0:T(8,128)} %bitcast.31, bf16[6656,2048]{1,0:T(8,128)(2,1)} %param.7), kind=kOutput, calls=%fused_computation.17 | convolution fusion | flops 27960279040 | bytes 99614720 | tf_op jit(solution)/shard_map/dot_general | solution.py:70
  701.9 2.7 copy.20
  704.6 2.7 copy.21
  707.3 37.5 %reduce-scatter.5.cloned.1.call-done = bf16[256,2048]{1,0:T(8,128)(2,1)} async-done(((bf16[1024,2048]{1,0:T(8,128)(2,1)}), bf16[256,2048]{1,0:T(8,128)(2,1)}) %reduce-scatter.5.cloned.1.call-update) | async-done | bytes 1048592 | tf_op jit(solution)/shard_map/reduce_scatter | solution.py:75
  (17 shorter events, 3.9 us)
Async XLA Ops:
  7.2 39.6 %all-gather.5.cloned.1.call-start = ((), (), s32[]{:S(2)}) async-start(), calls=%async_computation.4 | async-start | bytes 5242880 | tf_op jit(solution)/shard_map/all_gather | solution.py:78
  7.9 348.4 %reduce-scatter.7.cloned.1.call-start = ((), (), s32[]{:S(2)}) async-start(), calls=%async_computation.5 | async-start | bytes 15335424
  134.4 515.7 %all-gather.3.cloned.1.call-start = ((), (), s32[]{:S(2)}) async-start(), calls=%async_computation.2 | async-start | bytes 15335424 | tf_op jit(solution)/shard_map/all_gather | solution.py:71
  359.3 3.7 collective-permute-start.2
  364.8 39.6 %collective-permute-start.3 = (bf16[128,6656]{0,1:T(8,128)(2,1)}, bf16[128,6656]{0,1:T(8,128)(2,1)}, u32[]{:S(2)}, u32[]{:S(2)}) collective-permute-start(bf16[128,6656]{0,1:T(8,128)(2,1)} %fusion.14), channel_id=1, source_target_pairs={{0,2},{1,3},{2,0},{3,1},{4,6},{5,7},{6,4},{7,5},{8,10},{9,11},{10,... | collective-permute-start | bytes 5111816 | tf_op jit(solution)/shard_map/ppermute | solution.py:12
  406.8 3.5 copy-start
  406.8 3.5 copy-start.1
  412.4 3.7 collective-permute-start
  416.8 39.3 %collective-permute-start.1 = (bf16[128,6656]{0,1:T(8,128)(2,1)S(1)}, bf16[128,6656]{0,1:T(8,128)(2,1)S(1)}, u32[]{:S(2)}, u32[]{:S(2)}) collective-permute-start(bf16[128,6656]{0,1:T(8,128)(2,1)S(1)} %fusion.15), channel_id=1, source_target_pairs={{0,2},{1,3},{2,0},{3,1},{4,6},{5,7},{6,4},{7,5},{8,10},{9,11},{10,... | collective-permute-start | bytes 5111816 | tf_op jit(solution)/shard_map/ppermute | solution.py:12
  461.5 283.3 %reduce-scatter.5.cloned.1.call-start = ((), (), s32[]{:S(2)}) async-start(), calls=%async_computation.3 | async-start | bytes 5242880 | tf_op jit(solution)/shard_map/reduce_scatter | solution.py:75
Sparse Core Ops, SparseCore 0:
  9.6 37.1 all-gather.4
  134.5 221.7 reduce-scatter.6
  461.6 188.4 all-gather.2
  702.0 42.7 reduce-scatter.4
where the time goes:
time: 752 us; the launch traced here: 751 us
  waiting for transfers between devices  562 us (75%)
  matrix products  112 us (15%)
  local copies, waits for them, and re-layouts  51.6 us (7%)
  between operations  13.9 us (2%)
  other arithmetic  8.1 us (1%)
    unnamed x5, waiting for transfers between devices  222 us
    all_gather x1, waiting for transfers between devices, on_device(): lax.all_gather(rotated, 'dp', axis=0, tiled=True)  188 us
    ppermute x4, waiting for transfers between devices, from_partner(): lax.ppermute(value, axis, [(i, i ^ 1 << stride) for i in range(lax.axis_s...  75.5 us
    dot_general x1, matrix products, on_device(): lax.dot_general(grad_rows, weight, (((1,), (1,)), ((), ())), preferred_el...  52.7 us
    dot_general x1, matrix products, on_device(): jnp.dot(lax.all_gather(rotated, 'dp', axis=0, tiled=True), weight, prefer...  51.8 us
    all_gather x1, waiting for transfers between devices, on_device(): grad_rows = lax.all_gather(grad_out, 'tensor', axis=0, tiled=True)  38 us
    reduce_scatter x1, waiting for transfers between devices, on_device(): lax.psum_scatter(partial_value.astype(jnp.bfloat16), 'tensor', scatter_di...  37.5 us
    unnamed x11, local copies, waits for them, and re-layouts  34.2 us
  transfers between devices with their start and end apart: 8, of which 8 were waited for; matrix products, arithmetic and copies ran while one was open for 2% of the time, Pallas kernels for 0%

commit v1 on v0

v1 whole, which is shorter than its diff:
```python
import math

import jax
import jax.numpy as jnp
import numpy as np
from jax import lax
from jax.experimental import pallas as pl
from jax.experimental.pallas import tpu as pltpu
from jax.sharding import PartitionSpec as P

BLOCK = 128
STREAMS = 4
VMEM_LIMIT = 40 * 1024 * 1024
F32, BF16 = jnp.float32, jnp.bfloat16


def after(value, *earlier):
    return lax.optimization_barrier((value, *earlier))[0]


def sylvester(order):
    matrix = np.ones((1, 1), np.float32)
    while matrix.shape[0] < order:
        matrix = np.block([[matrix, matrix], [matrix, -matrix]])
    return matrix


def ring_cycle(count):
    return [*range(0, count, 2), *reversed(range(1, count, 2))]


def ring_tables(count):
    cycle = ring_cycle(count)
    place = np.argsort(cycle)
    behind = [[cycle[(place[i] - r) % count] for r in range(count)] for i in range(count)]
    ahead = [[(place[j] - place[i]) % count for j in range(count)] for i in range(count)]
    return np.concatenate([behind, ahead], axis=1).astype(np.int32)


def params():
    return pltpu.CompilerParams(vmem_limit_bytes=VMEM_LIMIT)


def spec_smem():
    return pl.BlockSpec(memory_space=pltpu.SMEM)


def dequantize_into(weight_ref, codes_ref, scales_ref, row0, col0):
    for i in range(codes_ref.shape[0] // BLOCK):
        for j in range(codes_ref.shape[1] // BLOCK):
            at = (pl.ds(i * BLOCK, BLOCK), pl.ds(j * BLOCK, BLOCK))
            wide = codes_ref[at].astype(F32) * scales_ref[row0 + i, col0 + j]
            weight_ref[at] = wide.astype(BF16)


def mixed(values, mix, scale):
    high = values.astype(BF16)
    low = (values - high.astype(F32)).astype(BF16)
    total = jnp.dot(high, mix, preferred_element_type=F32) + jnp.dot(
        low, mix, preferred_element_type=F32
    )
    return (total * scale).astype(BF16)


def mix_kernel(scale, sign_ref, mix_ref, own_ref, other_ref, out_ref):
    for j in range(own_ref.shape[1] // BLOCK):
        at = (slice(None), pl.ds(j * BLOCK, BLOCK))
        values = own_ref[at].astype(F32) * sign_ref[0] + other_ref[at].astype(F32)
        out_ref[at] = mixed(values, mix_ref[...], scale)


def local_mix(own, other, sign, mix, scale):
    rows, cols = own.shape
    return pl.pallas_call(
        lambda *refs: mix_kernel(scale, *refs),
        out_shape=jax.ShapeDtypeStruct((rows, cols), BF16),
        in_specs=[spec_smem()] + [pl.BlockSpec(memory_space=pltpu.VMEM)] * 3,
        out_specs=pl.BlockSpec(memory_space=pltpu.VMEM),
        compiler_params=params(),
        cost_estimate=pl.CostEstimate(
            flops=4 * rows * cols * BLOCK, bytes_accessed=6 * rows * cols, transcendentals=0
        ),
        name="local_mix",
    )(sign, mix, own, other)


def grads_kernel(scale, tile, sign_ref, mix_ref, own_ref, other_ref, gate_ref, up_ref, *refs):
    gate_grad_ref, up_grad_ref = refs[-2:]
    for j in range(tile // BLOCK):
        at = (slice(None), pl.ds(j * BLOCK, BLOCK))
        values = own_ref[at].astype(F32) * sign_ref[0] + other_ref[at].astype(F32)
        grad = mixed(values, mix_ref[...], scale).astype(F32)
        gate = gate_ref[at].astype(F32)
        sigmoid = jax.nn.sigmoid(gate)
        up_grad_ref[at] = (grad * (gate * sigmoid)).astype(BF16)
        gate_grad_ref[at] = (
            grad * up_ref[at].astype(F32) * sigmoid * (1.0 + gate * (1.0 - sigmoid))
        ).astype(BF16)


def local_grads(own, other, sign, mix, scale, gate_act, up_act, start, tile, made):
    rows, cols = own.shape
    whole = pl.BlockSpec((rows, tile), lambda i: (0, start // tile + i))
    part = pl.BlockSpec((rows, tile), lambda i: (0, i))
    rest = [pl.BlockSpec(memory_space=pl.ANY)] * len(made)
    return pl.pallas_call(
        lambda *refs: grads_kernel(scale, tile, *refs),
        grid=(cols // tile,),
        out_shape=[jax.ShapeDtypeStruct(gate_act.shape, BF16)] * 2,
        in_specs=[
            spec_smem(),
            pl.BlockSpec((BLOCK, BLOCK), lambda i: (0, 0)),
            part,
            part,
            whole,
            whole,
            *rest,
        ],
        out_specs=[whole, whole],
        input_output_aliases={6 + k: k for k in range(len(made))},
        compiler_params=params(),
        cost_estimate=pl.CostEstimate(
            flops=4 * rows * cols * BLOCK,
            bytes_accessed=12 * rows * cols,
            transcendentals=rows * cols,
        ),
        name="local_grads",
    )(sign, mix, own, other, gate_act, up_act, *made)


def arrange_kernel(count, group_ref, table_ref, *refs):
    out_ref = refs[-1]
    rows = out_ref.shape[0] // count
    for offset, block in enumerate(refs[:-1]):
        per = block.shape[0] // rows
        for i in range(per):
            place = table_ref[count + (group_ref[0] ^ offset) * per + i]
            start = pl.multiple_of(place * rows, rows)
            out_ref[pl.ds(start, rows), :] = block[pl.ds(i * rows, rows), :]


def arrange_rows(held, group, table):
    blocks = [held[offset] for offset in range(len(held))]
    rows, cols = blocks[0].shape
    return pl.pallas_call(
        lambda *refs: arrange_kernel(table.shape[0] // 2, *refs),
        out_shape=jax.ShapeDtypeStruct((rows * len(blocks), cols), BF16),
        in_specs=[spec_smem()] * 2 + [pl.BlockSpec(memory_space=pltpu.VMEM)] * len(blocks),
        out_specs=pl.BlockSpec(memory_space=pltpu.VMEM),
        compiler_params=params(),
        cost_estimate=pl.CostEstimate(
            flops=0, bytes_accessed=4 * rows * cols * len(blocks), transcendentals=0
        ),
        name="arrange_rows",
    )(group, table, *blocks)


def backward_kernel(row_block, scales_ref, grad_ref, codes_ref, out_ref, weight_ref):
    row0 = row_block + pl.program_id(0) * (codes_ref.shape[0] // BLOCK)
    dequantize_into(weight_ref, codes_ref, scales_ref, row0, 0)
    out_ref[...] = lax.dot_general(
        grad_ref[...], weight_ref[...], (((1,), (1,)), ((), ())), preferred_element_type=F32
    ).astype(BF16)


def backward_product(grad_rows, codes, scales, start, cols, tile):
    tokens, depth = grad_rows.shape
    return pl.pallas_call(
        lambda *refs: backward_kernel(start // BLOCK, *refs),
        grid=(cols // tile,),
        out_shape=pltpu.HBM((tokens, cols), BF16),
        in_specs=[
            spec_smem(),
            pl.BlockSpec((tokens, depth), lambda i: (0, 0)),
            pl.BlockSpec((tile, depth), lambda i: (start // tile + i, 0)),
        ],
        out_specs=pl.BlockSpec((tokens, tile), lambda i: (0, i)),
        scratch_shapes=[pltpu.VMEM((tile, depth), BF16)],
        compiler_params=params(),
        cost_estimate=pl.CostEstimate(
            flops=2 * tokens * depth * cols,
            bytes_accessed=2 * (tokens * depth + depth * cols + tokens * cols),
            transcendentals=0,
        ),
        name="backward_product",
    )(scales, grad_rows, codes)


def forward_kernel(count, row_block, has_sum, order_ref, scales_ref, *refs):
    blocks, codes_ref = refs[:count], refs[count]
    sum_ref = refs[count + 1] if has_sum else None
    out_ref, rows_ref, weight_ref = refs[-3:]
    tile = codes_ref.shape[1]

    @pl.when(pl.program_id(0) == 0)
    def _():
        for r, block in enumerate(blocks):
            size = block.shape[0]
            rows_ref[pl.ds(pl.multiple_of(order_ref[r] * size, size), size), :] = block[...]

    dequantize_into(
        weight_ref, codes_ref, scales_ref, row_block, pl.program_id(0) * (tile // BLOCK)
    )
    total = jnp.dot(rows_ref[...], weight_ref[...], preferred_element_type=F32)
    if has_sum:
        total = total + sum_ref[...]
    out_ref[...] = total.astype(out_ref.dtype)


def forward_product(blocks, order, codes, scales, start, running, out_dtype):
    size, cols = blocks[0].shape
    tokens, width = size * len(blocks), codes.shape[1]
    tile = min(256, width)
    sums = [] if running is None else [running]
    sliced = pl.BlockSpec((tokens, tile), lambda i: (0, i))
    return pl.pallas_call(
        lambda *refs: forward_kernel(len(blocks), start // BLOCK, bool(sums), *refs),
        grid=(width // tile,),
        out_shape=pltpu.HBM((tokens, width), out_dtype),
        in_specs=[
            spec_smem(),
            spec_smem(),
            *[pl.BlockSpec((size, cols), lambda i: (0, 0))] * len(blocks),
            pl.BlockSpec((pl.Element(cols), pl.Element(tile)), lambda i: (start, i * tile)),
            *[sliced] * len(sums),
        ],
        out_specs=sliced,
        scratch_shapes=[pltpu.VMEM((tokens, cols), BF16), pltpu.VMEM((cols, tile), BF16)],
        compiler_params=params(),
        cost_estimate=pl.CostEstimate(
            flops=2 * tokens * cols * width,
            bytes_accessed=2 * (tokens * cols + cols * width) + 8 * tokens * width,
            transcendentals=0,
        ),
        name="forward_product",
    )(order, scales, *blocks, codes, *sums)


def stream_columns(total, tile):
    units = total // tile
    count = min(STREAMS, units)
    sizes = sorted((units + k) // count for k in range(count))
    starts = np.cumsum([0, *sizes[:-1]])
    return [(int(a) * tile, int(b) * tile) for a, b in zip(starts, sizes)]


def on_device(gate_act, up_act, down_codes, down_scales, grad_out):
    groups, ring = lax.axis_size("tensor"), lax.axis_size("dp")
    group, member = lax.axis_index("tensor"), lax.axis_index("dp")
    bits = list(reversed(range(groups.bit_length() - 1)))
    rows, hidden_units = gate_act.shape
    tile = 256 if hidden_units % 256 == 0 else BLOCK
    streams = stream_columns(hidden_units, tile)
    cycle = ring_cycle(ring)
    half = ring // 2
    table = lax.dynamic_index_in_dim(jnp.asarray(ring_tables(ring)), member, 0, keepdims=False)

    pairs = {
        step: [(cycle[i], cycle[(i + step) % ring]) for i in range(ring)] for step in (1, -1)
    }

    def partner(value, bit):
        return lax.ppermute(value, "tensor", [(i, i ^ 1 << bit) for i in range(groups)])

    def sign(bit):
        return jnp.where(group >> bit & 1 == 1, -1.0, 1.0).astype(F32)

    def paired(own, other, bit):
        return (own.astype(F32) * sign(bit) + other.astype(F32)).astype(BF16)

    last_sign = sign(bits[-1]).reshape(1)
    mix = jnp.asarray(sylvester(BLOCK), BF16)
    scale = 1.0 / math.sqrt(groups * BLOCK)

    def reach(k, step):
        return half if (k % 2 == 0) == (step == 1) else ring - 1 - half

    def hidden(start, size):
        gate = lax.slice_in_dim(gate_act, start, start + size, axis=1).astype(F32)
        up = lax.slice_in_dim(up_act, start, start + size, axis=1).astype(F32)
        return (gate * jax.nn.sigmoid(gate) * up).astype(BF16)

    def gathered():
        held = {0: after(grad_out, token)}
        for bit in bits:
            held.update({o ^ 1 << bit: partner(value, bit) for o, value in list(held.items())})
            if bit == bits[0]:
                arrived = held[1 << bit]
        return held, arrived

    rotated = []
    token = None
    for k, (start, size) in enumerate(streams):
        if k == len(streams) // 2:
            held, token = gathered()
        own = hidden(start, size)
        if token is not None:
            own = after(own, token)
        other = token = partner(own, bits[0])
        for previous, bit in zip(bits, bits[1:]):
            own = paired(own, other, previous)
            other = partner(own, bit)
        rotated.append(local_mix(own, other, last_sign, mix, scale))
    grad_rows = arrange_rows(held, group.astype(jnp.int32).reshape(1), table)

    running = None
    for k, (start, size) in enumerate(streams):
        blocks = [rotated[k]] + [None] * (ring - 1)
        for step in (1, -1):
            moving = rotated[k]
            for hop in range(1, reach(k, step) + 1):
                moving = lax.ppermute(moving, "dp", pairs[step])
                blocks[hop * step % ring] = moving
        running = forward_product(
            blocks,
            table,
            down_codes,
            down_scales,
            start,
            running,
            BF16 if k == len(streams) - 1 else F32,
        )
    layer_output = lax.psum_scatter(running, "tensor", scatter_dimension=0, tiled=True)

    grads = []
    for k, (start, size) in enumerate(streams):
        partial = backward_product(grad_rows, down_codes, down_scales, start, size, tile)

        def term(offset):
            at = offset % ring * rows
            return lax.slice_in_dim(partial, at, at + rows, axis=0)

        total = term(0).astype(F32)
        for step in (1, -1):
            far = reach(k, step)
            moving = term(step * far)
            for hop in range(far - 1, -1, -1):
                moving = lax.ppermute(moving, "dp", pairs[step])
                if hop:
                    moving = (moving.astype(F32) + term(step * hop).astype(F32)).astype(BF16)
            total = total + moving.astype(F32)
        own = total.astype(BF16)
        other = partner(own, bits[0])
        for previous, bit in zip(bits, bits[1:]):
            own = paired(own, other, previous)
            other = partner(own, bit)
        grads = local_grads(
            own, other, last_sign, mix, scale, gate_act, up_act, start, tile, grads
        )
    gate_grad, up_grad = grads
    return (layer_output, gate_grad, up_grad)


def solution(mesh):
    return jax.shard_map(
        on_device,
        mesh=mesh,
        in_specs=(
            P("dp", "tensor"),
            P("dp", "tensor"),
            P("tensor", "dp"),
            P("tensor", "dp"),
            P("tensor", "dp"),
        ),
        out_specs=(P("tensor", "dp"), P("dp", "tensor"), P("dp", "tensor")),
        check_vma=False,
    )
```

time: 752 us -> 441 us (0.59)
  waiting for transfers between devices: 562 us -> 184 us
  Pallas kernels: 0 us -> 116 us
  matrix products: 112 us -> 0 us
  starting transfers between devices: 3.75 us -> 77.8 us
  local copies, waits for them, and re-layouts: 51.6 us -> 18.2 us
  other arithmetic: 8.1 us -> 27.4 us
    all_gather x2 -> x0, waiting for transfers between devices: 226 us -> none  [the longest x1 188 us: on_device(): lax.all_gather(rotated, 'dp', axis=0, tiled=True)]
    unnamed x5 -> x1, waiting for transfers between devices: 222 us -> 0.02 us
    pallas_call x0 -> x17, Pallas kernels: none -> 116 us  [the longest x4 53.2 us: forward_product(): pl.pallas_call(lambda *refs: forward_kernel(len(blocks), start // BLOCK,...]
    dot_general x4 -> x0, matrix products: 112 us -> none  [the longest x1 52.7 us: on_device(): lax.dot_general(grad_rows, weight, (((1,), (1,)), ((), ())), preferred_el...]
    ppermute x4 -> x75, waiting for transfers between devices: 75.5 us -> 184 us  [the longest x56 146 us: on_device(): moving = lax.ppermute(moving, 'dp', pairs[step])]
    ppermute x4 -> x75, starting transfers between devices: 3.19 us -> 77.8 us  [the longest x56 61.9 us: on_device(): moving = lax.ppermute(moving, 'dp', pairs[step])]
    reduce_scatter x1, waiting for transfers between devices: 37.5 us -> 0.01 us  [on_device(): lax.psum_scatter(running, 'tensor', scatter_dimension=0, tiled=True)]
    unnamed x11 -> x37, local copies, waits for them, and re-layouts: 34.2 us -> 9.65 us
  transfers between devices with their start and end apart: 8 -> 76, of which waited for: 8 -> 36; matrix products, arithmetic and copies ran while one was open for 2% -> 8% of each run, Pallas kernels for 0% -> 27%
where the time goes in v1:
time: 441 us; the launch traced here: 439 us
  waiting for transfers between devices  184 us (42%)
  Pallas kernels  116 us (26%)
  starting transfers between devices  77.8 us (18%)
  other arithmetic  27.4 us (6%)
  local copies, waits for them, and re-layouts  18.2 us (4%)
  between operations  14.4 us (3%)
    ppermute x56, waiting for transfers between devices, on_device(): moving = lax.ppermute(moving, 'dp', pairs[step])  146 us
    ppermute x56, starting transfers between devices, on_device(): moving = lax.ppermute(moving, 'dp', pairs[step])  61.9 us
    pallas_call x4, Pallas kernels, forward_product(): pl.pallas_call(lambda *refs: forward_kernel(len(blocks), start // BLOCK,...  53.2 us
    pallas_call x4, Pallas kernels, backward_product(): pl.pallas_call(lambda *refs: backward_kernel(start // BLOCK, *refs), grid...  46.9 us
    ppermute x19, waiting for transfers between devices, partner(): lax.ppermute(value, 'tensor', [(i, i ^ 1 << bit) for i in range(groups)])  38.1 us
    convert_element_type x12, other arithmetic, on_device(): moving = (moving.astype(F32) + term(step * hop).astype(F32)).astype(BF16)  16.1 us
    ppermute x19, starting transfers between devices, partner(): lax.ppermute(value, 'tensor', [(i, i ^ 1 << bit) for i in range(groups)])  15.8 us
    pallas_call x4, Pallas kernels, local_grads(): pl.pallas_call(lambda *refs: grads_kernel(scale, tile, *refs), grid=(cols...  13.1 us
  transfers between devices with their start and end apart: 76, of which 36 were waited for; matrix products, arithmetic and copies ran while one was open for 8% of the time, Pallas kernels for 27%

profile of v1, /device:TPU:0, one launch (start us, length us, event | category | flops | bytes accessed | tf_op | source)
XLA Modules:
  0.0 438.6 jit_solution(14034518141172159251)
XLA Ops:
  13.1 9.4 %collective-permute-done = bf16[128,1536]{1,0:T(8,128)(2,1)} collective-permute-done((bf16[128,1536]{1,0:T(8,128)(2,1)}, bf16[128,1536]{1,0:T(8,128)(2,1)}, u32[]{:S(2)}, u32[]{:S(2)}) %collective-permute-start) | collective-permute-done | bytes 393248 | tf_op jit(solution)/shard_map/ppermute | solution.py:263
  25.6 7.4 %collective-permute-done.1 = bf16[128,1536]{1,0:T(8,128)(2,1)S(1)} collective-permute-done((bf16[128,1536]{1,0:T(8,128)(2,1)}, bf16[128,1536]{1,0:T(8,128)(2,1)S(1)}, u32[]{:S(2)}, u32[]{:S(2)}) %collective-permute-start.1) | collective-permute-done | bytes 393248 | tf_op jit(solution)/shard_map/ppermute | solution.py:263
  41.5 6.1 %collective-permute-done.30.refs_3_ = bf16[128,1536]{1,0:T(8,128)(2,1)S(1)} collective-permute-done((bf16[128,1536]{1,0:T(8,128)(2,1)S(1)}, bf16[128,1536]{1,0:T(8,128)(2,1)S(1)}, u32[]{:S(2)}, u32[]{:S(2)}) %collective-permute-start.30) | collective-permute-done | bytes 393248 | tf_op jit(solution)/shard_map/ppermute | solution.py:312
  50.6 6.0 %collective-permute-done.2.refs_4_ = bf16[256,2048]{1,0:T(8,128)(2,1)S(1)} collective-permute-done((bf16[256,2048]{1,0:T(8,128)(2,1)}, bf16[256,2048]{1,0:T(8,128)(2,1)S(1)}, u32[]{:S(2)}, u32[]{:S(2)}) %collective-permute-start.2) | collective-permute-done | bytes 1048608 | tf_op jit(solution)/shard_map/ppermute | solution.py:263
  62.6 7.5 %collective-permute-done.35.refs_8_ = bf16[128,1536]{1,0:T(8,128)(2,1)} collective-permute-done((bf16[128,1536]{1,0:T(8,128)(2,1)}, bf16[128,1536]{1,0:T(8,128)(2,1)}, u32[]{:S(2)}, u32[]{:S(2)}) %collective-permute-start.35) | collective-permute-done | bytes 393248 | tf_op jit(solution)/shard_map/ppermute | solution.py:312
  84.5 7.9 %collective-permute-done.33.refs_6_ = bf16[128,1536]{1,0:T(8,128)(2,1)S(1)} collective-permute-done((bf16[128,1536]{1,0:T(8,128)(2,1)}, bf16[128,1536]{1,0:T(8,128)(2,1)S(1)}, u32[]{:S(2)}, u32[]{:S(2)}) %collective-permute-start.33) | collective-permute-done | bytes 393248 | tf_op jit(solution)/shard_map/ppermute | solution.py:312
  95.7 13.2 %forward_product.4.refs_11_ = f32[1024,2048]{1,0:T(8,128)} custom-call(s32[16]{0:T(128)S(1)} %dynamic-slice_bitcast_fusion.refs_0_.refs_1_, f32[52,16]{1,0:T(8,128)S(1)} %copy.19.refs_1_.refs_0_, bf16[128,1536]{1,0:T(8,128)(2,1)S(1)} %copy-done.6, bf16[128,1536]{1,0:T(8,128)(2,1)S(1)} %copy-done.11, bf16[128,1536]{1,0:T(8,128)(2,1)} %collective-permute-done.31.refs_4_, ...), custom_call_target="tpu_custom_call" | custom-call | flops 6442450944 | bytes 26214400 | tf_op jit(solution)/shard_map/forward_product/pallas_call | solution.py:216
  112.2 8.7 %collective-permute-done.24.refs_5_ = bf16[128,1536]{1,0:T(8,128)(2,1)S(1)} collective-permute-done((bf16[128,1536]{1,0:T(8,128)(2,1)S(1)}, bf16[128,1536]{1,0:T(8,128)(2,1)S(1)}, u32[]{:S(2)}, u32[]{:S(2)}) %collective-permute-start.24) | collective-permute-done | bytes 393248 | tf_op jit(solution)/shard_map/ppermute | solution.py:312
  125.9 13.3 %forward_product.5.refs_11_ = f32[1024,2048]{1,0:T(8,128)} custom-call(s32[16]{0:T(128)S(1)} %dynamic-slice_bitcast_fusion.refs_0_.refs_1_, f32[52,16]{1,0:T(8,128)S(1)} %copy.19.refs_1_.refs_0_, bf16[128,1536]{1,0:T(8,128)(2,1)} %local_mix.6.refs_2_, bf16[128,1536]{1,0:T(8,128)(2,1)} %collective-permute-done.22.refs_3_, ...), custom_call_target="tpu_custom_call" | custom-call | flops 6442450944 | bytes 26214400 | tf_op jit(solution)/shard_map/forward_product/pallas_call | solution.py:216
  140.0 10.9 %backward_product.7 = bf16[1024,1536]{1,0:T(8,128)(2,1)} custom-call(f32[52,16]{1,0:T(8,128)S(1)} %copy.19.refs_1_.refs_0_, bf16[1024,2048]{1,0:T(8,128)(2,1)S(1)} %arrange_rows.1.refs_1_, bf16[6656,2048]{1,0:T(8,128)(2,1)} %refs_2_.8), custom_call_target="tpu_custom_call" | custom-call | flops 6442450944 | bytes 13631488 | tf_op jit(solution)/shard_map/backward_product/pallas_call | solution.py:168
  150.9 10.9 %backward_product.6 = bf16[1024,1536]{1,0:T(8,128)(2,1)} custom-call(f32[52,16]{1,0:T(8,128)S(1)} %copy.19.refs_1_.refs_0_, bf16[1024,2048]{1,0:T(8,128)(2,1)S(1)} %arrange_rows.1.refs_1_, bf16[6656,2048]{1,0:T(8,128)(2,1)} %refs_2_.8), custom_call_target="tpu_custom_call" | custom-call | flops 6442450944 | bytes 13631488 | tf_op jit(solution)/shard_map/backward_product/pallas_call | solution.py:168
  161.8 12.6 %backward_product.5 = bf16[1024,1792]{1,0:T(8,128)(2,1)} custom-call(f32[52,16]{1,0:T(8,128)S(1)} %copy.19.refs_1_.refs_0_, bf16[1024,2048]{1,0:T(8,128)(2,1)S(1)} %arrange_rows.1.refs_1_, bf16[6656,2048]{1,0:T(8,128)(2,1)} %refs_2_.8), custom_call_target="tpu_custom_call" | custom-call | flops 7516192768 | bytes 15204352 | tf_op jit(solution)/shard_map/backward_product/pallas_call | solution.py:168
  174.4 12.5 %backward_product.4 = bf16[1024,1792]{1,0:T(8,128)(2,1)} custom-call(f32[52,16]{1,0:T(8,128)S(1)} %copy.19.refs_1_.refs_0_, bf16[1024,2048]{1,0:T(8,128)(2,1)S(1)} %arrange_rows.1.refs_1_, bf16[6656,2048]{1,0:T(8,128)(2,1)} %refs_2_.8), custom_call_target="tpu_custom_call" | custom-call | flops 7516192768 | bytes 15204352 | tf_op jit(solution)/shard_map/backward_product/pallas_call | solution.py:168
  212.2 8.3 %collective-permute-done.15.refs_4_ = bf16[128,1792]{1,0:T(8,128)(2,1)S(1)} collective-permute-done((bf16[128,1792]{1,0:T(8,128)(2,1)S(1)}, bf16[128,1792]{1,0:T(8,128)(2,1)S(1)}, u32[]{:S(2)}, u32[]{:S(2)}) %collective-permute-start.15) | collective-permute-done | bytes 458784 | tf_op jit(solution)/shard_map/ppermute | solution.py:312
  247.2 14.8 %collective-permute-done.20.refs_7_ = bf16[128,1792]{1,0:T(8,128)(2,1)S(1)} collective-permute-done((bf16[128,1792]{1,0:T(8,128)(2,1)S(1)}, bf16[128,1792]{1,0:T(8,128)(2,1)S(1)}, u32[]{:S(2)}, u32[]{:S(2)}) %collective-permute-start.20) | collective-permute-done | bytes 458784 | tf_op jit(solution)/shard_map/ppermute | solution.py:312
  264.5 7.3 %collective-permute-done.11.refs_7_ = bf16[128,1792]{1,0:T(8,128)(2,1)S(1)} collective-permute-done((bf16[128,1792]{1,0:T(8,128)(2,1)S(1)}, bf16[128,1792]{1,0:T(8,128)(2,1)S(1)}, u32[]{:S(2)}, u32[]{:S(2)}) %collective-permute-start.11) | collective-permute-done | bytes 458784 | tf_op jit(solution)/shard_map/ppermute | solution.py:312
  273.4 13.7 %forward_product.6.refs_11_ = f32[1024,2048]{1,0:T(8,128)} custom-call(s32[16]{0:T(128)S(1)} %dynamic-slice_bitcast_fusion.refs_0_.refs_1_, f32[52,16]{1,0:T(8,128)S(1)} %copy.19.refs_1_.refs_0_, bf16[128,1792]{1,0:T(8,128)(2,1)S(1)} %local_mix.5.refs_2_, bf16[128,1792]{1,0:T(8,128)(2,1)S(1)} %collective-permute-done.14.refs_3_, ...), custom_call_target="tpu_custom_call" | custom-call | flops 7516192768 | bytes 27787264 | tf_op jit(solution)/shard_map/forward_product/pallas_call | solution.py:216
  293.9 13.0 %forward_product.7 = bf16[1024,2048]{1,0:T(8,128)(2,1)} custom-call(s32[16]{0:T(128)S(1)} %dynamic-slice_bitcast_fusion.refs_0_.refs_1_, f32[52,16]{1,0:T(8,128)S(1)} %copy.19.refs_1_.refs_0_, bf16[128,1792]{1,0:T(8,128)(2,1)S(1)} %local_mix.4.refs_2_, bf16[128,1792]{1,0:T(8,128)(2,1)S(1)} %collective-permute-done.6.refs_3_, ...), custom_call_target="tpu_custom_call" | custom-call | flops 7516192768 | bytes 27787264 | tf_op jit(solution)/shard_map/forward_product/pallas_call | solution.py:216
  312.0 7.3 %collective-permute-done.61 = bf16[128,1536]{1,0:T(8,128)(2,1)S(1)} collective-permute-done((bf16[128,1536]{1,0:T(8,128)(2,1)}, bf16[128,1536]{1,0:T(8,128)(2,1)S(1)}, u32[]{:S(2)}, u32[]{:S(2)}) %collective-permute-start.61) | collective-permute-done | bytes 393248 | tf_op jit(solution)/shard_map/ppermute | solution.py:338
  332.6 4.9 %collective-permute-done.71 = bf16[128,1536]{1,0:T(8,128)(2,1)S(1)} collective-permute-done((bf16[128,1536]{1,0:T(8,128)(2,1)S(1)}, bf16[128,1536]{1,0:T(8,128)(2,1)S(1)}, u32[]{:S(2)}, u32[]{:S(2)}) %collective-permute-start.71) | collective-permute-done | bytes 393248 | tf_op jit(solution)/shard_map/ppermute | solution.py:338
  360.7 4.9 %collective-permute-done.44 = bf16[128,1792]{1,0:T(8,128)(2,1)S(1)} collective-permute-done((bf16[128,1792]{1,0:T(8,128)(2,1)S(1)}, bf16[128,1792]{1,0:T(8,128)(2,1)S(1)}, u32[]{:S(2)}, u32[]{:S(2)}) %collective-permute-start.44) | collective-permute-done | bytes 458784 | tf_op jit(solution)/shard_map/ppermute | solution.py:338
  377.6 4.9 %collective-permute-done.63 = bf16[128,1536]{1,0:T(8,128)(2,1)S(1)} collective-permute-done((bf16[128,1536]{1,0:T(8,128)(2,1)S(1)}, bf16[128,1536]{1,0:T(8,128)(2,1)S(1)}, u32[]{:S(2)}, u32[]{:S(2)}) %collective-permute-start.63) | collective-permute-done | bytes 393248 | tf_op jit(solution)/shard_map/ppermute | solution.py:338
  394.1 6.0 %collective-permute-done.45 = bf16[128,1792]{1,0:T(8,128)(2,1)S(1)} collective-permute-done((bf16[128,1792]{1,0:T(8,128)(2,1)S(1)}, bf16[128,1792]{1,0:T(8,128)(2,1)S(1)}, u32[]{:S(2)}, u32[]{:S(2)}) %collective-permute-start.45) | collective-permute-done | bytes 458784 | tf_op jit(solution)/shard_map/ppermute | solution.py:338
  402.2 10.6 %collective-permute-done.55 = bf16[128,1792]{1,0:T(8,128)(2,1)S(1)} collective-permute-done((bf16[128,1792]{1,0:T(8,128)(2,1)S(1)}, bf16[128,1792]{1,0:T(8,128)(2,1)S(1)}, u32[]{:S(2)}, u32[]{:S(2)}) %collective-permute-start.55) | collective-permute-done | bytes 458784 | tf_op jit(solution)/shard_map/ppermute | solution.py:263
  (215 shorter events, 201.9 us)
Async XLA Ops:
  7.2 424.6 %reduce-scatter.2.cloned.1.call-start = ((), (), s32[]{:S(2)}) async-start(), calls=%async_computation.1 | async-start | bytes 5242880 | tf_op jit(solution)/shard_map/reduce_scatter | solution.py:323
  70.1 69.0 %collective-permute-start.37 = (bf16[256,2048]{1,0:T(8,128)(2,1)}, bf16[256,2048]{1,0:T(8,128)(2,1)S(1)}, u32[]{:S(2)}, u32[]{:S(2)}) collective-permute-start(bf16[256,2048]{1,0:T(8,128)(2,1)} %refs_2_.4), channel_id=1, source_target_pairs={{0,1},{1,0},{2,3},{3,2},{4,5},{5,4},{6,7},{7,6},{8,9},{9,8},{10,11... | collective-permute-start | bytes 3145736 | tf_op jit(solution)/shard_map/ppermute | solution.py:263
  76.5 32.3 %collective-permute-start.23 = (bf16[128,1536]{1,0:T(8,128)(2,1)}, bf16[128,1536]{1,0:T(8,128)(2,1)S(1)}, u32[]{:S(2)}, u32[]{:S(2)}) collective-permute-start(bf16[128,1536]{1,0:T(8,128)(2,1)} %collective-permute-done.22.refs_3_), channel_id=1, source_target_pairs={{0,8},{8,16},{16,24},{24,28},{28,20},{20,12},{12,4},{4,0},{1,9},{9... | collective-permute-start | bytes 1179656 | tf_op jit(solution)/shard_map/ppermute | solution.py:312
  79.1 29.9 %collective-permute-start.27 = (bf16[128,1536]{1,0:T(8,128)(2,1)}, bf16[128,1536]{1,0:T(8,128)(2,1)S(1)}, u32[]{:S(2)}, u32[]{:S(2)}) collective-permute-start(bf16[128,1536]{1,0:T(8,128)(2,1)} %collective-permute-done.26.refs_8_), channel_id=1, source_target_pairs={{0,4},{8,0},{16,8},{24,16},{28,24},{20,28},{12,20},{4,12},{1,5},{9... | collective-permute-start | bytes 1179656 | tf_op jit(solution)/shard_map/ppermute | solution.py:312
  84.5 25.0 %collective-permute-start.13 = (bf16[128,1792]{1,0:T(8,128)(2,1)S(1)}, bf16[128,1792]{1,0:T(8,128)(2,1)S(1)}, u32[]{:S(2)}, u32[]{:S(2)}) collective-permute-start(bf16[128,1792]{1,0:T(8,128)(2,1)S(1)} %add_convert_fusion.14.refs_2_), channel_id=1, source_target_pairs={{0,1},{1,0},{2,3},{3,2},{4,5},{5,4},{6,7},{7,6},{8,9},{9,8},{10,11... | collective-permute-start | bytes 1376264 | tf_op jit(solution)/shard_map/ppermute | solution.py:263
  108.9 30.3 %collective-permute-start.38 = (bf16[256,2048]{1,0:T(8,128)(2,1)S(1)}, bf16[256,2048]{1,0:T(8,128)(2,1)S(1)}, u32[]{:S(2)}, u32[]{:S(2)}) collective-permute-start(bf16[256,2048]{1,0:T(8,128)(2,1)S(1)} %copy-done.9), channel_id=1, source_target_pairs={{0,1},{1,0},{2,3},{3,2},{4,5},{5,4},{6,7},{7,6},{8,9},{9,8},{10,11... | collective-permute-start | bytes 3145736 | tf_op jit(solution)/shard_map/ppermute | solution.py:263
  111.5 92.7 %collective-permute-start.14 = (bf16[128,1792]{1,0:T(8,128)(2,1)S(1)}, bf16[128,1792]{1,0:T(8,128)(2,1)S(1)}, u32[]{:S(2)}, u32[]{:S(2)}) collective-permute-start(bf16[128,1792]{1,0:T(8,128)(2,1)S(1)} %local_mix.5.refs_2_), channel_id=1, source_target_pairs={{0,8},{8,16},{16,24},{24,28},{28,20},{20,12},{12,4},{4,0},{1,9},{9... | collective-permute-start | bytes 1376264 | tf_op jit(solution)/shard_map/ppermute | solution.py:312
  120.9 87.2 %collective-permute-start.18 = (bf16[128,1792]{1,0:T(8,128)(2,1)S(1)}, bf16[128,1792]{1,0:T(8,128)(2,1)S(1)}, u32[]{:S(2)}, u32[]{:S(2)}) collective-permute-start(bf16[128,1792]{1,0:T(8,128)(2,1)S(1)} %local_mix.5.refs_2_), channel_id=1, source_target_pairs={{0,4},{8,0},{16,8},{24,16},{28,24},{20,28},{12,20},{4,12},{1,5},{9... | collective-permute-start | bytes 1376264 | tf_op jit(solution)/shard_map/ppermute | solution.py:312
  122.5 74.3 %collective-permute-start.5 = (bf16[128,1792]{1,0:T(8,128)(2,1)S(1)}, bf16[128,1792]{1,0:T(8,128)(2,1)S(1)}, u32[]{:S(2)}, u32[]{:S(2)}) collective-permute-start(bf16[128,1792]{1,0:T(8,128)(2,1)S(1)} %add_convert_fusion.15.refs_2_), channel_id=1, source_target_pairs={{0,1},{1,0},{2,3},{3,2},{4,5},{5,4},{6,7},{7,6},{8,9},{9,8},{10,11... | collective-permute-start | bytes 1376264 | tf_op jit(solution)/shard_map/ppermute | solution.py:263
  200.8 26.8 %collective-permute-start.42 = (bf16[128,1792]{1,0:T(8,128)(2,1)S(1)}, bf16[128,1792]{1,0:T(8,128)(2,1)S(1)}, u32[]{:S(2)}, u32[]{:S(2)}) collective-permute-start(bf16[128,1792]{1,0:T(8,128)(2,1)S(1)} %get-tuple-element.38), channel_id=1, source_target_pairs={{0,4},{8,0},{16,8},{24,16},{28,24},{20,28},{12,20},{4,12},{1,5},{9... | collective-permute-start | bytes 1376264 | tf_op jit(solution)/shard_map/ppermute | solution.py:338
  208.1 27.4 %collective-permute-start.6 = (bf16[128,1792]{1,0:T(8,128)(2,1)S(1)}, bf16[128,1792]{1,0:T(8,128)(2,1)S(1)}, u32[]{:S(2)}, u32[]{:S(2)}) collective-permute-start(bf16[128,1792]{1,0:T(8,128)(2,1)S(1)} %local_mix.4.refs_2_), channel_id=1, source_target_pairs={{0,8},{8,16},{16,24},{24,28},{28,20},{20,12},{12,4},{4,0},{1,9},{9... | collective-permute-start | bytes 1376264 | tf_op jit(solution)/shard_map/ppermute | solution.py:312
  227.6 79.4 %collective-permute-start.70 = (bf16[128,1536]{1,0:T(8,128)(2,1)}, bf16[128,1536]{1,0:T(8,128)(2,1)}, u32[]{:S(2)}, u32[]{:S(2)}) collective-permute-start(bf16[128,1536]{1,0:T(8,128)(2,1)} %get-tuple-element.48), channel_id=1, source_target_pairs={{0,4},{8,0},{16,8},{24,16},{28,24},{20,28},{12,20},{4,12},{1,5},{9... | collective-permute-start | bytes 1179656 | tf_op jit(solution)/shard_map/ppermute | solution.py:338
  233.9 28.1 %collective-permute-start.20 = (bf16[128,1792]{1,0:T(8,128)(2,1)S(1)}, bf16[128,1792]{1,0:T(8,128)(2,1)S(1)}, u32[]{:S(2)}, u32[]{:S(2)}) collective-permute-start(bf16[128,1792]{1,0:T(8,128)(2,1)S(1)} %collective-permute-done.19.refs_8_), channel_id=1, source_target_pairs={{0,4},{8,0},{16,8},{24,16},{28,24},{20,28},{12,20},{4,12},{1,5},{9... | collective-permute-start | bytes 1376264 | tf_op jit(solution)/shard_map/ppermute | solution.py:312
  235.5 27.0 %collective-permute-start.7 = (bf16[128,1792]{1,0:T(8,128)(2,1)S(1)}, bf16[128,1792]{1,0:T(8,128)(2,1)S(1)}, u32[]{:S(2)}, u32[]{:S(2)}) collective-permute-start(bf16[128,1792]{1,0:T(8,128)(2,1)S(1)} %collective-permute-done.6.refs_3_), channel_id=1, source_target_pairs={{0,8},{8,16},{16,24},{24,28},{28,20},{20,12},{12,4},{4,0},{1,9},{9... | collective-permute-start | bytes 1376264 | tf_op jit(solution)/shard_map/ppermute | solution.py:312
  240.1 23.9 %collective-permute-start.17 = (bf16[128,1792]{1,0:T(8,128)(2,1)S(1)}, bf16[128,1792]{1,0:T(8,128)(2,1)S(1)}, u32[]{:S(2)}, u32[]{:S(2)}) collective-permute-start(bf16[128,1792]{1,0:T(8,128)(2,1)S(1)} %collective-permute-done.16.refs_5_), channel_id=1, source_target_pairs={{0,8},{8,16},{16,24},{24,28},{28,20},{20,12},{12,4},{4,0},{1,9},{9... | collective-permute-start | bytes 1376264 | tf_op jit(solution)/shard_map/ppermute | solution.py:312
  243.7 28.1 %collective-permute-start.11 = (bf16[128,1792]{1,0:T(8,128)(2,1)S(1)}, bf16[128,1792]{1,0:T(8,128)(2,1)S(1)}, u32[]{:S(2)}, u32[]{:S(2)}) collective-permute-start(bf16[128,1792]{1,0:T(8,128)(2,1)S(1)} %collective-permute-done.10.refs_8_), channel_id=1, source_target_pairs={{0,4},{8,0},{16,8},{24,16},{28,24},{20,28},{12,20},{4,12},{1,5},{9... | collective-permute-start | bytes 1376264 | tf_op jit(solution)/shard_map/ppermute | solution.py:312
  262.0 48.7 %collective-permute-start.57 = (bf16[128,1536]{1,0:T(8,128)(2,1)}, bf16[128,1536]{1,0:T(8,128)(2,1)}, u32[]{:S(2)}, u32[]{:S(2)}) collective-permute-start(bf16[128,1536]{1,0:T(8,128)(2,1)} %get-tuple-element.53), channel_id=1, source_target_pairs={{0,8},{8,16},{16,24},{24,28},{28,20},{20,12},{12,4},{4,0},{1,9},{9... | collective-permute-start | bytes 1179656 | tf_op jit(solution)/shard_map/ppermute | solution.py:338
  262.4 59.9 %collective-permute-start.52 = (bf16[128,1792]{1,0:T(8,128)(2,1)}, bf16[128,1792]{1,0:T(8,128)(2,1)}, u32[]{:S(2)}, u32[]{:S(2)}) collective-permute-start(bf16[128,1792]{1,0:T(8,128)(2,1)} %get-tuple-element.32), channel_id=1, source_target_pairs={{0,4},{8,0},{16,8},{24,16},{28,24},{20,28},{12,20},{4,12},{1,5},{9... | collective-permute-start | bytes 1376264 | tf_op jit(solution)/shard_map/ppermute | solution.py:338
  287.1 38.5 %collective-permute-start.39 = (bf16[128,1792]{1,0:T(8,128)(2,1)}, bf16[128,1792]{1,0:T(8,128)(2,1)}, u32[]{:S(2)}, u32[]{:S(2)}) collective-permute-start(bf16[128,1792]{1,0:T(8,128)(2,1)} %get-tuple-element.37), channel_id=1, source_target_pairs={{0,8},{8,16},{16,24},{24,28},{28,20},{20,12},{12,4},{4,0},{1,9},{9... | collective-permute-start | bytes 1376264 | tf_op jit(solution)/shard_map/ppermute | solution.py:338
  332.0 23.8 %collective-permute-start.53 = (bf16[128,1792]{1,0:T(8,128)(2,1)S(1)}, bf16[128,1792]{1,0:T(8,128)(2,1)S(1)}, u32[]{:S(2)}, u32[]{:S(2)}) collective-permute-start(bf16[128,1792]{1,0:T(8,128)(2,1)S(1)} %get-tuple-element.30), channel_id=1, source_target_pairs={{0,4},{8,0},{16,8},{24,16},{28,24},{20,28},{12,20},{4,12},{1,5},{9... | collective-permute-start | bytes 1376264 | tf_op jit(solution)/shard_map/ppermute | solution.py:338
  340.5 25.2 %collective-permute-start.44 = (bf16[128,1792]{1,0:T(8,128)(2,1)S(1)}, bf16[128,1792]{1,0:T(8,128)(2,1)S(1)}, u32[]{:S(2)}, u32[]{:S(2)}) collective-permute-start(bf16[128,1792]{1,0:T(8,128)(2,1)S(1)} %get-tuple-element.36), channel_id=1, source_target_pairs={{0,4},{8,0},{16,8},{24,16},{28,24},{20,28},{12,20},{4,12},{1,5},{9... | collective-permute-start | bytes 1376264 | tf_op jit(solution)/shard_map/ppermute | solution.py:338
  349.6 24.5 %collective-permute-start.72 = (bf16[128,1536]{1,0:T(8,128)(2,1)S(1)}, bf16[128,1536]{1,0:T(8,128)(2,1)S(1)}, u32[]{:S(2)}, u32[]{:S(2)}) collective-permute-start(bf16[128,1536]{1,0:T(8,128)(2,1)S(1)} %get-tuple-element.44), channel_id=1, source_target_pairs={{0,4},{8,0},{16,8},{24,16},{28,24},{20,28},{12,20},{4,12},{1,5},{9... | collective-permute-start | bytes 1179656 | tf_op jit(solution)/shard_map/ppermute | solution.py:338
  367.9 24.5 %collective-permute-start.54 = (bf16[128,1792]{1,0:T(8,128)(2,1)S(1)}, bf16[128,1792]{1,0:T(8,128)(2,1)S(1)}, u32[]{:S(2)}, u32[]{:S(2)}) collective-permute-start(bf16[128,1792]{1,0:T(8,128)(2,1)S(1)} %get-tuple-element.28), channel_id=1, source_target_pairs={{0,4},{8,0},{16,8},{24,16},{28,24},{20,28},{12,20},{4,12},{1,5},{9... | collective-permute-start | bytes 1376264 | tf_op jit(solution)/shard_map/ppermute | solution.py:338
  386.1 31.8 %collective-permute-start.64 = (bf16[128,1536]{1,0:T(8,128)(2,1)S(1)}, bf16[128,1536]{1,0:T(8,128)(2,1)S(1)}, u32[]{:S(2)}, u32[]{:S(2)}) collective-permute-start(bf16[128,1536]{1,0:T(8,128)(2,1)S(1)} %add_convert_fusion.24), channel_id=1, source_target_pairs={{0,2},{1,3},{2,0},{3,1},{4,6},{5,7},{6,4},{7,5},{8,10},{9,11},{10,... | collective-permute-start | bytes 1179656 | tf_op jit(solution)/shard_map/ppermute | solution.py:263
  (70 other events, 1348.4 us)
Sparse Core Ops, SparseCore 0:
  307.1 44.6 reduce-scatter.1

commit v2 on v1

v2 whole, which is shorter than its diff:
```python
import math

import jax
import jax.numpy as jnp
import numpy as np
from jax import lax
from jax.experimental import pallas as pl
from jax.experimental.pallas import tpu as pltpu
from jax.sharding import PartitionSpec as P

BLOCK = 128
SMALL_SHARE = 4 / 26
VMEM_LIMIT = 40 * 1024 * 1024
F32, BF16 = jnp.float32, jnp.bfloat16


def after(value, *earlier):
    return lax.optimization_barrier((value, *earlier))[0]


def sylvester(order):
    matrix = np.ones((1, 1), np.float32)
    while matrix.shape[0] < order:
        matrix = np.block([[matrix, matrix], [matrix, -matrix]])
    return matrix


def ring_cycle(count):
    return [*range(0, count, 2), *reversed(range(1, count, 2))]


def ring_tables(count):
    cycle = ring_cycle(count)
    place = np.argsort(cycle)
    behind = [[cycle[(place[i] - r) % count] for r in range(count)] for i in range(count)]
    ahead = [[(place[j] - place[i]) % count for j in range(count)] for i in range(count)]
    return np.concatenate([behind, ahead], axis=1).astype(np.int32)


def params():
    return pltpu.CompilerParams(vmem_limit_bytes=VMEM_LIMIT)


def spec_smem():
    return pl.BlockSpec(memory_space=pltpu.SMEM)


def dequantize_into(weight_ref, codes_ref, scales_ref, row0, col0):
    for i in range(codes_ref.shape[0] // BLOCK):
        for j in range(codes_ref.shape[1] // BLOCK):
            at = (pl.ds(i * BLOCK, BLOCK), pl.ds(j * BLOCK, BLOCK))
            wide = codes_ref[at].astype(F32) * scales_ref[row0 + i, col0 + j]
            weight_ref[at] = wide.astype(BF16)


def mixed(values, mix, scale):
    high = values.astype(BF16)
    low = (values - high.astype(F32)).astype(BF16)
    total = jnp.dot(high, mix, preferred_element_type=F32) + jnp.dot(
        low, mix, preferred_element_type=F32
    )
    return (total * scale).astype(BF16)


def mix_kernel(scale, sign_ref, mix_ref, own_ref, other_ref, out_ref):
    for j in range(own_ref.shape[1] // BLOCK):
        at = (slice(None), pl.ds(j * BLOCK, BLOCK))
        values = own_ref[at].astype(F32) * sign_ref[0] + other_ref[at].astype(F32)
        out_ref[at] = mixed(values, mix_ref[...], scale)


def local_mix(own, other, sign, mix, scale):
    rows, cols = own.shape
    return pl.pallas_call(
        lambda *refs: mix_kernel(scale, *refs),
        out_shape=jax.ShapeDtypeStruct((rows, cols), BF16),
        in_specs=[spec_smem()] + [pl.BlockSpec(memory_space=pltpu.VMEM)] * 3,
        out_specs=pl.BlockSpec(memory_space=pltpu.VMEM),
        compiler_params=params(),
        cost_estimate=pl.CostEstimate(
            flops=4 * rows * cols * BLOCK, bytes_accessed=6 * rows * cols, transcendentals=0
        ),
        name="local_mix",
    )(sign, mix, own, other)


def grads_kernel(scale, tile, sign_ref, mix_ref, own_ref, other_ref, gate_ref, up_ref, *refs):
    gate_grad_ref, up_grad_ref = refs[-2:]
    for j in range(tile // BLOCK):
        at = (slice(None), pl.ds(j * BLOCK, BLOCK))
        values = own_ref[at].astype(F32) * sign_ref[0] + other_ref[at].astype(F32)
        grad = mixed(values, mix_ref[...], scale).astype(F32)
        gate = gate_ref[at].astype(F32)
        sigmoid = jax.nn.sigmoid(gate)
        up_grad_ref[at] = (grad * (gate * sigmoid)).astype(BF16)
        gate_grad_ref[at] = (
            grad * up_ref[at].astype(F32) * sigmoid * (1.0 + gate * (1.0 - sigmoid))
        ).astype(BF16)


def local_grads(own, other, sign, mix, scale, gate_act, up_act, start, tile, made):
    rows, cols = own.shape
    whole = pl.BlockSpec((rows, tile), lambda i: (0, start // tile + i))
    part = pl.BlockSpec((rows, tile), lambda i: (0, i))
    rest = [pl.BlockSpec(memory_space=pl.ANY)] * len(made)
    return pl.pallas_call(
        lambda *refs: grads_kernel(scale, tile, *refs),
        grid=(cols // tile,),
        out_shape=[jax.ShapeDtypeStruct(gate_act.shape, BF16)] * 2,
        in_specs=[
            spec_smem(),
            pl.BlockSpec((BLOCK, BLOCK), lambda i: (0, 0)),
            part,
            part,
            whole,
            whole,
            *rest,
        ],
        out_specs=[whole, whole],
        input_output_aliases={6 + k: k for k in range(len(made))},
        compiler_params=params(),
        cost_estimate=pl.CostEstimate(
            flops=4 * rows * cols * BLOCK,
            bytes_accessed=12 * rows * cols,
            transcendentals=rows * cols,
        ),
        name="local_grads",
    )(sign, mix, own, other, gate_act, up_act, *made)


def arrange_kernel(table_ref, rows_ref, out_ref):
    count = table_ref.shape[0] // 2
    size = out_ref.shape[0] // count
    for i in range(count):
        start = pl.multiple_of(table_ref[count + i] * size, size)
        out_ref[pl.ds(start, size), :] = rows_ref[pl.ds(i * size, size), :]


def arrange_rows(rows, table):
    return pl.pallas_call(
        arrange_kernel,
        out_shape=jax.ShapeDtypeStruct(rows.shape, BF16),
        in_specs=[spec_smem(), pl.BlockSpec(memory_space=pltpu.VMEM)],
        out_specs=pl.BlockSpec(memory_space=pltpu.VMEM),
        compiler_params=params(),
        cost_estimate=pl.CostEstimate(flops=0, bytes_accessed=4 * rows.size, transcendentals=0),
        name="arrange_rows",
    )(table, rows)


def backward_kernel(row_block, scales_ref, grad_ref, codes_ref, *refs):
    out_ref, weight_ref = refs[-2:]
    row0 = row_block + pl.program_id(0) * (codes_ref.shape[0] // BLOCK)
    dequantize_into(weight_ref, codes_ref, scales_ref, row0, 0)
    out_ref[...] = lax.dot_general(
        grad_ref[...], weight_ref[...], (((1,), (1,)), ((), ())), preferred_element_type=F32
    ).astype(BF16)


def backward_product(grad_rows, codes, scales, start, cols, tile, pieces):
    tokens, depth = grad_rows.shape
    (first, count), made = pieces
    return pl.pallas_call(
        lambda *refs: backward_kernel(start // BLOCK + first * (tile // BLOCK), *refs),
        grid=(count,),
        out_shape=pltpu.HBM((tokens, cols), BF16),
        in_specs=[
            spec_smem(),
            pl.BlockSpec((tokens, depth), lambda i: (0, 0)),
            pl.BlockSpec((tile, depth), lambda i: (start // tile + first + i, 0)),
            *[pl.BlockSpec(memory_space=pl.ANY)] * len(made),
        ],
        out_specs=pl.BlockSpec((tokens, tile), lambda i: (0, first + i)),
        scratch_shapes=[pltpu.VMEM((tile, depth), BF16)],
        input_output_aliases={3 + k: k for k in range(len(made))},
        compiler_params=params(),
        cost_estimate=pl.CostEstimate(
            flops=2 * tokens * depth * count * tile,
            bytes_accessed=2 * (tokens * depth + (depth + tokens) * count * tile),
            transcendentals=0,
        ),
        name="backward_product",
    )(scales, grad_rows, codes, *made)


def forward_kernel(count, row_block, col_block, has_sum, order_ref, scales_ref, *refs):
    blocks, codes_ref = refs[:count], refs[count]
    sum_ref = refs[count + 1] if has_sum else None
    out_ref, rows_ref, weight_ref = refs[-3:]
    tile = codes_ref.shape[1]

    @pl.when(pl.program_id(0) == 0)
    def _():
        for r, block in enumerate(blocks):
            size = block.shape[0]
            rows_ref[pl.ds(pl.multiple_of(order_ref[r] * size, size), size), :] = block[...]

    col0 = col_block + pl.program_id(0) * (tile // BLOCK)
    dequantize_into(weight_ref, codes_ref, scales_ref, row_block, col0)
    total = jnp.dot(rows_ref[...], weight_ref[...], preferred_element_type=F32)
    if has_sum:
        total = total + sum_ref[...]
    out_ref[...] = total.astype(out_ref.dtype)


def forward_product(blocks, order, codes, scales, start, columns, running, offset, out_dtype):
    size, depth = blocks[0].shape
    tokens, (first, width) = size * len(blocks), columns
    tile = min(256, width)
    sums = [] if running is None else [running]
    return pl.pallas_call(
        lambda *refs: forward_kernel(
            len(blocks), start // BLOCK, first // BLOCK, bool(sums), *refs
        ),
        grid=(width // tile,),
        out_shape=pltpu.HBM((tokens, width), out_dtype),
        in_specs=[
            spec_smem(),
            spec_smem(),
            *[
                pl.BlockSpec((size, depth), lambda i: (0, 0), pipeline_mode=pl.Buffered(1))
            ] * len(blocks),
            pl.BlockSpec(
                (pl.Element(depth), pl.Element(tile)), lambda i: (start, (first // tile + i) * tile)
            ),
            *[pl.BlockSpec((tokens, tile), lambda i: (0, offset // tile + i))] * len(sums),
        ],
        out_specs=pl.BlockSpec((tokens, tile), lambda i: (0, i)),
        scratch_shapes=[pltpu.VMEM((tokens, depth), BF16), pltpu.VMEM((depth, tile), BF16)],
        compiler_params=params(),
        cost_estimate=pl.CostEstimate(
            flops=2 * tokens * depth * width,
            bytes_accessed=2 * (tokens * depth + depth * width) + 8 * tokens * width,
            transcendentals=0,
        ),
        name="forward_product",
    )(order, scales, *blocks, codes, *sums)


def stream_columns(sizes, tile):
    starts = np.cumsum([0, *sizes[:-1]])
    return [(int(a) * tile, int(b) * tile) for a, b in zip(starts, sizes)]


class Gather:
    def __init__(self, ring, first, own):
        self.ring, self.hop = ring, 0
        half = ring["count"] // 2
        self.reach = {first: half, -first: ring["count"] - 1 - half}
        self.blocks = {0: own}

    def advance(self, *tokens):
        self.hop += 1
        for step, reach in self.reach.items():
            if self.hop <= reach:
                moving = after(self.blocks[(self.hop - 1) * step % self.ring["count"]], *tokens)
                self.blocks[self.hop * step % self.ring["count"]] = self.ring["send"](moving, step)

    def arrived(self):
        return [
            self.blocks[self.hop * step % self.ring["count"]]
            for step, reach in self.reach.items()
            if self.hop <= reach
        ]

    def all_blocks(self):
        return [self.blocks[r] for r in range(self.ring["count"])]


class Scatter:
    def __init__(self, ring, first, partial):
        self.ring, self.hop, self.partial = ring, 0, partial
        half = ring["count"] // 2
        self.reach = {first: half, -first: ring["count"] - 1 - half}
        self.sums = {}

    def term(self, offset):
        rows = self.partial.shape[0] // self.ring["count"]
        at = offset % self.ring["count"] * rows
        return lax.slice_in_dim(self.partial, at, at + rows, axis=0)

    def advance(self, *tokens):
        self.hop += 1
        for step, reach in self.reach.items():
            if self.hop <= reach:
                moving = self.term(step * (reach - self.hop + 1))
                if self.hop > 1:
                    moving = (self.sums[step].astype(F32) + moving.astype(F32)).astype(BF16)
                self.sums[step] = self.ring["send"](after(moving, *tokens), step)

    def arrived(self):
        return [self.sums[step] for step, reach in self.reach.items() if self.hop <= reach]

    def total(self):
        parts = [self.term(0), *self.sums.values()]
        return sum(part.astype(F32) for part in parts).astype(BF16)


def on_device(gate_act, up_act, down_codes, down_scales, grad_out):
    groups, ring = lax.axis_size("tensor"), lax.axis_size("dp")
    group, member = lax.axis_index("tensor"), lax.axis_index("dp")
    bits = list(reversed(range(groups.bit_length() - 1)))
    rows, hidden_units = gate_act.shape
    tile = 256 if hidden_units % 256 == 0 else BLOCK
    units = hidden_units // tile
    small = max(1, round(units * SMALL_SHARE))
    large = (units - small) // 2
    ahead_streams = stream_columns([small, large, units - small - large], tile)
    back_streams = stream_columns([units - small - large, large, small], tile)
    cycle = ring_cycle(ring)
    table = lax.dynamic_index_in_dim(jnp.asarray(ring_tables(ring)), member, 0, keepdims=False)
    around = {
        "count": ring,
        "send": lambda value, step: lax.ppermute(
            value, "dp", [(cycle[i], cycle[(i + step) % ring]) for i in range(ring)]
        ),
    }

    def partner(value, bit):
        return lax.ppermute(value, "tensor", [(i, i ^ 1 << bit) for i in range(groups)])

    def sign(bit):
        return jnp.where(group >> bit & 1 == 1, -1.0, 1.0).astype(F32)

    def paired(own, other, bit):
        return (own.astype(F32) * sign(bit) + other.astype(F32)).astype(BF16)

    last_sign = sign(bits[-1]).reshape(1)
    mix = jnp.asarray(sylvester(BLOCK), BF16)
    scale = 1.0 / math.sqrt(groups * BLOCK)

    def hidden(start, size):
        gate = lax.slice_in_dim(gate_act, start, start + size, axis=1).astype(F32)
        up = lax.slice_in_dim(up_act, start, start + size, axis=1).astype(F32)
        return (gate * jax.nn.sigmoid(gate) * up).astype(BF16)

    def exchanged(own, token):
        own = after(own, *token)
        other = arrived = partner(own, bits[0])
        for previous, bit in zip(bits, bits[1:]):
            own = paired(own, other, previous)
            other = partner(own, bit)
        return own, other, arrived

    gathers, token = [], []
    for k, (start, size) in enumerate(ahead_streams):
        own, other, arrived = exchanged(hidden(start, size), token)
        token = [arrived]
        if k == 1:
            gathered = lax.all_gather(after(grad_out, arrived), "tensor", axis=0, tiled=True)
        rotated = local_mix(own, other, last_sign, mix, scale)
        gathers.append(Gather(around, 1 if k % 2 == 0 else -1, rotated))
        gathers[k].advance()
        if k:
            gathers[0].advance(*token)

    half = down_codes.shape[1] // 2
    running, whole_sum = {}, []

    def forward(k, columns, *tokens):
        start, _ = ahead_streams[k]
        first = columns[0]
        earlier = [] if k == 0 else [whole_sum[0]] if k == 1 else [running[first]]
        running[first] = forward_product(
            gathers[k].all_blocks(),
            after(table, *tokens),
            down_codes,
            down_scales,
            start,
            columns,
            earlier[0] if earlier else None,
            first if k == 1 else 0,
            BF16 if k == len(gathers) - 1 else F32,
        )
        if k == 0:
            whole_sum.append(running[first])
        return running[first]

    partials = {}

    def backward(k, piece, *tokens):
        start, cols = back_streams[k]
        tiles = cols // tile
        cut = (tiles + 1) // 2 if k < len(back_streams) - 1 else tiles
        place = (0, cut) if piece == 0 else (cut, tiles - cut)
        partials[k] = backward_product(
            after(grad_rows, *tokens),
            down_codes,
            down_scales,
            start,
            cols,
            tile,
            (place, [] if piece == 0 else [partials[k]]),
        )
        return partials[k]

    small_ring, ring_a, ring_b = gathers
    for _ in range(small_ring.hop, ring // 2):
        small_ring.advance()
    grad_rows = arrange_rows(gathered, table)

    last = ring // 2
    work = [
        lambda *t: forward(0, (0, 2 * half), *t),
        lambda *t: backward(0, 0, *t),
        lambda *t: backward(0, 1, *t),
        lambda *t: backward(1, 0, *t),
        lambda *t: backward(1, 1, *t),
        lambda *t: backward(2, 0, *t),
    ]
    done = []
    for hop in range(2, last + 1):
        for current in (ring_a, ring_b):
            arrived = current.arrived()
            current.advance(*done)
            if work:
                done = [work.pop(0)(*arrived, *done)]
    while work:
        done = [work.pop(0)(*done)]

    work = [
        lambda *t: forward(1, (0, half), *t),
        lambda *t: forward(1, (half, half), *t),
        lambda *t: forward(2, (0, half), *t),
        lambda *t: forward(2, (half, half), *t),
    ]
    sums = [Scatter(around, 1 if k % 2 == 0 else -1, partials[k]) for k in range(3)]
    sum_a, sum_b, small_sum = sums
    sum_a.advance(*ring_a.arrived())
    sum_b.advance(*ring_b.arrived())
    done = []
    for hop in range(2, last + 1):
        for current in (sum_a, sum_b):
            arrived = current.arrived()
            current.advance(*done)
            if work:
                done = [work.pop(0)(*arrived, *done)]
    while work:
        done = [work.pop(0)(*done)]
    layer_output = lax.psum_scatter(
        jnp.concatenate([running[0], running[half]], axis=1),
        "tensor",
        scatter_dimension=0,
        tiled=True,
    )
    small_sum.advance(*sum_a.arrived())
    for _ in range(last - 1):
        small_sum.advance()

    grads, token = [], []
    for k, (start, size) in enumerate(back_streams):
        own, other, arrived = exchanged(sums[k].total(), token)
        token = [arrived]
        grads = local_grads(
            own, other, last_sign, mix, scale, gate_act, up_act, start, tile, grads
        )
        if k == 0:
            token = [arrived, *grads]
    gate_grad, up_grad = grads
    return (layer_output, gate_grad, up_grad)


def solution(mesh):
    return jax.shard_map(
        on_device,
        mesh=mesh,
        in_specs=(
            P("dp", "tensor"),
            P("dp", "tensor"),
            P("tensor", "dp"),
            P("tensor", "dp"),
            P("tensor", "dp"),
        ),
        out_specs=(P("tensor", "dp"), P("dp", "tensor"), P("dp", "tensor")),
        check_vma=False,
    )
```

time: 441 us -> 428 us (0.971)
  starting transfers between devices: 77.8 us -> 63.8 us
    ppermute x19 -> x12, waiting for transfers between devices: 38.1 us -> 51.1 us  [partner(): lax.ppermute(value, 'tensor', [(i, i ^ 1 << bit) for i in range(groups)])]
    ppermute x56 -> x42, starting transfers between devices: 61.9 us -> 49.1 us  [on_device(): lax.ppermute(value, 'dp', [(cycle[i], cycle[(i + step) % ring]) for i in...]
    ppermute x56 -> x42, waiting for transfers between devices: 146 us -> 135 us  [on_device(): lax.ppermute(value, 'dp', [(cycle[i], cycle[(i + step) % ring]) for i in...]
    convert_element_type x16 -> x12, other arithmetic: 18.7 us -> 14.6 us  [the longest x9 11.6 us: advance(): moving = (self.sums[step].astype(F32) + moving.astype(F32)).astype(BF16)]
    pallas_call x4 -> x5, Pallas kernels: 53.2 us -> 56 us  [forward_product(): pl.pallas_call(lambda *refs: forward_kernel(len(blocks), start // BLOCK,...]
    pallas_call x5 -> x6, Pallas kernels: 47.7 us -> 49 us  [the longest x5 48.2 us: backward_product(): pl.pallas_call(lambda *refs: backward_kernel(start // BLOCK + first * (ti...]
    ppermute x19 -> x12, starting transfers between devices: 15.8 us -> 14.6 us  [partner(): lax.ppermute(value, 'tensor', [(i, i ^ 1 << bit) for i in range(groups)])]
    unnamed x37 -> x53, local copies, waits for them, and re-layouts: 9.65 us -> 10.4 us
  transfers between devices with their start and end apart: 76 -> 56, of which waited for: 36 -> 22; matrix products, arithmetic and copies ran while one was open for 8% -> 6% of each run, Pallas kernels for 27% -> 26%
where the time goes in v2:
time: 428 us; the launch traced here: 426 us
  waiting for transfers between devices  186 us (43%)
  Pallas kernels  120 us (28%)
  starting transfers between devices  63.8 us (15%)
  other arithmetic  25.8 us (6%)
  local copies, waits for them, and re-layouts  15.1 us (4%)
  between operations  14.5 us (3%)
    ppermute x42, waiting for transfers between devices, on_device(): lax.ppermute(value, 'dp', [(cycle[i], cycle[(i + step) % ring]) for i in...  135 us
    pallas_call x5, Pallas kernels, forward_product(): pl.pallas_call(lambda *refs: forward_kernel(len(blocks), start // BLOCK,...  56 us
    ppermute x12, waiting for transfers between devices, partner(): lax.ppermute(value, 'tensor', [(i, i ^ 1 << bit) for i in range(groups)])  51.1 us
    ppermute x42, starting transfers between devices, on_device(): lax.ppermute(value, 'dp', [(cycle[i], cycle[(i + step) % ring]) for i in...  49.1 us
    pallas_call x5, Pallas kernels, backward_product(): pl.pallas_call(lambda *refs: backward_kernel(start // BLOCK + first * (ti...  48.2 us
    ppermute x12, starting transfers between devices, partner(): lax.ppermute(value, 'tensor', [(i, i ^ 1 << bit) for i in range(groups)])  14.6 us
    pallas_call x3, Pallas kernels, local_grads(): pl.pallas_call(lambda *refs: grads_kernel(scale, tile, *refs), grid=(cols...  12.9 us
    convert_element_type x9, other arithmetic, advance(): moving = (self.sums[step].astype(F32) + moving.astype(F32)).astype(BF16)  11.6 us
  transfers between devices with their start and end apart: 56, of which 22 were waited for; matrix products, arithmetic and copies ran while one was open for 6% of the time, Pallas kernels for 26%

profile of v2, /device:TPU:0, one launch (start us, length us, event | category | flops | bytes accessed | tf_op | source)
XLA Modules:
  0.0 425.8 jit_solution(6091858128026574603)
XLA Ops:
  19.5 15.7 %collective-permute-done.1 = bf16[128,2816]{1,0:T(8,128)(2,1)} collective-permute-done((bf16[128,2816]{1,0:T(8,128)(2,1)S(1)}, bf16[128,2816]{1,0:T(8,128)(2,1)}, u32[]{:S(2)}, u32[]{:S(2)}) %collective-permute-start.1) | collective-permute-done | bytes 720928 | tf_op jit(solution)/shard_map/ppermute | solution.py:320
  38.5 22.9 %collective-permute-done.7 = bf16[128,2816]{1,0:T(8,128)(2,1)S(1)} collective-permute-done((bf16[128,2816]{1,0:T(8,128)(2,1)S(1)}, bf16[128,2816]{1,0:T(8,128)(2,1)S(1)}, u32[]{:S(2)}, u32[]{:S(2)}) %collective-permute-start.7) | collective-permute-done | bytes 720928 | tf_op jit(solution)/shard_map/ppermute | solution.py:320
  75.0 16.1 %collective-permute-done.16.refs_9_ = bf16[128,1024]{1,0:T(8,128)(2,1)S(1)} collective-permute-done((bf16[128,1024]{1,0:T(8,128)(2,1)S(1)}, bf16[128,1024]{1,0:T(8,128)(2,1)S(1)}, u32[]{:S(2)}, u32[]{:S(2)}) %collective-permute-start.16) | collective-permute-done | bytes 262176 | tf_op jit(solution)/shard_map/ppermute | solution.py:314
  106.4 17.3 %collective-permute-done.18.refs_7_ = bf16[128,1024]{1,0:T(8,128)(2,1)} collective-permute-done((bf16[128,1024]{1,0:T(8,128)(2,1)}, bf16[128,1024]{1,0:T(8,128)(2,1)}, u32[]{:S(2)}, u32[]{:S(2)}) %collective-permute-start.18) | collective-permute-done | bytes 262176 | tf_op jit(solution)/shard_map/ppermute | solution.py:314
  127.2 10.8 %forward_product.5.refs_11_ = f32[1024,2048]{1,0:T(8,128)} custom-call(s32[16]{0:T(128)S(1)} %dynamic-slice_bitcast_fusion.table_ref.refs_0_, f32[52,16]{1,0:T(8,128)S(1)} %copy.18.refs_1_.refs_0_, bf16[128,1024]{1,0:T(8,128)(2,1)S(1)} %local_mix.5.refs_2_, bf16[128,1024]{1,0:T(8,128)(2,1)S(1)} %collective-permute-done.12.refs_3_, ...), custom_call_target="tpu_custom_call" | custom-call | flops 4294967296 | bytes 23068672 | tf_op jit(solution)/shard_map/forward_product/pallas_call | solution.py:211
  143.2 11.3 %backward_product.5.refs_3_ = bf16[1024,2816]{1,0:T(8,128)(2,1)} custom-call(f32[52,16]{1,0:T(8,128)S(1)} %copy.18.refs_1_.refs_0_, bf16[1024,2048]{1,0:T(8,128)(2,1)S(1)} %arrange_rows.1.refs_1_, bf16[6656,2048]{1,0:T(8,128)(2,1)} %refs_2_.9), custom_call_target="tpu_custom_call" | custom-call | flops 6442450944 | bytes 13631488 | tf_op jit(solution)/shard_map/backward_product/pallas_call | solution.py:163
  155.0 9.2 %backward_product.6 = bf16[1024,2816]{1,0:T(8,128)(2,1)} custom-call(f32[52,16]{1,0:T(8,128)S(1)} %copy.18.refs_1_.refs_0_, bf16[1024,2048]{1,0:T(8,128)(2,1)S(1)} %arrange_rows.1.refs_1_, bf16[6656,2048]{1,0:T(8,128)(2,1)} %refs_2_.9, bf16[1024,2816]{1,0:T(8,128)(2,1)} %backward_product.5.refs_3_), custom_call_target="tpu_custom_call", output_to_operand_aliasing={{}: (3, {})} | custom-call | flops 5368709120 | bytes 12058624 | tf_op jit(solution)/shard_map/backward_product/pallas_call | solution.py:163
  167.5 10.6 %backward_product.7.refs_3_ = bf16[1024,2816]{1,0:T(8,128)(2,1)} custom-call(f32[52,16]{1,0:T(8,128)S(1)} %copy.18.refs_1_.refs_0_, bf16[1024,2048]{1,0:T(8,128)(2,1)S(1)} %arrange_rows.1.refs_1_, bf16[6656,2048]{1,0:T(8,128)(2,1)} %refs_2_.9), custom_call_target="tpu_custom_call" | custom-call | flops 6442450944 | bytes 13631488 | tf_op jit(solution)/shard_map/backward_product/pallas_call | solution.py:163
  180.1 13.6 %collective-permute-done.27.refs_5_ = bf16[128,2816]{1,0:T(8,128)(2,1)S(1)} collective-permute-done((bf16[128,2816]{1,0:T(8,128)(2,1)}, bf16[128,2816]{1,0:T(8,128)(2,1)S(1)}, u32[]{:S(2)}, u32[]{:S(2)}) %collective-permute-start.27) | collective-permute-done | bytes 720928 | tf_op jit(solution)/shard_map/ppermute | solution.py:314
  193.7 9.2 %backward_product.8 = bf16[1024,2816]{1,0:T(8,128)(2,1)} custom-call(f32[52,16]{1,0:T(8,128)S(1)} %copy.18.refs_1_.refs_0_, bf16[1024,2048]{1,0:T(8,128)(2,1)S(1)} %arrange_rows.1.refs_1_, bf16[6656,2048]{1,0:T(8,128)(2,1)} %refs_2_.9, bf16[1024,2816]{1,0:T(8,128)(2,1)} %backward_product.7.refs_3_), custom_call_target="tpu_custom_call", output_to_operand_aliasing={{}: (3, {})} | custom-call | flops 5368709120 | bytes 12058624 | tf_op jit(solution)/shard_map/backward_product/pallas_call | solution.py:163
  207.1 14.9 %collective-permute-done.29.refs_6_ = bf16[128,2816]{1,0:T(8,128)(2,1)S(1)} collective-permute-done((bf16[128,2816]{1,0:T(8,128)(2,1)S(1)}, bf16[128,2816]{1,0:T(8,128)(2,1)S(1)}, u32[]{:S(2)}, u32[]{:S(2)}) %collective-permute-start.29) | collective-permute-done | bytes 720928 | tf_op jit(solution)/shard_map/ppermute | solution.py:314
  225.6 11.7 %collective-permute-done.23 = bf16[128,2816]{1,0:T(8,128)(2,1)S(1)} collective-permute-done((bf16[128,2816]{1,0:T(8,128)(2,1)S(1)}, bf16[128,2816]{1,0:T(8,128)(2,1)S(1)}, u32[]{:S(2)}, u32[]{:S(2)}) %collective-permute-start.23) | collective-permute-done | bytes 720928 | tf_op jit(solution)/shard_map/ppermute | solution.py:314
  237.4 11.3 %forward_product.6.refs_11_ = f32[1024,1024]{1,0:T(8,128)} custom-call(s32[16]{0:T(128)S(1)} %dynamic-slice_bitcast_fusion.table_ref.refs_0_, f32[52,16]{1,0:T(8,128)S(1)} %copy.18.refs_1_.refs_0_, bf16[128,2816]{1,0:T(8,128)(2,1)S(1)} %local_mix.3.refs_2_, bf16[128,2816]{1,0:T(8,128)(2,1)} %collective-permute-done.5.refs_3_, ...), custom_call_target="tpu_custom_call" | custom-call | flops 5905580032 | bytes 19922944 | tf_op jit(solution)/shard_map/forward_product/pallas_call | solution.py:211
  253.4 9.7 %collective-permute-done.24 = bf16[128,2816]{1,0:T(8,128)(2,1)S(1)} collective-permute-done((bf16[128,2816]{1,0:T(8,128)(2,1)S(1)}, bf16[128,2816]{1,0:T(8,128)(2,1)S(1)}, u32[]{:S(2)}, u32[]{:S(2)}) %collective-permute-start.24) | collective-permute-done | bytes 720928 | tf_op jit(solution)/shard_map/ppermute | solution.py:314
  272.4 11.3 %forward_product.7.refs_11_ = f32[1024,1024]{1,0:T(8,128)} custom-call(s32[16]{0:T(128)S(1)} %dynamic-slice_bitcast_fusion.table_ref.refs_0_, f32[52,16]{1,0:T(8,128)S(1)} %copy.18.refs_1_.refs_0_, bf16[128,2816]{1,0:T(8,128)(2,1)S(1)} %local_mix.3.refs_2_, bf16[128,2816]{1,0:T(8,128)(2,1)} %collective-permute-done.5.refs_3_, ...), custom_call_target="tpu_custom_call" | custom-call | flops 5905580032 | bytes 19922944 | tf_op jit(solution)/shard_map/forward_product/pallas_call | solution.py:211
  286.8 11.2 %forward_product.8 = bf16[1024,1024]{1,0:T(8,128)(2,1)} custom-call(s32[16]{0:T(128)S(1)} %dynamic-slice_bitcast_fusion.table_ref.refs_0_, f32[52,16]{1,0:T(8,128)S(1)} %copy.18.refs_1_.refs_0_, bf16[128,2816]{1,0:T(8,128)(2,1)S(1)} %local_mix.4.refs_2_, bf16[128,2816]{1,0:T(8,128)(2,1)S(1)} %copy-done.8, bf16[128,2816]{1,0:T(8,128)(2,1)} %collective-permute-done.20.refs_4_, ...), custom_call_target="tpu_custom_call" | custom-call | flops 5905580032 | bytes 19922944 | tf_op jit(solution)/shard_map/forward_product/pallas_call | solution.py:211
  298.0 11.3 %forward_product.9 = bf16[1024,1024]{1,0:T(8,128)(2,1)} custom-call(s32[16]{0:T(128)S(1)} %dynamic-slice_bitcast_fusion.table_ref.refs_0_, f32[52,16]{1,0:T(8,128)S(1)} %copy.18.refs_1_.refs_0_, bf16[128,2816]{1,0:T(8,128)(2,1)S(1)} %local_mix.4.refs_2_, bf16[128,2816]{1,0:T(8,128)(2,1)S(1)} %copy-done.8, bf16[128,2816]{1,0:T(8,128)(2,1)} %collective-permute-done.20.refs_4_, ...), custom_call_target="tpu_custom_call" | custom-call | flops 5905580032 | bytes 19922944 | tf_op jit(solution)/shard_map/forward_product/pallas_call | solution.py:211
  315.6 14.6 %collective-permute-done.35 = bf16[128,2816]{1,0:T(8,128)(2,1)S(1)} collective-permute-done((bf16[128,2816]{1,0:T(8,128)(2,1)S(1)}, bf16[128,2816]{1,0:T(8,128)(2,1)S(1)}, u32[]{:S(2)}, u32[]{:S(2)}) %collective-permute-start.35) | collective-permute-done | bytes 720928 | tf_op jit(solution)/shard_map/ppermute | solution.py:314
  334.7 7.9 %backward_product.9 = bf16[1024,1024]{1,0:T(8,128)(2,1)} custom-call(f32[52,16]{1,0:T(8,128)S(1)} %copy.18.refs_1_.refs_0_, bf16[1024,2048]{1,0:T(8,128)(2,1)S(1)} %copy-done.1, bf16[6656,2048]{1,0:T(8,128)(2,1)} %refs_2_.9), custom_call_target="tpu_custom_call" | custom-call | flops 4294967296 | bytes 10485760 | tf_op jit(solution)/shard_map/backward_product/pallas_call | solution.py:163
  360.0 8.7 %collective-permute-done.44 = bf16[128,2816]{1,0:T(8,128)(2,1)S(1)} collective-permute-done((bf16[128,2816]{1,0:T(8,128)(2,1)S(1)}, bf16[128,2816]{1,0:T(8,128)(2,1)S(1)}, u32[]{:S(2)}, u32[]{:S(2)}) %collective-permute-start.44) | collective-permute-done | bytes 720928 | tf_op jit(solution)/shard_map/ppermute | solution.py:314
  375.0 6.7 %collective-permute-done.45 = bf16[128,2816]{1,0:T(8,128)(2,1)S(1)} collective-permute-done((bf16[128,2816]{1,0:T(8,128)(2,1)S(1)}, bf16[128,2816]{1,0:T(8,128)(2,1)S(1)}, u32[]{:S(2)}, u32[]{:S(2)}) %collective-permute-start.45) | collective-permute-done | bytes 720928 | tf_op jit(solution)/shard_map/ppermute | solution.py:314
  383.4 5.4 %local_grads.3 = (bf16[128,6656]{1,0:T(8,128)(2,1)}, bf16[128,6656]{1,0:T(8,128)(2,1)}) custom-call(f32[1]{0:T(128)} %bitcast.1.refs_0_, bf16[128,128]{1,0:T(8,128)(2,1)S(1)} %copy-done.9, bf16[128,2816]{1,0:T(8,128)(2,1)S(1)} %add_convert_fusion.1.refs_2_, bf16[128,2816]{1,0:T(8,128)(2,1)S(1)} %collective-permute-done.49.refs_3_, ...), custom_call_target="tpu_custom_call" | custom-call | flops 184549376 | bytes 4325376 | tf_op jit(solution)/shard_map/local_grads/pallas_call | solution.py:106
  400.4 4.5 %collective-permute-done.50 = bf16[128,2816]{1,0:T(8,128)(2,1)S(1)} collective-permute-done((bf16[128,2816]{1,0:T(8,128)(2,1)S(1)}, bf16[128,2816]{1,0:T(8,128)(2,1)S(1)}, u32[]{:S(2)}, u32[]{:S(2)}) %collective-permute-start.50) | collective-permute-done | bytes 720928 | tf_op jit(solution)/shard_map/ppermute | solution.py:320
  411.4 5.4 %local_grads.4 = (bf16[128,6656]{1,0:T(8,128)(2,1)}, bf16[128,6656]{1,0:T(8,128)(2,1)}) custom-call(f32[1]{0:T(128)} %bitcast.1.refs_0_, bf16[128,128]{1,0:T(8,128)(2,1)S(1)} %copy-done.9, bf16[128,2816]{1,0:T(8,128)(2,1)S(1)} %add_convert_fusion.refs_2_, ...), custom_call_target="tpu_custom_call", output_to_operand_aliasing={{0}: (6, {}), {1}: (7, {})} | custom-call | flops 184549376 | bytes 4325376 | tf_op jit(solution)/shard_map/local_grads/pallas_call | solution.py:106
  (186 shorter events, 139.9 us)
Async XLA Ops:
  7.2 133.0 %all-gather.2.cloned.1.call-start = ((), (), s32[]{:S(2)}) async-start(), calls=%async_computation.1 | async-start | bytes 5242880 | tf_op jit(solution)/shard_map/all_gather | solution.py:350
  35.2 383.7 %reduce-scatter.2.cloned.1.call-start = ((), (), s32[]{:S(2)}) async-start(), calls=%async_computation.2 | async-start | bytes 5242880 | tf_op jit(solution)/shard_map/reduce_scatter | solution.py:440
  35.4 27.5 %collective-permute-start.11 = (bf16[128,1024]{1,0:T(8,128)(2,1)S(1)}, bf16[128,1024]{1,0:T(8,128)(2,1)S(1)}, u32[]{:S(2)}, u32[]{:S(2)}) collective-permute-start(bf16[128,1024]{1,0:T(8,128)(2,1)S(1)} %add_convert_fusion.23.refs_2_), channel_id=1, source_target_pairs={{0,1},{1,0},{2,3},{3,2},{4,5},{5,4},{6,7},{7,6},{8,9},{9,8},{10,11... | collective-permute-start | bytes 786440 | tf_op jit(solution)/shard_map/ppermute | solution.py:320
  35.4 26.0 %collective-permute-start.7 = (bf16[128,2816]{1,0:T(8,128)(2,1)S(1)}, bf16[128,2816]{1,0:T(8,128)(2,1)S(1)}, u32[]{:S(2)}, u32[]{:S(2)}) collective-permute-start(bf16[128,2816]{1,0:T(8,128)(2,1)S(1)} %get-tuple-element.52), channel_id=1, source_target_pairs={{0,2},{1,3},{2,0},{3,1},{4,6},{5,7},{6,4},{7,5},{8,10},{9,11},{10,... | collective-permute-start | bytes 2162696 | tf_op jit(solution)/shard_map/ppermute | solution.py:320
  38.3 26.4 %collective-permute-start.2 = (bf16[128,2816]{1,0:T(8,128)(2,1)S(1)}, bf16[128,2816]{1,0:T(8,128)(2,1)S(1)}, u32[]{:S(2)}, u32[]{:S(2)}) collective-permute-start(bf16[128,2816]{1,0:T(8,128)(2,1)S(1)} %add_convert_fusion.15.refs_2_), channel_id=1, source_target_pairs={{0,1},{1,0},{2,3},{3,2},{4,5},{5,4},{6,7},{7,6},{8,9},{9,8},{10,11... | collective-permute-start | bytes 2162696 | tf_op jit(solution)/shard_map/ppermute | solution.py:320
  62.8 30.4 %collective-permute-start.8 = (bf16[128,2816]{1,0:T(8,128)(2,1)S(1)}, bf16[128,2816]{1,0:T(8,128)(2,1)}, u32[]{:S(2)}, u32[]{:S(2)}) collective-permute-start(bf16[128,2816]{1,0:T(8,128)(2,1)S(1)} %add_convert_fusion.14.refs_2_), channel_id=1, source_target_pairs={{0,1},{1,0},{2,3},{3,2},{4,5},{5,4},{6,7},{7,6},{8,9},{9,8},{10,11... | collective-permute-start | bytes 2162696 | tf_op jit(solution)/shard_map/ppermute | solution.py:320
  67.2 36.3 %collective-permute-start.3 = (bf16[128,2816]{1,0:T(8,128)(2,1)S(1)}, bf16[128,2816]{1,0:T(8,128)(2,1)S(1)}, u32[]{:S(2)}, u32[]{:S(2)}) collective-permute-start(bf16[128,2816]{1,0:T(8,128)(2,1)S(1)} %local_mix.3.refs_2_), channel_id=1, source_target_pairs={{0,4},{8,0},{16,8},{24,16},{28,24},{20,28},{12,20},{4,12},{1,5},{9... | collective-permute-start | bytes 2162696 | tf_op jit(solution)/shard_map/ppermute | solution.py:314
  73.3 31.8 %collective-permute-start.5 = (bf16[128,2816]{1,0:T(8,128)(2,1)S(1)}, bf16[128,2816]{1,0:T(8,128)(2,1)}, u32[]{:S(2)}, u32[]{:S(2)}) collective-permute-start(bf16[128,2816]{1,0:T(8,128)(2,1)S(1)} %local_mix.3.refs_2_), channel_id=1, source_target_pairs={{0,8},{8,16},{16,24},{24,28},{28,20},{20,12},{12,4},{4,0},{1,9},{9... | collective-permute-start | bytes 2162696 | tf_op jit(solution)/shard_map/ppermute | solution.py:314
  94.9 43.2 %collective-permute-start.9 = (bf16[128,2816]{1,0:T(8,128)(2,1)S(1)}, bf16[128,2816]{1,0:T(8,128)(2,1)S(1)}, u32[]{:S(2)}, u32[]{:S(2)}) collective-permute-start(bf16[128,2816]{1,0:T(8,128)(2,1)S(1)} %local_mix.4.refs_2_), channel_id=1, source_target_pairs={{0,8},{8,16},{16,24},{24,28},{28,20},{20,12},{12,4},{4,0},{1,9},{9... | collective-permute-start | bytes 2162696 | tf_op jit(solution)/shard_map/ppermute | solution.py:314
  98.9 40.9 %collective-permute-start.10 = (bf16[128,2816]{1,0:T(8,128)(2,1)S(1)}, bf16[128,2816]{1,0:T(8,128)(2,1)}, u32[]{:S(2)}, u32[]{:S(2)}) collective-permute-start(bf16[128,2816]{1,0:T(8,128)(2,1)S(1)} %local_mix.4.refs_2_), channel_id=1, source_target_pairs={{0,4},{8,0},{16,8},{24,16},{28,24},{20,28},{12,20},{4,12},{1,5},{9... | collective-permute-start | bytes 2162696 | tf_op jit(solution)/shard_map/ppermute | solution.py:314
  105.2 49.4 %collective-permute-start.4 = (bf16[128,2816]{1,0:T(8,128)(2,1)S(1)}, bf16[128,2816]{1,0:T(8,128)(2,1)}, u32[]{:S(2)}, u32[]{:S(2)}) collective-permute-start(bf16[128,2816]{1,0:T(8,128)(2,1)S(1)} %collective-permute-done.3.refs_9_), channel_id=1, source_target_pairs={{0,4},{8,0},{16,8},{24,16},{28,24},{20,28},{12,20},{4,12},{1,5},{9... | collective-permute-start | bytes 2162696 | tf_op jit(solution)/shard_map/ppermute | solution.py:314
  123.7 30.8 %collective-permute-start.6 = (bf16[128,2816]{1,0:T(8,128)(2,1)}, bf16[128,2816]{1,0:T(8,128)(2,1)}, u32[]{:S(2)}, u32[]{:S(2)}) collective-permute-start(bf16[128,2816]{1,0:T(8,128)(2,1)} %collective-permute-done.5.refs_3_), channel_id=1, source_target_pairs={{0,8},{8,16},{16,24},{24,28},{28,20},{20,12},{12,4},{4,0},{1,9},{9... | collective-permute-start | bytes 2162696 | tf_op jit(solution)/shard_map/ppermute | solution.py:314
  138.1 26.1 %collective-permute-start.20 = (bf16[128,2816]{1,0:T(8,128)(2,1)S(1)}, bf16[128,2816]{1,0:T(8,128)(2,1)}, u32[]{:S(2)}, u32[]{:S(2)}) collective-permute-start(bf16[128,2816]{1,0:T(8,128)(2,1)S(1)} %collective-permute-done.9.refs_3_), channel_id=1, source_target_pairs={{0,8},{8,16},{16,24},{24,28},{28,20},{20,12},{12,4},{4,0},{1,9},{9... | collective-permute-start | bytes 2162696 | tf_op jit(solution)/shard_map/ppermute | solution.py:314
  139.9 26.0 %collective-permute-start.21 = (bf16[128,2816]{1,0:T(8,128)(2,1)}, bf16[128,2816]{1,0:T(8,128)(2,1)}, u32[]{:S(2)}, u32[]{:S(2)}) collective-permute-start(bf16[128,2816]{1,0:T(8,128)(2,1)} %collective-permute-done.10.refs_9_), channel_id=1, source_target_pairs={{0,4},{8,0},{16,8},{24,16},{28,24},{20,28},{12,20},{4,12},{1,5},{9... | collective-permute-start | bytes 2162696 | tf_op jit(solution)/shard_map/ppermute | solution.py:314
  154.6 23.6 %collective-permute-start.19 = (bf16[128,2816]{1,0:T(8,128)(2,1)}, bf16[128,2816]{1,0:T(8,128)(2,1)S(1)}, u32[]{:S(2)}, u32[]{:S(2)}) collective-permute-start(bf16[128,2816]{1,0:T(8,128)(2,1)} %collective-permute-done.4.refs_8_), channel_id=1, source_target_pairs={{0,4},{8,0},{16,8},{24,16},{28,24},{20,28},{12,20},{4,12},{1,5},{9... | collective-permute-start | bytes 2162696 | tf_op jit(solution)/shard_map/ppermute | solution.py:314
  164.2 38.6 %collective-permute-start.28 = (bf16[128,2816]{1,0:T(8,128)(2,1)}, bf16[128,2816]{1,0:T(8,128)(2,1)S(1)}, u32[]{:S(2)}, u32[]{:S(2)}) collective-permute-start(bf16[128,2816]{1,0:T(8,128)(2,1)} %collective-permute-done.20.refs_4_), channel_id=1, source_target_pairs={{0,8},{8,16},{16,24},{24,28},{28,20},{20,12},{12,4},{4,0},{1,9},{9... | collective-permute-start | bytes 2162696 | tf_op jit(solution)/shard_map/ppermute | solution.py:314
  165.8 27.8 %collective-permute-start.27 = (bf16[128,2816]{1,0:T(8,128)(2,1)}, bf16[128,2816]{1,0:T(8,128)(2,1)S(1)}, u32[]{:S(2)}, u32[]{:S(2)}) collective-permute-start(bf16[128,2816]{1,0:T(8,128)(2,1)} %collective-permute-done.6.refs_4_), channel_id=1, source_target_pairs={{0,8},{8,16},{16,24},{24,28},{28,20},{20,12},{12,4},{4,0},{1,9},{9... | collective-permute-start | bytes 2162696 | tf_op jit(solution)/shard_map/ppermute | solution.py:314
  178.2 25.4 %collective-permute-start.22 = (bf16[128,2816]{1,0:T(8,128)(2,1)S(1)}, bf16[128,2816]{1,0:T(8,128)(2,1)S(1)}, u32[]{:S(2)}, u32[]{:S(2)}) collective-permute-start(bf16[128,2816]{1,0:T(8,128)(2,1)S(1)} %collective-permute-done.19.refs_7_), channel_id=1, source_target_pairs={{0,4},{8,0},{16,8},{24,16},{28,24},{20,28},{12,20},{4,12},{1,5},{9... | collective-permute-start | bytes 2162696 | tf_op jit(solution)/shard_map/ppermute | solution.py:314
  204.9 32.5 %collective-permute-start.23 = (bf16[128,2816]{1,0:T(8,128)(2,1)S(1)}, bf16[128,2816]{1,0:T(8,128)(2,1)S(1)}, u32[]{:S(2)}, u32[]{:S(2)}) collective-permute-start(bf16[128,2816]{1,0:T(8,128)(2,1)S(1)} %get-tuple-element.65), channel_id=1, source_target_pairs={{0,8},{8,16},{16,24},{24,28},{28,20},{20,12},{12,4},{4,0},{1,9},{9... | collective-permute-start | bytes 2162696 | tf_op jit(solution)/shard_map/ppermute | solution.py:314
  221.9 26.8 %collective-permute-start.31 = (bf16[128,2816]{1,0:T(8,128)(2,1)S(1)}, bf16[128,2816]{1,0:T(8,128)(2,1)S(1)}, u32[]{:S(2)}, u32[]{:S(2)}) collective-permute-start(bf16[128,2816]{1,0:T(8,128)(2,1)S(1)} %get-tuple-element.72), channel_id=1, source_target_pairs={{0,8},{8,16},{16,24},{24,28},{28,20},{20,12},{12,4},{4,0},{1,9},{9... | collective-permute-start | bytes 2162696 | tf_op jit(solution)/shard_map/ppermute | solution.py:314
  222.7 26.1 %collective-permute-start.30 = (bf16[128,2816]{1,0:T(8,128)(2,1)S(1)}, bf16[128,2816]{1,0:T(8,128)(2,1)S(1)}, u32[]{:S(2)}, u32[]{:S(2)}) collective-permute-start(bf16[128,2816]{1,0:T(8,128)(2,1)S(1)} %get-tuple-element.71), channel_id=1, source_target_pairs={{0,4},{8,0},{16,8},{24,16},{28,24},{20,28},{12,20},{4,12},{1,5},{9... | collective-permute-start | bytes 2162696 | tf_op jit(solution)/shard_map/ppermute | solution.py:314
  224.0 60.6 %collective-permute-start.32 = (bf16[128,2816]{1,0:T(8,128)(2,1)}, bf16[128,2816]{1,0:T(8,128)(2,1)S(1)}, u32[]{:S(2)}, u32[]{:S(2)}) collective-permute-start(bf16[128,2816]{1,0:T(8,128)(2,1)} %collective-permute-done.21.refs_8_), channel_id=1, source_target_pairs={{0,4},{8,0},{16,8},{24,16},{28,24},{20,28},{12,20},{4,12},{1,5},{9... | collective-permute-start | bytes 2162696 | tf_op jit(solution)/shard_map/ppermute | solution.py:314
  270.2 27.8 %collective-permute-start.34 = (bf16[128,2816]{1,0:T(8,128)(2,1)}, bf16[128,2816]{1,0:T(8,128)(2,1)S(1)}, u32[]{:S(2)}, u32[]{:S(2)}) collective-permute-start(bf16[128,2816]{1,0:T(8,128)(2,1)} %get-tuple-element.78), channel_id=1, source_target_pairs={{0,8},{8,16},{16,24},{24,28},{28,20},{20,12},{12,4},{4,0},{1,9},{9... | collective-permute-start | bytes 2162696 | tf_op jit(solution)/shard_map/ppermute | solution.py:314
  343.6 25.1 %collective-permute-start.44 = (bf16[128,2816]{1,0:T(8,128)(2,1)S(1)}, bf16[128,2816]{1,0:T(8,128)(2,1)S(1)}, u32[]{:S(2)}, u32[]{:S(2)}) collective-permute-start(bf16[128,2816]{1,0:T(8,128)(2,1)S(1)} %copy-done.19), channel_id=1, source_target_pairs={{0,4},{8,0},{16,8},{24,16},{28,24},{20,28},{12,20},{4,12},{1,5},{9... | collective-permute-start | bytes 2162696 | tf_op jit(solution)/shard_map/ppermute | solution.py:314
  (58 other events, 853.7 us)
Sparse Core Ops, SparseCore 0:
  35.3 42.6 all-gather.1
  313.6 53.8 reduce-scatter.1

commit v3 on v1

--- a/solution.py
+++ b/solution.py
@@ -9,7 +9,8 @@
 from jax.sharding import PartitionSpec as P
 
 BLOCK = 128
-STREAMS = 4
+AHEAD = (4, 11, 11)
+BACK = (11, 11, 4)
 VMEM_LIMIT = 40 * 1024 * 1024
 F32, BF16 = jnp.float32, jnp.bfloat16
 
@@ -39,6 +40,12 @@
 
 def params():
     return pltpu.CompilerParams(vmem_limit_bytes=VMEM_LIMIT)
+
+
+def cost(operations, moved):
+    return pl.CostEstimate(
+        flops=operations // 16, bytes_accessed=moved // 16, transcendentals=0
+    )
 
 
 def spec_smem():
@@ -77,9 +84,7 @@
         in_specs=[spec_smem()] + [pl.BlockSpec(memory_space=pltpu.VMEM)] * 3,
         out_specs=pl.BlockSpec(memory_space=pltpu.VMEM),
         compiler_params=params(),
-        cost_estimate=pl.CostEstimate(
-            flops=4 * rows * cols * BLOCK, bytes_accessed=6 * rows * cols, transcendentals=0
-        ),
+        cost_estimate=cost(4 * rows * cols * BLOCK, 6 * rows * cols),
         name="local_mix",
     )(sign, mix, own, other)
 
@@ -98,8 +103,11 @@
         ).astype(BF16)
 
 
-def local_grads(own, other, sign, mix, scale, gate_act, up_act, start, tile, made):
+def local_grads(own, other, sign, mix, scale, gate_act, up_act, start, made):
     rows, cols = own.shape
+    tile = math.gcd(start, cols)
+    if tile % (2 * BLOCK) == 0:
+        tile //= 2
     whole = pl.BlockSpec((rows, tile), lambda i: (0, start // tile + i))
     part = pl.BlockSpec((rows, tile), lambda i: (0, i))
     rest = [pl.BlockSpec(memory_space=pl.ANY)] * len(made)
@@ -119,11 +127,7 @@
         out_specs=[whole, whole],
         input_output_aliases={6 + k: k for k in range(len(made))},
         compiler_params=params(),
-        cost_estimate=pl.CostEstimate(
-            flops=4 * rows * cols * BLOCK,
-            bytes_accessed=12 * rows * cols,
-            transcendentals=rows * cols,
-        ),
+        cost_estimate=cost(4 * rows * cols * BLOCK, 12 * rows * cols),
         name="local_grads",
     )(sign, mix, own, other, gate_act, up_act, *made)
 
@@ -148,9 +152,7 @@
         in_specs=[spec_smem()] * 2 + [pl.BlockSpec(memory_space=pltpu.VMEM)] * len(blocks),
         out_specs=pl.BlockSpec(memory_space=pltpu.VMEM),
         compiler_params=params(),
-        cost_estimate=pl.CostEstimate(
-            flops=0, bytes_accessed=4 * rows * cols * len(blocks), transcendentals=0
-        ),
+        cost_estimate=cost(0, 4 * rows * cols * len(blocks)),
         name="arrange_rows",
     )(group, table, *blocks)
 
@@ -177,16 +179,14 @@
         out_specs=pl.BlockSpec((tokens, tile), lambda i: (0, i)),
         scratch_shapes=[pltpu.VMEM((tile, depth), BF16)],
         compiler_params=params(),
-        cost_estimate=pl.CostEstimate(
-            flops=2 * tokens * depth * cols,
-            bytes_accessed=2 * (tokens * depth + depth * cols + tokens * cols),
-            transcendentals=0,
+        cost_estimate=cost(
+            2 * tokens * depth * cols, 2 * (tokens * depth + (depth + tokens) * cols)
         ),
         name="backward_product",
     )(scales, grad_rows, codes)
 
 
-def forward_kernel(count, row_block, has_sum, order_ref, scales_ref, *refs):
+def forward_kernel(count, bits, row_block, has_sum, group_ref, order_ref, scales_ref, *refs):
     blocks, codes_ref = refs[:count], refs[count]
     sum_ref = refs[count + 1] if has_sum else None
     out_ref, rows_ref, weight_ref = refs[-3:]
@@ -194,9 +194,13 @@
 
     @pl.when(pl.program_id(0) == 0)
     def _():
+        per = max(1, count >> bits)
         for r, block in enumerate(blocks):
             size = block.shape[0]
-            rows_ref[pl.ds(pl.multiple_of(order_ref[r] * size, size), size), :] = block[...]
+            offset = order_ref[r] // per ^ group_ref[0]
+            turned = sum((offset >> i & 1) << bits - 1 - i for i in range(bits))
+            start = (turned * per + order_ref[r] % per) * size
+            rows_ref[pl.ds(pl.multiple_of(start, size), size), :] = block[...]
 
     dequantize_into(
         weight_ref, codes_ref, scales_ref, row_block, pl.program_id(0) * (tile // BLOCK)
@@ -207,41 +211,97 @@
     out_ref[...] = total.astype(out_ref.dtype)
 
 
-def forward_product(blocks, order, codes, scales, start, running, out_dtype):
-    size, cols = blocks[0].shape
+def forward_product(blocks, bits, group, order, codes, scales, start, running, out_dtype):
+    size, depth = blocks[0].shape
     tokens, width = size * len(blocks), codes.shape[1]
     tile = min(256, width)
     sums = [] if running is None else [running]
     sliced = pl.BlockSpec((tokens, tile), lambda i: (0, i))
     return pl.pallas_call(
-        lambda *refs: forward_kernel(len(blocks), start // BLOCK, bool(sums), *refs),
+        lambda *refs: forward_kernel(len(blocks), bits, start // BLOCK, bool(sums), *refs),
         grid=(width // tile,),
         out_shape=pltpu.HBM((tokens, width), out_dtype),
         in_specs=[
             spec_smem(),
             spec_smem(),
-            *[pl.BlockSpec((size, cols), lambda i: (0, 0))] * len(blocks),
-            pl.BlockSpec((pl.Element(cols), pl.Element(tile)), lambda i: (start, i * tile)),
+            spec_smem(),
+            *[
+                pl.BlockSpec((size, depth), lambda i: (0, 0), pipeline_mode=pl.Buffered(1))
+            ] * len(blocks),
+            pl.BlockSpec((pl.Element(depth), pl.Element(tile)), lambda i: (start, i * tile)),
             *[sliced] * len(sums),
         ],
         out_specs=sliced,
-        scratch_shapes=[pltpu.VMEM((tokens, cols), BF16), pltpu.VMEM((cols, tile), BF16)],
+        scratch_shapes=[pltpu.VMEM((tokens, depth), BF16), pltpu.VMEM((depth, tile), BF16)],
         compiler_params=params(),
-        cost_estimate=pl.CostEstimate(
-            flops=2 * tokens * cols * width,
-            bytes_accessed=2 * (tokens * cols + cols * width) + 8 * tokens * width,
-            transcendentals=0,
+        cost_estimate=cost(
+            2 * tokens * depth * width, 2 * (tokens + width) * depth + 8 * tokens * width
         ),
         name="forward_product",
-    )(order, scales, *blocks, codes, *sums)
-
-
-def stream_columns(total, tile):
-    units = total // tile
-    count = min(STREAMS, units)
-    sizes = sorted((units + k) // count for k in range(count))
+    )(group, order, scales, *blocks, codes, *sums)
+
+
+def shares(units, parts):
+    ends = [round(units * sum(parts[: i + 1]) / sum(parts)) for i in range(len(parts))]
+    return [end - begin for begin, end in zip([0, *ends], ends)]
+
+
+def stream_columns(sizes, tile):
     starts = np.cumsum([0, *sizes[:-1]])
     return [(int(a) * tile, int(b) * tile) for a, b in zip(starts, sizes)]
+
+
+class Ring:
+    def __init__(self, count, send, long_way):
+        self.count, self.send = count, send
+        self.reach = {long_way: count // 2, -long_way: count - 1 - count // 2}
+        self.hops = {1: 0, -1: 0}
+
+    def advance(self, step, *tokens):
+        moving = self.outgoing(step)
+        self.hops[step] += 1
+        arrived = self.send(after(moving, *tokens), step)
+        self.incoming(step, arrived)
+        return arrived
+
+
+class Gather(Ring):
+    def __init__(self, count, send, long_way, own):
+        super().__init__(count, send, long_way)
+        self.blocks = {0: own}
+
+    def outgoing(self, step):
+        return self.blocks[self.hops[step] * step % self.count]
+
+    def incoming(self, step, arrived):
+        self.blocks[self.hops[step] * step % self.count] = arrived
+
+    def all_blocks(self):
+        return [self.blocks[r] for r in range(self.count)]
+
+
+class Scatter(Ring):
+    def __init__(self, count, send, long_way, terms):
+        super().__init__(count, send, long_way)
+        self.terms, self.sums = terms, {}
+
+    def term(self, offset):
+        rows = self.terms.shape[0] // self.count
+        at = offset % self.count * rows
+        return lax.slice_in_dim(self.terms, at, at + rows, axis=0)
+
+    def outgoing(self, step):
+        term = self.term(step * (self.reach[step] - self.hops[step]))
+        if step not in self.sums:
+            return term
+        return (self.sums[step].astype(F32) + term.astype(F32)).astype(BF16)
+
+    def incoming(self, step, arrived):
+        self.sums[step] = arrived
+
+    def total(self, *tokens):
+        parts = [after(part, *tokens) for part in (self.term(0), *self.sums.values())]
+        return sum(part.astype(F32) for part in parts).astype(BF16)
 
 
 def on_device(gate_act, up_act, down_codes, down_scales, grad_out):
@@ -250,14 +310,16 @@
     bits = list(reversed(range(groups.bit_length() - 1)))
     rows, hidden_units = gate_act.shape
     tile = 256 if hidden_units % 256 == 0 else BLOCK
-    streams = stream_columns(hidden_units, tile)
+    units = hidden_units // tile
+    ahead_streams = stream_columns(shares(units, AHEAD), tile)
+    back_streams = stream_columns(shares(units, BACK), tile)
     cycle = ring_cycle(ring)
-    half = ring // 2
     table = lax.dynamic_index_in_dim(jnp.asarray(ring_tables(ring)), member, 0, keepdims=False)
 
-    pairs = {
-        step: [(cycle[i], cycle[(i + step) % ring]) for i in range(ring)] for step in (1, -1)
-    }
+    def send(value, step):
+        return lax.ppermute(
+            value, "dp", [(cycle[i], cycle[(i + step) % ring]) for i in range(ring)]
+        )
 
     def partner(value, bit):
         return lax.ppermute(value, "tensor", [(i, i ^ 1 << bit) for i in range(groups)])
@@ -268,84 +330,128 @@
     def paired(own, other, bit):
         return (own.astype(F32) * sign(bit) + other.astype(F32)).astype(BF16)
 
+    group_index = group.astype(jnp.int32).reshape(1)
     last_sign = sign(bits[-1]).reshape(1)
     mix = jnp.asarray(sylvester(BLOCK), BF16)
     scale = 1.0 / math.sqrt(groups * BLOCK)
-
-    def reach(k, step):
-        return half if (k % 2 == 0) == (step == 1) else ring - 1 - half
 
     def hidden(start, size):
         gate = lax.slice_in_dim(gate_act, start, start + size, axis=1).astype(F32)
         up = lax.slice_in_dim(up_act, start, start + size, axis=1).astype(F32)
         return (gate * jax.nn.sigmoid(gate) * up).astype(BF16)
 
-    def gathered():
-        held = {0: after(grad_out, token)}
-        for bit in bits:
-            held.update({o ^ 1 << bit: partner(value, bit) for o, value in list(held.items())})
-            if bit == bits[0]:
-                arrived = held[1 << bit]
-        return held, arrived
-
-    rotated = []
-    token = None
-    for k, (start, size) in enumerate(streams):
-        if k == len(streams) // 2:
-            held, token = gathered()
-        own = hidden(start, size)
-        if token is not None:
-            own = after(own, token)
-        other = token = partner(own, bits[0])
+    def exchanged(own, token, later=()):
+        own = after(own, *token)
+        other = arrived = partner(own, bits[0])
+        other = after(other, *later)
         for previous, bit in zip(bits, bits[1:]):
             own = paired(own, other, previous)
             other = partner(own, bit)
-        rotated.append(local_mix(own, other, last_sign, mix, scale))
-    grad_rows = arrange_rows(held, group.astype(jnp.int32).reshape(1), table)
-
-    running = None
-    for k, (start, size) in enumerate(streams):
-        blocks = [rotated[k]] + [None] * (ring - 1)
-        for step in (1, -1):
-            moving = rotated[k]
-            for hop in range(1, reach(k, step) + 1):
-                moving = lax.ppermute(moving, "dp", pairs[step])
-                blocks[hop * step % ring] = moving
-        running = forward_product(
-            blocks,
-            table,
-            down_codes,
-            down_scales,
-            start,
-            running,
-            BF16 if k == len(streams) - 1 else F32,
+        return own, other, arrived
+
+    last = ring // 2
+    gathers, token, seen, later = [], [], [], []
+    for k, (start, size) in enumerate(ahead_streams):
+        if k == 1:
+            later = hop
+        if k == 2:
+            for _ in range(3, last):
+                later = [gathers[0].advance(step, rotated) for step in (1, -1)]
+            later += [gathers[0].advance(1)]
+        own, other, arrived = exchanged(hidden(start, size), token, later)
+        if k == 1:
+            seen = [gathers[0].advance(step) for step in (1, -1)]
+        if k == 2:
+            seen = hop
+        rotated = local_mix(own, after(other, *seen), last_sign, mix, scale)
+        gathers.append(Gather(ring, send, -1 if k == 1 else 1, rotated))
+        token = [arrived]
+        if k < 2:
+            hop = [gathers[k].advance(step) for step in (1, -1)]
+        if k == 1:
+            token += seen
+    held = {0: after(grad_out, *token)}
+    for bit in bits:
+        held.update({o ^ 1 << bit: partner(x, bit) for o, x in list(held.items())})
+        if bit == bits[0]:
+            held = {o: after(x, rotated) for o, x in held.items()}
+    grad_rows = arrange_rows(held, group_index, table)
+    _, ring_a, ring_b = gathers
+
+    running, partials = [None], []
+
+    def forward(k, *tokens):
+        running.append(
+            forward_product(
+                gathers[k].all_blocks(),
+                len(bits),
+                group_index,
+                after(table, *tokens),
+                down_codes,
+                down_scales,
+                ahead_streams[k][0],
+                running[-1],
+                BF16 if k == len(gathers) - 1 else F32,
+            )
         )
-    layer_output = lax.psum_scatter(running, "tensor", scatter_dimension=0, tiled=True)
-
+        return running[-1]
+
+    def backward(k, *tokens):
+        start, cols = back_streams[k]
+        partials.append(
+            backward_product(after(grad_rows, *tokens), down_codes, down_scales, start, cols, tile)
+        )
+        return partials[-1]
+
+    done = {"hops": [*hop, rotated], "work": []}
+
+    def level(hops, work=None, *tokens):
+        before = [*done["hops"], *done["work"]]
+        done["hops"] = [current.advance(step, *done["work"], *tokens) for current, step in hops]
+        done["work"] = [work[0](*work[1:], *before)] if work else []
+
+    both = [(ring_a, -1), (ring_b, 1), (ring_a, 1), (ring_b, -1)]
+    work = [(forward, 0), (backward, 0)]
+    for _ in range(2, last):
+        level(both, work.pop(0) if work else None)
+    sum_a = Scatter(ring, send, 1, partials[0])
+    level([(ring_b, 1), (ring_a, -1), (sum_a, 1), (ring_b, -1)], (backward, 1))
+    sum_b = Scatter(ring, send, -1, partials[1])
+    level([(ring_b, 1), (sum_a, -1), (sum_a, 1), (sum_b, -1)], (forward, 1))
+    both = [(sum_a, 1), (sum_a, -1), (sum_b, 1), (sum_b, -1)]
+    level(both, (forward, 2))
+    layer_output = running[-1]
+    def halved(value, bit, *tokens):
+        kept = value.shape[0] // 2
+        other = partner(after(lax.slice_in_dim(value, kept, 2 * kept, axis=0), *tokens), bit)
+        own = lax.slice_in_dim(value, 0, kept, axis=0)
+        return (own.astype(F32) + other.astype(F32)).astype(BF16)
+
+    before = [*done["hops"], *done["work"]]
+    for bit in reversed(bits[1:]):
+        layer_output = halved(layer_output, bit, *before)
+    done["hops"].append(layer_output)
+    level(both, (backward, 2))
+    for _ in range(4, last):
+        level(both)
+    small_sum = Scatter(ring, send, 1, partials[2])
+
+    small_both = [(small_sum, 1), (small_sum, -1)]
+    level([(small_sum, 1), (sum_b, 1), (sum_b, -1)])
+    first = exchanged(sum_a.total(partials[2]), [])
+    layer_output = halved(layer_output, bits[0], first[2])
+    for _ in range(2, last):
+        level(small_both)
+    total = sum_b.total()
+    second = exchanged(total, [layer_output])
+    level(small_both, None, total)
     grads = []
-    for k, (start, size) in enumerate(streams):
-        partial = backward_product(grad_rows, down_codes, down_scales, start, size, tile)
-
-        def term(offset):
-            at = offset % ring * rows
-            return lax.slice_in_dim(partial, at, at + rows, axis=0)
-
-        total = term(0).astype(F32)
-        for step in (1, -1):
-            far = reach(k, step)
-            moving = term(step * far)
-            for hop in range(far - 1, -1, -1):
-                moving = lax.ppermute(moving, "dp", pairs[step])
-                if hop:
-                    moving = (moving.astype(F32) + term(step * hop).astype(F32)).astype(BF16)
-            total = total + moving.astype(F32)
-        own = total.astype(BF16)
-        other = partner(own, bits[0])
-        for previous, bit in zip(bits, bits[1:]):
-            own = paired(own, other, previous)
-            other = partner(own, bit)
+    for k, (start, size) in enumerate(back_streams):
+        own, other, _ = (
+            (first, second)[k] if k < 2 else exchanged(small_sum.total(), [second[2]], grads)
+        )
         grads = local_grads(
-            own, other, last_sign, mix, scale, gate_act, up_act, start, tile, grads
+            own, other, last_sign, mix, scale, gate_act, up_act, start, grads
         )
     gate_grad, up_grad = grads
     return (layer_output, gate_grad, up_grad)

time: 441 us -> 331 us (0.75)
  waiting for transfers between devices: 184 us -> 127 us
  starting transfers between devices: 77.8 us -> 59 us
  between operations: 14.4 us -> 1.05 us
  Pallas kernels: 116 us -> 103 us
  other arithmetic: 27.4 us -> 20.8 us
    ppermute x56 -> x42, waiting for transfers between devices: 146 us -> 90.6 us  [send(): lax.ppermute(value, 'dp', [(cycle[i], cycle[(i + step) % ring]) for i in...]
    ppermute x56 -> x42, starting transfers between devices: 61.9 us -> 43.8 us  [send(): lax.ppermute(value, 'dp', [(cycle[i], cycle[(i + step) % ring]) for i in...]
    pallas_call x4 -> x3, Pallas kernels: 13.1 us -> 7.13 us  [local_grads(): pl.pallas_call(lambda *refs: grads_kernel(scale, tile, *refs), grid=(cols...]
    pallas_call x4 -> x3, Pallas kernels: 53.2 us -> 48.9 us  [forward_product(): pl.pallas_call(lambda *refs: forward_kernel(len(blocks), bits, start // B...]
    pallas_call x4 -> x3, Pallas kernels: 46.9 us -> 43.3 us  [backward_product(): pl.pallas_call(lambda *refs: backward_kernel(start // BLOCK, *refs), grid...]
    convert_element_type x16 -> x14, other arithmetic: 18.7 us -> 15.1 us  [the longest x9 10.9 us: outgoing(): return (self.sums[step].astype(F32) + term.astype(F32)).astype(BF16)]
    ppermute x19 -> x17, waiting for transfers between devices: 38.1 us -> 36.2 us  [partner(): lax.ppermute(value, 'tensor', [(i, i ^ 1 << bit) for i in range(groups)])]
    ppermute x19 -> x17, starting transfers between devices: 15.8 us -> 15.2 us  [partner(): lax.ppermute(value, 'tensor', [(i, i ^ 1 << bit) for i in range(groups)])]
  transfers between devices with their start and end apart: 76 -> 59, of which waited for: 36 -> 28; matrix products, arithmetic and copies ran while one was open for 8% -> 8% of each run, Pallas kernels for 27% -> 31%
where the time goes in v3:
time: 331 us; the launch traced here: 329 us
  waiting for transfers between devices  127 us (38%)
  Pallas kernels  103 us (31%)
  starting transfers between devices  59 us (18%)
  other arithmetic  20.8 us (6%)
  local copies, waits for them, and re-layouts  18.5 us (6%)
    ppermute x42, waiting for transfers between devices, send(): lax.ppermute(value, 'dp', [(cycle[i], cycle[(i + step) % ring]) for i in...  90.6 us
    pallas_call x3, Pallas kernels, forward_product(): pl.pallas_call(lambda *refs: forward_kernel(len(blocks), bits, start // B...  48.9 us
    ppermute x42, starting transfers between devices, send(): lax.ppermute(value, 'dp', [(cycle[i], cycle[(i + step) % ring]) for i in...  43.8 us
    pallas_call x3, Pallas kernels, backward_product(): pl.pallas_call(lambda *refs: backward_kernel(start // BLOCK, *refs), grid...  43.3 us
    ppermute x17, waiting for transfers between devices, partner(): lax.ppermute(value, 'tensor', [(i, i ^ 1 << bit) for i in range(groups)])  36.2 us
    ppermute x17, starting transfers between devices, partner(): lax.ppermute(value, 'tensor', [(i, i ^ 1 << bit) for i in range(groups)])  15.2 us
    convert_element_type x9, other arithmetic, outgoing(): return (self.sums[step].astype(F32) + term.astype(F32)).astype(BF16)  10.9 us
    unnamed x55, local copies, waits for them, and re-layouts  10.2 us
  transfers between devices with their start and end apart: 59, of which 28 were waited for; matrix products, arithmetic and copies ran while one was open for 8% of the time, Pallas kernels for 31%

profile of v3, /device:TPU:0, one launch (start us, length us, event | category | flops | bytes accessed | tf_op | source)
XLA Modules:
  0.0 329.0 jit_solution(1894876599057848570)
XLA Ops:
  1.8 3.0 collective-permute-start
  4.9 3.5 %fusion.8 = (bf16[128,2816]{1,0:T(8,128)(2,1)S(1)}, bf16[128,2816]{1,0:T(8,128)(2,1)}) fusion(bf16[128,6656]{1,0:T(8,128)(2,1)} %refs_5_.5, bf16[128,6656]{1,0:T(8,128)(2,1)} %refs_4_.5), kind=kLoop, calls=%fused_computation.30 | loop fusion | flops 5767168 | bytes 4325376 | tf_op jit(solution)/shard_map/convert_element_type | solution.py:341
  17.0 6.3 %collective-permute-done.5.refs_10_ = bf16[128,1024]{1,0:T(8,128)(2,1)S(1)} collective-permute-done((bf16[128,1024]{1,0:T(8,128)(2,1)S(1)}, bf16[128,1024]{1,0:T(8,128)(2,1)S(1)}, u32[]{:S(2)}, u32[]{:S(2)}) %collective-permute-start.5) | collective-permute-done | bytes 262176 | tf_op jit(solution)/shard_map/ppermute | solution.py:320
  24.5 4.0 %collective-permute-done.1 = bf16[128,2816]{1,0:T(8,128)(2,1)S(1)} collective-permute-done((bf16[128,2816]{1,0:T(8,128)(2,1)S(1)}, bf16[128,2816]{1,0:T(8,128)(2,1)S(1)}, u32[]{:S(2)}, u32[]{:S(2)}) %collective-permute-start.1) | collective-permute-done | bytes 720928 | tf_op jit(solution)/shard_map/ppermute | solution.py:325
  30.9 6.6 %collective-permute-done.6.refs_9_ = bf16[128,1024]{1,0:T(8,128)(2,1)S(1)} collective-permute-done((bf16[128,1024]{1,0:T(8,128)(2,1)S(1)}, bf16[128,1024]{1,0:T(8,128)(2,1)S(1)}, u32[]{:S(2)}, u32[]{:S(2)}) %collective-permute-start.6) | collective-permute-done | bytes 262176 | tf_op jit(solution)/shard_map/ppermute | solution.py:320
  42.8 5.2 %collective-permute-done.9.refs_6_ = bf16[128,1024]{1,0:T(8,128)(2,1)S(1)} collective-permute-done((bf16[128,1024]{1,0:T(8,128)(2,1)S(1)}, bf16[128,1024]{1,0:T(8,128)(2,1)S(1)}, u32[]{:S(2)}, u32[]{:S(2)}) %collective-permute-start.9) | collective-permute-done | bytes 262176 | tf_op jit(solution)/shard_map/ppermute | solution.py:320
  50.9 5.2 %collective-permute-done.7 = bf16[128,2816]{1,0:T(8,128)(2,1)S(1)} collective-permute-done((bf16[128,2816]{1,0:T(8,128)(2,1)S(1)}, bf16[128,2816]{1,0:T(8,128)(2,1)S(1)}, u32[]{:S(2)}, u32[]{:S(2)}) %collective-permute-start.7) | collective-permute-done | bytes 720928 | tf_op jit(solution)/shard_map/ppermute | solution.py:325
  57.9 7.1 %collective-permute-done.14.refs_10_ = bf16[128,2816]{1,0:T(8,128)(2,1)S(1)} collective-permute-done((bf16[128,2816]{1,0:T(8,128)(2,1)S(1)}, bf16[128,2816]{1,0:T(8,128)(2,1)S(1)}, u32[]{:S(2)}, u32[]{:S(2)}) %collective-permute-start.14) | collective-permute-done | bytes 720928 | tf_op jit(solution)/shard_map/ppermute | solution.py:320
  66.3 3.7 %collective-permute-done.13.refs_4_ = bf16[128,2816]{1,0:T(8,128)(2,1)} collective-permute-done((bf16[128,2816]{1,0:T(8,128)(2,1)S(1)}, bf16[128,2816]{1,0:T(8,128)(2,1)}, u32[]{:S(2)}, u32[]{:S(2)}) %collective-permute-start.13) | collective-permute-done | bytes 720928 | tf_op jit(solution)/shard_map/ppermute | solution.py:320
  71.7 8.0 %collective-permute-done.18.refs_4_ = bf16[256,2048]{1,0:T(8,128)(2,1)} collective-permute-done((bf16[256,2048]{1,0:T(8,128)(2,1)S(1)}, bf16[256,2048]{1,0:T(8,128)(2,1)}, u32[]{:S(2)}, u32[]{:S(2)}) %collective-permute-start.18) | collective-permute-done | bytes 1048608 | tf_op jit(solution)/shard_map/ppermute | solution.py:325
  89.5 10.6 %forward_product.3.refs_12_ = f32[1024,2048]{1,0:T(8,128)} custom-call(s32[1]{0:T(128)} %bitcast.refs_0_, s32[16]{0:T(128)S(1)} %dynamic-slice_bitcast_fusion.refs_1_, f32[52,16]{1,0:T(8,128)S(1)} %copy.14.refs_2_.refs_0_, bf16[128,1024]{1,0:T(8,128)(2,1)S(1)} %local_mix.3.refs_3_, bf16[128,1024]{1,0:T(8,128)(2,1)S(1)} %copy-done.8, ...), custom_call_target="tpu_custom_call" | custom-call | flops 268435456 | bytes 1441792 | tf_op jit(solution)/shard_map/forward_product/pallas_call | solution.py:220
  106.3 17.6 %backward_product.3 = bf16[1024,2816]{1,0:T(8,128)(2,1)} custom-call(f32[52,16]{1,0:T(8,128)S(1)} %copy.14.refs_2_.refs_0_, bf16[1024,2048]{1,0:T(8,128)(2,1)S(1)} %arrange_rows.1.refs_1_, bf16[6656,2048]{1,0:T(8,128)(2,1)} %refs_2_.9), custom_call_target="tpu_custom_call" | custom-call | flops 738197504 | bytes 1343488 | tf_op jit(solution)/shard_map/backward_product/pallas_call | solution.py:170
  128.7 6.1 %collective-permute-done.26.refs_9_ = bf16[128,2816]{1,0:T(8,128)(2,1)S(1)} collective-permute-done((bf16[128,2816]{1,0:T(8,128)(2,1)}, bf16[128,2816]{1,0:T(8,128)(2,1)S(1)}, u32[]{:S(2)}, u32[]{:S(2)}) %collective-permute-start.26) | collective-permute-done | bytes 720928 | tf_op jit(solution)/shard_map/ppermute | solution.py:320
  138.0 17.8 %backward_product.4 = bf16[1024,2816]{1,0:T(8,128)(2,1)} custom-call(f32[52,16]{1,0:T(8,128)S(1)} %copy.14.refs_2_.refs_0_, bf16[1024,2048]{1,0:T(8,128)(2,1)S(1)} %arrange_rows.1.refs_1_, bf16[6656,2048]{1,0:T(8,128)(2,1)} %refs_2_.9), custom_call_target="tpu_custom_call" | custom-call | flops 738197504 | bytes 1343488 | tf_op jit(solution)/shard_map/backward_product/pallas_call | solution.py:170
  167.8 19.4 %forward_product.4.refs_12_ = f32[1024,2048]{1,0:T(8,128)} custom-call(s32[1]{0:T(128)} %bitcast.refs_0_, s32[16]{0:T(128)S(1)} %dynamic-slice_bitcast_fusion.refs_1_, f32[52,16]{1,0:T(8,128)S(1)} %copy.14.refs_2_.refs_0_, bf16[128,2816]{1,0:T(8,128)(2,1)S(1)} %local_mix.4.refs_3_, bf16[128,2816]{1,0:T(8,128)(2,1)} %collective-permute-done.13.refs_4_, ...), custom_call_target="tpu_custom_call" | custom-call | flops 738197504 | bytes 2129920 | tf_op jit(solution)/shard_map/forward_product/pallas_call | solution.py:220
  187.2 8.0 %collective-permute-done.31 = bf16[128,2816]{1,0:T(8,128)(2,1)} collective-permute-done((bf16[128,2816]{1,0:T(8,128)(2,1)}, bf16[128,2816]{1,0:T(8,128)(2,1)}, u32[]{:S(2)}, u32[]{:S(2)}) %collective-permute-start.31) | collective-permute-done | bytes 720928 | tf_op jit(solution)/shard_map/ppermute | solution.py:320
  198.8 3.2 add_convert_fusion.13
  204.0 3.4 %copy-done = f32[1024,2048]{1,0:T(8,128)S(1)} copy-done((f32[1024,2048]{1,0:T(8,128)S(1)}, f32[1024,2048]{1,0:T(8,128)}, u32[]{:S(2)}) %copy-start) | copy-done | bytes 8388632
  207.4 18.9 %forward_product.5 = bf16[1024,2048]{1,0:T(8,128)(2,1)} custom-call(s32[1]{0:T(128)} %bitcast.refs_0_, s32[16]{0:T(128)S(1)} %dynamic-slice_bitcast_fusion.refs_1_, f32[52,16]{1,0:T(8,128)S(1)} %copy.14.refs_2_.refs_0_, bf16[128,2816]{1,0:T(8,128)(2,1)S(1)} %local_mix.5.refs_3_, bf16[128,2816]{1,0:T(8,128)(2,1)} %collective-permute-done.15.refs_4_, ...), custom_call_target="tpu_custom_call" | custom-call | flops 738197504 | bytes 2129920 | tf_op jit(solution)/shard_map/forward_product/pallas_call | solution.py:220
  239.1 7.8 %backward_product.5 = bf16[1024,1024]{1,0:T(8,128)(2,1)} custom-call(f32[52,16]{1,0:T(8,128)S(1)} %copy.14.refs_2_.refs_0_, bf16[1024,2048]{1,0:T(8,128)(2,1)S(1)} %arrange_rows.1.refs_1_, bf16[6656,2048]{1,0:T(8,128)(2,1)} %refs_2_.9), custom_call_target="tpu_custom_call" | custom-call | flops 268435456 | bytes 655360 | tf_op jit(solution)/shard_map/backward_product/pallas_call | solution.py:170
  246.9 6.4 %collective-permute-done.40 = bf16[128,2816]{1,0:T(8,128)(2,1)} collective-permute-done((bf16[128,2816]{1,0:T(8,128)(2,1)}, bf16[128,2816]{1,0:T(8,128)(2,1)}, u32[]{:S(2)}, u32[]{:S(2)}) %collective-permute-start.40) | collective-permute-done | bytes 720928 | tf_op jit(solution)/shard_map/ppermute | solution.py:320
  257.7 10.4 %collective-permute-done.48 = bf16[128,2816]{1,0:T(8,128)(2,1)S(1)} collective-permute-done((bf16[128,2816]{1,0:T(8,128)(2,1)S(1)}, bf16[128,2816]{1,0:T(8,128)(2,1)S(1)}, u32[]{:S(2)}, u32[]{:S(2)}) %collective-permute-start.48) | collective-permute-done | bytes 720928 | tf_op jit(solution)/shard_map/ppermute | solution.py:320
  276.0 15.8 %collective-permute-done.51 = bf16[128,1024]{1,0:T(8,128)(2,1)S(1)} collective-permute-done((bf16[128,1024]{1,0:T(8,128)(2,1)S(1)}, bf16[128,1024]{1,0:T(8,128)(2,1)S(1)}, u32[]{:S(2)}, u32[]{:S(2)}) %collective-permute-start.51) | collective-permute-done | bytes 262176 | tf_op jit(solution)/shard_map/ppermute | solution.py:320
  306.2 9.8 %collective-permute-done.54 = bf16[128,2816]{1,0:T(8,128)(2,1)S(1)} collective-permute-done((bf16[128,2816]{1,0:T(8,128)(2,1)S(1)}, bf16[128,2816]{1,0:T(8,128)(2,1)S(1)}, u32[]{:S(2)}, u32[]{:S(2)}) %collective-permute-start.54) | collective-permute-done | bytes 720928 | tf_op jit(solution)/shard_map/ppermute | solution.py:325
  (191 shorter events, 120.0 us)
Async XLA Ops:
  70.0 30.1 %collective-permute-start.21 = (bf16[128,2816]{1,0:T(8,128)(2,1)}, bf16[128,2816]{1,0:T(8,128)(2,1)}, u32[]{:S(2)}, u32[]{:S(2)}) collective-permute-start(bf16[128,2816]{1,0:T(8,128)(2,1)} %collective-permute-done.13.refs_4_), channel_id=1, source_target_pairs={{0,8},{8,16},{16,24},{24,28},{28,20},{20,12},{12,4},{4,0},{1,9},{9... | collective-permute-start | bytes 2162696 | tf_op jit(solution)/shard_map/ppermute | solution.py:320
  71.6 32.1 %collective-permute-start.17 = (bf16[256,2048]{1,0:T(8,128)(2,1)S(1)}, bf16[256,2048]{1,0:T(8,128)(2,1)}, u32[]{:S(2)}, u32[]{:S(2)}) collective-permute-start(bf16[256,2048]{1,0:T(8,128)(2,1)S(1)} %copy-done.4), channel_id=1, source_target_pairs={{0,1},{1,0},{2,3},{3,2},{4,5},{5,4},{6,7},{7,6},{8,9},{9,8},{10,11... | collective-permute-start | bytes 3145736 | tf_op jit(solution)/shard_map/ppermute | solution.py:325
  79.6 24.6 %collective-permute-start.19 = (bf16[256,2048]{1,0:T(8,128)(2,1)}, bf16[256,2048]{1,0:T(8,128)(2,1)}, u32[]{:S(2)}, u32[]{:S(2)}) collective-permute-start(bf16[256,2048]{1,0:T(8,128)(2,1)} %collective-permute-done.18.refs_4_), channel_id=1, source_target_pairs={{0,1},{1,0},{2,3},{3,2},{4,5},{5,4},{6,7},{7,6},{8,9},{9,8},{10,11... | collective-permute-start | bytes 3145736 | tf_op jit(solution)/shard_map/ppermute | solution.py:325
  100.1 23.9 %collective-permute-start.24 = (bf16[128,2816]{1,0:T(8,128)(2,1)}, bf16[128,2816]{1,0:T(8,128)(2,1)S(1)}, u32[]{:S(2)}, u32[]{:S(2)}) collective-permute-start(bf16[128,2816]{1,0:T(8,128)(2,1)} %collective-permute-done.20.refs_9_), channel_id=1, source_target_pairs={{0,4},{8,0},{16,8},{24,16},{28,24},{20,28},{12,20},{4,12},{1,5},{9... | collective-permute-start | bytes 2162696 | tf_op jit(solution)/shard_map/ppermute | solution.py:320
  101.2 33.6 %collective-permute-start.25 = (bf16[128,2816]{1,0:T(8,128)(2,1)}, bf16[128,2816]{1,0:T(8,128)(2,1)S(1)}, u32[]{:S(2)}, u32[]{:S(2)}) collective-permute-start(bf16[128,2816]{1,0:T(8,128)(2,1)} %collective-permute-done.21.refs_5_), channel_id=1, source_target_pairs={{0,8},{8,16},{16,24},{24,28},{28,20},{20,12},{12,4},{4,0},{1,9},{9... | collective-permute-start | bytes 2162696 | tf_op jit(solution)/shard_map/ppermute | solution.py:320
  102.1 33.8 %collective-permute-start.16 = (bf16[128,2816]{1,0:T(8,128)(2,1)}, bf16[128,2816]{1,0:T(8,128)(2,1)S(1)}, u32[]{:S(2)}, u32[]{:S(2)}) collective-permute-start(bf16[128,2816]{1,0:T(8,128)(2,1)} %collective-permute-done.15.refs_4_), channel_id=1, source_target_pairs={{0,8},{8,16},{16,24},{24,28},{28,20},{20,12},{12,4},{4,0},{1,9},{9... | collective-permute-start | bytes 2162696 | tf_op jit(solution)/shard_map/ppermute | solution.py:320
  103.7 31.1 %collective-permute-start.26 = (bf16[128,2816]{1,0:T(8,128)(2,1)}, bf16[128,2816]{1,0:T(8,128)(2,1)S(1)}, u32[]{:S(2)}, u32[]{:S(2)}) collective-permute-start(bf16[128,2816]{1,0:T(8,128)(2,1)} %collective-permute-done.22.refs_10_), channel_id=1, source_target_pairs={{0,4},{8,0},{16,8},{24,16},{28,24},{20,28},{12,20},{4,12},{1,5},{9... | collective-permute-start | bytes 2162696 | tf_op jit(solution)/shard_map/ppermute | solution.py:320
  124.0 39.9 %collective-permute-start.32 = (bf16[128,2816]{1,0:T(8,128)(2,1)S(1)}, bf16[128,2816]{1,0:T(8,128)(2,1)S(1)}, u32[]{:S(2)}, u32[]{:S(2)}) collective-permute-start(bf16[128,2816]{1,0:T(8,128)(2,1)S(1)} %collective-permute-done.24.refs_8_), channel_id=1, source_target_pairs={{0,4},{8,0},{16,8},{24,16},{28,24},{20,28},{12,20},{4,12},{1,5},{9... | collective-permute-start | bytes 2162696 | tf_op jit(solution)/shard_map/ppermute | solution.py:320
  127.8 32.4 %collective-permute-start.29 = (bf16[128,2816]{1,0:T(8,128)(2,1)S(1)}, bf16[128,2816]{1,0:T(8,128)(2,1)S(1)}, u32[]{:S(2)}, u32[]{:S(2)}) collective-permute-start(bf16[128,2816]{1,0:T(8,128)(2,1)S(1)} %get-tuple-element.80), channel_id=1, source_target_pairs={{0,8},{8,16},{16,24},{24,28},{28,20},{20,12},{12,4},{4,0},{1,9},{9... | collective-permute-start | bytes 2162696 | tf_op jit(solution)/shard_map/ppermute | solution.py:320
  136.0 30.9 %collective-permute-start.23 = (bf16[128,2816]{1,0:T(8,128)(2,1)S(1)}, bf16[128,2816]{1,0:T(8,128)(2,1)S(1)}, u32[]{:S(2)}, u32[]{:S(2)}) collective-permute-start(bf16[128,2816]{1,0:T(8,128)(2,1)S(1)} %collective-permute-done.16.refs_5_), channel_id=1, source_target_pairs={{0,8},{8,16},{16,24},{24,28},{28,20},{20,12},{12,4},{4,0},{1,9},{9... | collective-permute-start | bytes 2162696 | tf_op jit(solution)/shard_map/ppermute | solution.py:320
  136.9 30.0 %collective-permute-start.33 = (bf16[128,2816]{1,0:T(8,128)(2,1)S(1)}, bf16[128,2816]{1,0:T(8,128)(2,1)S(1)}, u32[]{:S(2)}, u32[]{:S(2)}) collective-permute-start(bf16[128,2816]{1,0:T(8,128)(2,1)S(1)} %collective-permute-done.26.refs_9_), channel_id=1, source_target_pairs={{0,4},{8,0},{16,8},{24,16},{28,24},{20,28},{12,20},{4,12},{1,5},{9... | collective-permute-start | bytes 2162696 | tf_op jit(solution)/shard_map/ppermute | solution.py:320
  155.8 43.0 %collective-permute-start.28 = (bf16[128,2816]{1,0:T(8,128)(2,1)}, bf16[128,2816]{1,0:T(8,128)(2,1)}, u32[]{:S(2)}, u32[]{:S(2)}) collective-permute-start(bf16[128,2816]{1,0:T(8,128)(2,1)} %get-tuple-element.79), channel_id=1, source_target_pairs={{0,4},{8,0},{16,8},{24,16},{28,24},{20,28},{12,20},{4,12},{1,5},{9... | collective-permute-start | bytes 2162696 | tf_op jit(solution)/shard_map/ppermute | solution.py:320
  160.2 35.1 %collective-permute-start.31 = (bf16[128,2816]{1,0:T(8,128)(2,1)}, bf16[128,2816]{1,0:T(8,128)(2,1)}, u32[]{:S(2)}, u32[]{:S(2)}) collective-permute-start(bf16[128,2816]{1,0:T(8,128)(2,1)} %get-tuple-element.82), channel_id=1, source_target_pairs={{0,4},{8,0},{16,8},{24,16},{28,24},{20,28},{12,20},{4,12},{1,5},{9... | collective-permute-start | bytes 2162696 | tf_op jit(solution)/shard_map/ppermute | solution.py:320
  163.9 34.9 %collective-permute-start.30 = (bf16[128,2816]{1,0:T(8,128)(2,1)}, bf16[128,2816]{1,0:T(8,128)(2,1)}, u32[]{:S(2)}, u32[]{:S(2)}) collective-permute-start(bf16[128,2816]{1,0:T(8,128)(2,1)} %add_convert_fusion.15), channel_id=1, source_target_pairs={{0,8},{8,16},{16,24},{24,28},{28,20},{20,12},{12,4},{4,0},{1,9},{9... | collective-permute-start | bytes 2162696 | tf_op jit(solution)/shard_map/ppermute | solution.py:320
  166.9 37.2 %collective-permute-start.27 = (bf16[128,2816]{1,0:T(8,128)(2,1)S(1)}, bf16[128,2816]{1,0:T(8,128)(2,1)S(1)}, u32[]{:S(2)}, u32[]{:S(2)}) collective-permute-start(bf16[128,2816]{1,0:T(8,128)(2,1)S(1)} %collective-permute-done.23.refs_6_), channel_id=1, source_target_pairs={{0,8},{8,16},{16,24},{24,28},{28,20},{20,12},{12,4},{4,0},{1,9},{9... | collective-permute-start | bytes 2162696 | tf_op jit(solution)/shard_map/ppermute | solution.py:320
  196.7 31.6 %collective-permute-start.37 = (bf16[128,2816]{1,0:T(8,128)(2,1)S(1)}, bf16[128,2816]{1,0:T(8,128)(2,1)S(1)}, u32[]{:S(2)}, u32[]{:S(2)}) collective-permute-start(bf16[128,2816]{1,0:T(8,128)(2,1)S(1)} %add_convert_fusion.12), channel_id=1, source_target_pairs={{0,4},{8,0},{16,8},{24,16},{28,24},{20,28},{12,20},{4,12},{1,5},{9... | collective-permute-start | bytes 2162696 | tf_op jit(solution)/shard_map/ppermute | solution.py:320
  198.3 30.0 %collective-permute-start.36 = (bf16[128,2816]{1,0:T(8,128)(2,1)S(1)}, bf16[128,2816]{1,0:T(8,128)(2,1)S(1)}, u32[]{:S(2)}, u32[]{:S(2)}) collective-permute-start(bf16[128,2816]{1,0:T(8,128)(2,1)S(1)} %copy-done.23), channel_id=1, source_target_pairs={{0,8},{8,16},{16,24},{24,28},{28,20},{20,12},{12,4},{4,0},{1,9},{9... | collective-permute-start | bytes 2162696 | tf_op jit(solution)/shard_map/ppermute | solution.py:320
  202.0 28.8 %collective-permute-start.34 = (bf16[128,2816]{1,0:T(8,128)(2,1)}, bf16[128,2816]{1,0:T(8,128)(2,1)}, u32[]{:S(2)}, u32[]{:S(2)}) collective-permute-start(bf16[128,2816]{1,0:T(8,128)(2,1)} %get-tuple-element.87), channel_id=1, source_target_pairs={{0,8},{8,16},{16,24},{24,28},{28,20},{20,12},{12,4},{4,0},{1,9},{9... | collective-permute-start | bytes 2162696 | tf_op jit(solution)/shard_map/ppermute | solution.py:320
  202.9 27.9 %collective-permute-start.35 = (bf16[128,2816]{1,0:T(8,128)(2,1)}, bf16[128,2816]{1,0:T(8,128)(2,1)}, u32[]{:S(2)}, u32[]{:S(2)}) collective-permute-start(bf16[128,2816]{1,0:T(8,128)(2,1)} %get-tuple-element.88), channel_id=1, source_target_pairs={{0,4},{8,0},{16,8},{24,16},{28,24},{20,28},{12,20},{4,12},{1,5},{9... | collective-permute-start | bytes 2162696 | tf_op jit(solution)/shard_map/ppermute | solution.py:320
  236.1 32.0 %collective-permute-start.48 = (bf16[128,2816]{1,0:T(8,128)(2,1)S(1)}, bf16[128,2816]{1,0:T(8,128)(2,1)S(1)}, u32[]{:S(2)}, u32[]{:S(2)}) collective-permute-start(bf16[128,2816]{1,0:T(8,128)(2,1)S(1)} %get-tuple-element.102), channel_id=1, source_target_pairs={{0,8},{8,16},{16,24},{24,28},{28,20},{20,12},{12,4},{4,0},{1,9},{9... | collective-permute-start | bytes 2162696 | tf_op jit(solution)/shard_map/ppermute | solution.py:320
  236.4 31.7 %collective-permute-start.46 = (bf16[128,2816]{1,0:T(8,128)(2,1)S(1)}, bf16[128,2816]{1,0:T(8,128)(2,1)S(1)}, u32[]{:S(2)}, u32[]{:S(2)}) collective-permute-start(bf16[128,2816]{1,0:T(8,128)(2,1)S(1)} %get-tuple-element.100), channel_id=1, source_target_pairs={{0,4},{8,0},{16,8},{24,16},{28,24},{20,28},{12,20},{4,12},{1,5},{9... | collective-permute-start | bytes 2162696 | tf_op jit(solution)/shard_map/ppermute | solution.py:320
  268.4 28.2 %collective-permute-start.49 = (bf16[128,2816]{1,0:T(8,128)(2,1)S(1)}, bf16[128,2816]{1,0:T(8,128)(2,1)S(1)}, u32[]{:S(2)}, u32[]{:S(2)}) collective-permute-start(bf16[128,2816]{1,0:T(8,128)(2,1)S(1)} %get-tuple-element.103), channel_id=1, source_target_pairs={{0,8},{8,16},{16,24},{24,28},{28,20},{20,12},{12,4},{4,0},{1,9},{9... | collective-permute-start | bytes 2162696 | tf_op jit(solution)/shard_map/ppermute | solution.py:320
  268.8 27.9 %collective-permute-start.47 = (bf16[128,2816]{1,0:T(8,128)(2,1)S(1)}, bf16[128,2816]{1,0:T(8,128)(2,1)S(1)}, u32[]{:S(2)}, u32[]{:S(2)}) collective-permute-start(bf16[128,2816]{1,0:T(8,128)(2,1)S(1)} %get-tuple-element.101), channel_id=1, source_target_pairs={{0,4},{8,0},{16,8},{24,16},{28,24},{20,28},{12,20},{4,12},{1,5},{9... | collective-permute-start | bytes 2162696 | tf_op jit(solution)/shard_map/ppermute | solution.py:320
  274.2 24.2 %collective-permute-start.42 = (bf16[256,2048]{1,0:T(8,128)(2,1)S(1)}, bf16[256,2048]{1,0:T(8,128)(2,1)S(1)}, u32[]{:S(2)}, u32[]{:S(2)}) collective-permute-start(bf16[256,2048]{1,0:T(8,128)(2,1)S(1)} %slice.147), channel_id=1, source_target_pairs={{0,2},{1,3},{2,0},{3,1},{4,6},{5,7},{6,4},{7,5},{8,10},{9,11},{10,... | collective-permute-start | bytes 3145736 | tf_op jit(solution)/shard_map/ppermute | solution.py:325
  (62 other events, 828.8 us)

commit v4 on v3

--- a/solution.py
+++ b/solution.py
@@ -167,6 +167,8 @@
 
 def backward_product(grad_rows, codes, scales, start, cols, tile):
     tokens, depth = grad_rows.shape
+    if start % (2 * tile) == 0 and cols % (2 * tile) == 0:
+        tile *= 2
     return pl.pallas_call(
         lambda *refs: backward_kernel(start // BLOCK, *refs),
         grid=(cols // tile,),
@@ -186,59 +188,79 @@
     )(scales, grad_rows, codes)
 
 
-def forward_kernel(count, bits, row_block, has_sum, group_ref, order_ref, scales_ref, *refs):
-    blocks, codes_ref = refs[:count], refs[count]
-    sum_ref = refs[count + 1] if has_sum else None
-    out_ref, rows_ref, weight_ref = refs[-3:]
+def forward_kernel(counts, bits, row_block, has_sum, group_ref, order_ref, scales_ref, *refs):
+    total_blocks = sum(counts)
+    blocks, codes_ref = refs[:total_blocks], refs[total_blocks]
+    sum_ref = refs[total_blocks + 1] if has_sum else None
+    out_ref, rows_ref, weight_ref, sems = refs[-4:]
     tile = codes_ref.shape[1]
-
-    @pl.when(pl.program_id(0) == 0)
+    per = max(1, counts[0] >> bits)
+    step = pl.program_id(0)
+
+    def copies():
+        column = 0
+        for part, count in enumerate(counts):
+            for r in range(count):
+                i = part * count + r
+                size, width = blocks[i].shape
+                offset = order_ref[r] // per ^ group_ref[0]
+                turned = sum((offset >> k & 1) << bits - 1 - k for k in range(bits))
+                start = pl.multiple_of((turned * per + order_ref[r] % per) * size, size)
+                place = rows_ref.at[pl.ds(start, size), pl.ds(column, width)]
+                yield pltpu.make_async_copy(blocks[i], place, sems.at[i])
+            column += blocks[part * count].shape[1]
+
+    @pl.when(step == 0)
     def _():
-        per = max(1, count >> bits)
-        for r, block in enumerate(blocks):
-            size = block.shape[0]
-            offset = order_ref[r] // per ^ group_ref[0]
-            turned = sum((offset >> i & 1) << bits - 1 - i for i in range(bits))
-            start = (turned * per + order_ref[r] % per) * size
-            rows_ref[pl.ds(pl.multiple_of(start, size), size), :] = block[...]
-
-    dequantize_into(
-        weight_ref, codes_ref, scales_ref, row_block, pl.program_id(0) * (tile // BLOCK)
-    )
+        for copy in copies():
+            copy.start()
+
+    dequantize_into(weight_ref, codes_ref, scales_ref, row_block, step * (tile // BLOCK))
+
+    @pl.when(step == 0)
+    def _():
+        for copy in copies():
+            copy.wait()
+
     total = jnp.dot(rows_ref[...], weight_ref[...], preferred_element_type=F32)
     if has_sum:
         total = total + sum_ref[...]
     out_ref[...] = total.astype(out_ref.dtype)
 
 
-def forward_product(blocks, bits, group, order, codes, scales, start, running, out_dtype):
-    size, depth = blocks[0].shape
-    tokens, width = size * len(blocks), codes.shape[1]
-    tile = min(256, width)
+def forward_product(parts, bits, group, order, codes, scales, start, running, out_dtype):
+    size, count = parts[0][0].shape[0], len(parts[0])
+    depth = sum(blocks[0].shape[1] for blocks in parts)
+    tokens, width = size * count, codes.shape[1]
+    tile = min(512, width)
     sums = [] if running is None else [running]
     sliced = pl.BlockSpec((tokens, tile), lambda i: (0, i))
     return pl.pallas_call(
-        lambda *refs: forward_kernel(len(blocks), bits, start // BLOCK, bool(sums), *refs),
+        lambda *refs: forward_kernel(
+            [count] * len(parts), bits, start // BLOCK, bool(sums), *refs
+        ),
         grid=(width // tile,),
         out_shape=pltpu.HBM((tokens, width), out_dtype),
         in_specs=[
             spec_smem(),
             spec_smem(),
             spec_smem(),
-            *[
-                pl.BlockSpec((size, depth), lambda i: (0, 0), pipeline_mode=pl.Buffered(1))
-            ] * len(blocks),
+            *[pl.BlockSpec(memory_space=pltpu.HBM)] * (count * len(parts)),
             pl.BlockSpec((pl.Element(depth), pl.Element(tile)), lambda i: (start, i * tile)),
             *[sliced] * len(sums),
         ],
         out_specs=sliced,
-        scratch_shapes=[pltpu.VMEM((tokens, depth), BF16), pltpu.VMEM((depth, tile), BF16)],
+        scratch_shapes=[
+            pltpu.VMEM((tokens, depth), BF16),
+            pltpu.VMEM((depth, tile), BF16),
+            pltpu.SemaphoreType.DMA((count * len(parts),)),
+        ],
         compiler_params=params(),
         cost_estimate=cost(
             2 * tokens * depth * width, 2 * (tokens + width) * depth + 8 * tokens * width
         ),
         name="forward_product",
-    )(group, order, scales, *blocks, codes, *sums)
+    )(group, order, scales, *[block for blocks in parts for block in blocks], codes, *sums)
 
 
 def shares(units, parts):
@@ -370,28 +392,24 @@
             hop = [gathers[k].advance(step) for step in (1, -1)]
         if k == 1:
             token += seen
-    held = {0: after(grad_out, *token)}
-    for bit in bits:
-        held.update({o ^ 1 << bit: partner(x, bit) for o, x in list(held.items())})
-        if bit == bits[0]:
-            held = {o: after(x, rotated) for o, x in held.items()}
-    grad_rows = arrange_rows(held, group_index, table)
+    own = after(grad_out, *token)
+    held = {0: own, 1 << bits[0]: partner(own, bits[0])}
     _, ring_a, ring_b = gathers
 
     running, partials = [None], []
 
-    def forward(k, *tokens):
+    def forward(which, *tokens):
         running.append(
             forward_product(
-                gathers[k].all_blocks(),
+                [gathers[k].all_blocks() for k in which],
                 len(bits),
                 group_index,
                 after(table, *tokens),
                 down_codes,
                 down_scales,
-                ahead_streams[k][0],
+                ahead_streams[which[0]][0],
                 running[-1],
-                BF16 if k == len(gathers) - 1 else F32,
+                BF16 if which[-1] == len(gathers) - 1 else F32,
             )
         )
         return running[-1]
@@ -411,15 +429,20 @@
         done["work"] = [work[0](*work[1:], *before)] if work else []
 
     both = [(ring_a, -1), (ring_b, 1), (ring_a, 1), (ring_b, -1)]
-    work = [(forward, 0), (backward, 0)]
-    for _ in range(2, last):
-        level(both, work.pop(0) if work else None)
+    level(both)
+    held = {o: after(x, rotated) for o, x in held.items()}
+    for bit in bits[1:]:
+        held.update({o ^ 1 << bit: partner(x, bit) for o, x in list(held.items())})
+    grad_rows = arrange_rows(held, group_index, table)
+    level(both, (backward, 0))
+    for _ in range(4, last):
+        level(both)
     sum_a = Scatter(ring, send, 1, partials[0])
     level([(ring_b, 1), (ring_a, -1), (sum_a, 1), (ring_b, -1)], (backward, 1))
     sum_b = Scatter(ring, send, -1, partials[1])
-    level([(ring_b, 1), (sum_a, -1), (sum_a, 1), (sum_b, -1)], (forward, 1))
+    level([(ring_b, 1), (sum_a, -1), (sum_a, 1), (sum_b, -1)], (forward, (0, 1)))
     both = [(sum_a, 1), (sum_a, -1), (sum_b, 1), (sum_b, -1)]
-    level(both, (forward, 2))
+    level(both, (forward, (2,)))
     layer_output = running[-1]
     def halved(value, bit, *tokens):
         kept = value.shape[0] // 2

time: 331 us -> 328 us (level)
  local copies, waits for them, and re-layouts: 18.5 us -> 12.3 us
  waiting for transfers between devices: 127 us -> 133 us
    ppermute x42, waiting for transfers between devices: 90.6 us -> 96 us  [send(): lax.ppermute(value, 'dp', [(cycle[i], cycle[(i + step) % ring]) for i in...]
    unnamed x55 -> x63, local copies, waits for them, and re-layouts: 10.2 us -> 6.04 us
    pallas_call x3 -> x2, Pallas kernels: 48.9 us -> 45.9 us  [forward_product(): pl.pallas_call(lambda *refs: forward_kernel([count] * len(parts), bits, s...]
  transfers between devices with their start and end apart: 59 -> 59, of which waited for: 28 -> 31; matrix products, arithmetic and copies ran while one was open for 8% -> 8% of each run, Pallas kernels for 31% -> 30%
where the time goes in v4:
time: 328 us; the launch traced here: 326 us
  waiting for transfers between devices  133 us (41%)
  Pallas kernels  100 us (30%)
  starting transfers between devices  59.9 us (18%)
  other arithmetic  19.9 us (6%)
  local copies, waits for them, and re-layouts  12.3 us (4%)
    ppermute x42, waiting for transfers between devices, send(): lax.ppermute(value, 'dp', [(cycle[i], cycle[(i + step) % ring]) for i in...  96 us
    pallas_call x2, Pallas kernels, forward_product(): pl.pallas_call(lambda *refs: forward_kernel([count] * len(parts), bits, s...  45.9 us
    ppermute x42, starting transfers between devices, send(): lax.ppermute(value, 'dp', [(cycle[i], cycle[(i + step) % ring]) for i in...  45.3 us
    pallas_call x3, Pallas kernels, backward_product(): pl.pallas_call(lambda *refs: backward_kernel(start // BLOCK, *refs), grid...  43.5 us
    ppermute x17, waiting for transfers between devices, partner(): lax.ppermute(value, 'tensor', [(i, i ^ 1 << bit) for i in range(groups)])  37 us
    ppermute x17, starting transfers between devices, partner(): lax.ppermute(value, 'tensor', [(i, i ^ 1 << bit) for i in range(groups)])  14.6 us
    convert_element_type x9, other arithmetic, outgoing(): return (self.sums[step].astype(F32) + term.astype(F32)).astype(BF16)  9.85 us
    pallas_call x3, Pallas kernels, local_grads(): pl.pallas_call(lambda *refs: grads_kernel(scale, tile, *refs), grid=(cols...  7.12 us
  transfers between devices with their start and end apart: 59, of which 31 were waited for; matrix products, arithmetic and copies ran while one was open for 8% of the time, Pallas kernels for 30%

profile of v4, /device:TPU:0, one launch (start us, length us, event | category | flops | bytes accessed | tf_op | source)
XLA Modules:
  0.0 326.4 jit_solution(1312033808431688889)
XLA Ops:
  4.9 3.5 %fusion.8 = (bf16[128,2816]{1,0:T(8,128)(2,1)S(1)}, bf16[128,2816]{1,0:T(8,128)(2,1)}) fusion(bf16[128,6656]{1,0:T(8,128)(2,1)} %refs_5_.5, bf16[128,6656]{1,0:T(8,128)(2,1)} %refs_4_.5), kind=kLoop, calls=%fused_computation.30 | loop fusion | flops 5767168 | bytes 4325376 | tf_op jit(solution)/shard_map/convert_element_type | solution.py:363
  17.0 6.3 %collective-permute-done.5.refs_10_ = bf16[128,1024]{1,0:T(8,128)(2,1)S(1)} collective-permute-done((bf16[128,1024]{1,0:T(8,128)(2,1)S(1)}, bf16[128,1024]{1,0:T(8,128)(2,1)S(1)}, u32[]{:S(2)}, u32[]{:S(2)}) %collective-permute-start.5) | collective-permute-done | bytes 262176 | tf_op jit(solution)/shard_map/ppermute | solution.py:342
  24.5 4.0 %collective-permute-done.1 = bf16[128,2816]{1,0:T(8,128)(2,1)S(1)} collective-permute-done((bf16[128,2816]{1,0:T(8,128)(2,1)S(1)}, bf16[128,2816]{1,0:T(8,128)(2,1)S(1)}, u32[]{:S(2)}, u32[]{:S(2)}) %collective-permute-start.1) | collective-permute-done | bytes 720928 | tf_op jit(solution)/shard_map/ppermute | solution.py:347
  30.9 6.6 %collective-permute-done.6.refs_9_ = bf16[128,1024]{1,0:T(8,128)(2,1)S(1)} collective-permute-done((bf16[128,1024]{1,0:T(8,128)(2,1)S(1)}, bf16[128,1024]{1,0:T(8,128)(2,1)S(1)}, u32[]{:S(2)}, u32[]{:S(2)}) %collective-permute-start.6) | collective-permute-done | bytes 262176 | tf_op jit(solution)/shard_map/ppermute | solution.py:342
  42.8 5.2 %collective-permute-done.9.refs_6_ = bf16[128,1024]{1,0:T(8,128)(2,1)S(1)} collective-permute-done((bf16[128,1024]{1,0:T(8,128)(2,1)S(1)}, bf16[128,1024]{1,0:T(8,128)(2,1)S(1)}, u32[]{:S(2)}, u32[]{:S(2)}) %collective-permute-start.9) | collective-permute-done | bytes 262176 | tf_op jit(solution)/shard_map/ppermute | solution.py:342
  50.9 5.2 %collective-permute-done.7 = bf16[128,2816]{1,0:T(8,128)(2,1)S(1)} collective-permute-done((bf16[128,2816]{1,0:T(8,128)(2,1)S(1)}, bf16[128,2816]{1,0:T(8,128)(2,1)S(1)}, u32[]{:S(2)}, u32[]{:S(2)}) %collective-permute-start.7) | collective-permute-done | bytes 720928 | tf_op jit(solution)/shard_map/ppermute | solution.py:347
  58.6 6.4 %collective-permute-done.14.refs_18_ = bf16[128,2816]{1,0:T(8,128)(2,1)S(1)} collective-permute-done((bf16[128,2816]{1,0:T(8,128)(2,1)S(1)}, bf16[128,2816]{1,0:T(8,128)(2,1)S(1)}, u32[]{:S(2)}, u32[]{:S(2)}) %collective-permute-start.14) | collective-permute-done | bytes 720928 | tf_op jit(solution)/shard_map/ppermute | solution.py:342
  66.3 3.6 %collective-permute-done.13.refs_12_ = bf16[128,2816]{1,0:T(8,128)(2,1)S(1)} collective-permute-done((bf16[128,2816]{1,0:T(8,128)(2,1)S(1)}, bf16[128,2816]{1,0:T(8,128)(2,1)S(1)}, u32[]{:S(2)}, u32[]{:S(2)}) %collective-permute-start.13) | collective-permute-done | bytes 720928 | tf_op jit(solution)/shard_map/ppermute | solution.py:342
  71.5 8.1 %collective-permute-done.18.refs_4_ = bf16[256,2048]{1,0:T(8,128)(2,1)} collective-permute-done((bf16[256,2048]{1,0:T(8,128)(2,1)S(1)}, bf16[256,2048]{1,0:T(8,128)(2,1)}, u32[]{:S(2)}, u32[]{:S(2)}) %collective-permute-start.18) | collective-permute-done | bytes 1048608 | tf_op jit(solution)/shard_map/ppermute | solution.py:347
  82.1 4.4 %collective-permute-done.21.refs_13_ = bf16[128,2816]{1,0:T(8,128)(2,1)S(1)} collective-permute-done((bf16[128,2816]{1,0:T(8,128)(2,1)S(1)}, bf16[128,2816]{1,0:T(8,128)(2,1)S(1)}, u32[]{:S(2)}, u32[]{:S(2)}) %collective-permute-start.21) | collective-permute-done | bytes 720928 | tf_op jit(solution)/shard_map/ppermute | solution.py:342
  89.8 8.9 %collective-permute-done.22.refs_10_ = bf16[128,2816]{1,0:T(8,128)(2,1)} collective-permute-done((bf16[128,2816]{1,0:T(8,128)(2,1)S(1)}, bf16[128,2816]{1,0:T(8,128)(2,1)}, u32[]{:S(2)}, u32[]{:S(2)}) %collective-permute-start.22) | collective-permute-done | bytes 720928 | tf_op jit(solution)/shard_map/ppermute | solution.py:342
  105.0 17.6 %backward_product.3 = bf16[1024,2816]{1,0:T(8,128)(2,1)} custom-call(f32[52,16]{1,0:T(8,128)S(1)} %copy.14.refs_0_.refs_2_, bf16[1024,2048]{1,0:T(8,128)(2,1)S(1)} %arrange_rows.1.refs_1_, bf16[6656,2048]{1,0:T(8,128)(2,1)} %refs_2_.8), custom_call_target="tpu_custom_call" | custom-call | flops 738197504 | bytes 1343488 | tf_op jit(solution)/shard_map/backward_product/pallas_call | solution.py:172
  129.4 3.9 %collective-permute-done.16.refs_5_ = bf16[128,2816]{1,0:T(8,128)(2,1)S(1)} collective-permute-done((bf16[128,2816]{1,0:T(8,128)(2,1)}, bf16[128,2816]{1,0:T(8,128)(2,1)S(1)}, u32[]{:S(2)}, u32[]{:S(2)}) %collective-permute-start.16) | collective-permute-done | bytes 720928 | tf_op jit(solution)/shard_map/ppermute | solution.py:342
  135.4 17.8 %backward_product.4 = bf16[1024,2816]{1,0:T(8,128)(2,1)} custom-call(f32[52,16]{1,0:T(8,128)S(1)} %copy.14.refs_0_.refs_2_, bf16[1024,2048]{1,0:T(8,128)(2,1)S(1)} %arrange_rows.1.refs_1_, bf16[6656,2048]{1,0:T(8,128)(2,1)} %refs_2_.8), custom_call_target="tpu_custom_call" | custom-call | flops 738197504 | bytes 1343488 | tf_op jit(solution)/shard_map/backward_product/pallas_call | solution.py:172
  160.1 4.2 %collective-permute-done.23.refs_6_ = bf16[128,2816]{1,0:T(8,128)(2,1)S(1)} collective-permute-done((bf16[128,2816]{1,0:T(8,128)(2,1)S(1)}, bf16[128,2816]{1,0:T(8,128)(2,1)S(1)}, u32[]{:S(2)}, u32[]{:S(2)}) %collective-permute-start.23) | collective-permute-done | bytes 720928 | tf_op jit(solution)/shard_map/ppermute | solution.py:342
  165.2 25.1 %forward_product.2.refs_12_ = f32[1024,2048]{1,0:T(8,128)} custom-call(s32[1]{0:T(128)} %bitcast.refs_0_, s32[16]{0:T(128)S(1)} %dynamic-slice_bitcast_fusion.refs_1_, f32[52,16]{1,0:T(8,128)S(1)} %copy.14.refs_0_.refs_2_, bf16[128,1024]{1,0:T(8,128)(2,1)S(1)} %local_mix.3.refs_3_, bf16[128,1024]{1,0:T(8,128)(2,1)S(1)} %copy-done.12, ...), custom_call_target="tpu_custom_call" | custom-call | flops 1006632960 | bytes 2523136 | tf_op jit(solution)/shard_map/forward_product/pallas_call | solution.py:238
  199.1 3.4 %copy-done = f32[1024,2048]{1,0:T(8,128)S(1)} copy-done((f32[1024,2048]{1,0:T(8,128)S(1)}, f32[1024,2048]{1,0:T(8,128)}, u32[]{:S(2)}) %copy-start) | copy-done | bytes 8388632
  202.5 20.8 %forward_product.3 = bf16[1024,2048]{1,0:T(8,128)(2,1)} custom-call(s32[1]{0:T(128)} %bitcast.refs_0_, s32[16]{0:T(128)S(1)} %dynamic-slice_bitcast_fusion.refs_1_, f32[52,16]{1,0:T(8,128)S(1)} %copy.14.refs_0_.refs_2_, bf16[128,2816]{1,0:T(8,128)(2,1)S(1)} %local_mix.5.refs_3_, bf16[128,2816]{1,0:T(8,128)(2,1)} %collective-permute-done.15.refs_4_, ...), custom_call_target="tpu_custom_call" | custom-call | flops 738197504 | bytes 2129920 | tf_op jit(solution)/shard_map/forward_product/pallas_call | solution.py:238
  227.6 3.3 add_convert_fusion.11
  236.1 8.2 %backward_product.5 = bf16[1024,1024]{1,0:T(8,128)(2,1)} custom-call(f32[52,16]{1,0:T(8,128)S(1)} %copy.14.refs_0_.refs_2_, bf16[1024,2048]{1,0:T(8,128)(2,1)S(1)} %arrange_rows.1.refs_1_, bf16[6656,2048]{1,0:T(8,128)(2,1)} %refs_2_.8), custom_call_target="tpu_custom_call" | custom-call | flops 268435456 | bytes 655360 | tf_op jit(solution)/shard_map/backward_product/pallas_call | solution.py:172
  244.3 6.5 %collective-permute-done.40 = bf16[128,2816]{1,0:T(8,128)(2,1)} collective-permute-done((bf16[128,2816]{1,0:T(8,128)(2,1)}, bf16[128,2816]{1,0:T(8,128)(2,1)}, u32[]{:S(2)}, u32[]{:S(2)}) %collective-permute-start.40) | collective-permute-done | bytes 720928 | tf_op jit(solution)/shard_map/ppermute | solution.py:342
  255.9 9.6 %collective-permute-done.48 = bf16[128,2816]{1,0:T(8,128)(2,1)S(1)} collective-permute-done((bf16[128,2816]{1,0:T(8,128)(2,1)S(1)}, bf16[128,2816]{1,0:T(8,128)(2,1)S(1)}, u32[]{:S(2)}, u32[]{:S(2)}) %collective-permute-start.48) | collective-permute-done | bytes 720928 | tf_op jit(solution)/shard_map/ppermute | solution.py:342
  273.6 16.5 %collective-permute-done.51 = bf16[128,1024]{1,0:T(8,128)(2,1)S(1)} collective-permute-done((bf16[128,1024]{1,0:T(8,128)(2,1)S(1)}, bf16[128,1024]{1,0:T(8,128)(2,1)S(1)}, u32[]{:S(2)}, u32[]{:S(2)}) %collective-permute-start.51) | collective-permute-done | bytes 262176 | tf_op jit(solution)/shard_map/ppermute | solution.py:342
  303.4 10.0 %collective-permute-done.54 = bf16[128,2816]{1,0:T(8,128)(2,1)S(1)} collective-permute-done((bf16[128,2816]{1,0:T(8,128)(2,1)S(1)}, bf16[128,2816]{1,0:T(8,128)(2,1)S(1)}, u32[]{:S(2)}, u32[]{:S(2)}) %collective-permute-start.54) | collective-permute-done | bytes 720928 | tf_op jit(solution)/shard_map/ppermute | solution.py:347
  (197 shorter events, 116.2 us)
Async XLA Ops:
  56.0 23.6 %collective-permute-start.18 = (bf16[256,2048]{1,0:T(8,128)(2,1)S(1)}, bf16[256,2048]{1,0:T(8,128)(2,1)}, u32[]{:S(2)}, u32[]{:S(2)}) collective-permute-start(bf16[256,2048]{1,0:T(8,128)(2,1)S(1)} %copy-done.4), channel_id=1, source_target_pairs={{0,2},{1,3},{2,0},{3,1},{4,6},{5,7},{6,4},{7,5},{8,10},{9,11},{10,... | collective-permute-start | bytes 3145736 | tf_op jit(solution)/shard_map/ppermute | solution.py:347
  71.4 31.0 %collective-permute-start.17 = (bf16[256,2048]{1,0:T(8,128)(2,1)S(1)}, bf16[256,2048]{1,0:T(8,128)(2,1)}, u32[]{:S(2)}, u32[]{:S(2)}) collective-permute-start(bf16[256,2048]{1,0:T(8,128)(2,1)S(1)} %copy-done.4), channel_id=1, source_target_pairs={{0,1},{1,0},{2,3},{3,2},{4,5},{5,4},{6,7},{7,6},{8,9},{9,8},{10,11... | collective-permute-start | bytes 3145736 | tf_op jit(solution)/shard_map/ppermute | solution.py:347
  79.6 23.3 %collective-permute-start.19 = (bf16[256,2048]{1,0:T(8,128)(2,1)}, bf16[256,2048]{1,0:T(8,128)(2,1)}, u32[]{:S(2)}, u32[]{:S(2)}) collective-permute-start(bf16[256,2048]{1,0:T(8,128)(2,1)} %collective-permute-done.18.refs_4_), channel_id=1, source_target_pairs={{0,1},{1,0},{2,3},{3,2},{4,5},{5,4},{6,7},{7,6},{8,9},{9,8},{10,11... | collective-permute-start | bytes 3145736 | tf_op jit(solution)/shard_map/ppermute | solution.py:347
  87.4 35.3 %collective-permute-start.24 = (bf16[128,2816]{1,0:T(8,128)(2,1)}, bf16[128,2816]{1,0:T(8,128)(2,1)}, u32[]{:S(2)}, u32[]{:S(2)}) collective-permute-start(bf16[128,2816]{1,0:T(8,128)(2,1)} %collective-permute-done.20.refs_17_), channel_id=1, source_target_pairs={{0,4},{8,0},{16,8},{24,16},{28,24},{20,28},{12,20},{4,12},{1,5},{9... | collective-permute-start | bytes 2162696 | tf_op jit(solution)/shard_map/ppermute | solution.py:342
  98.6 30.8 %collective-permute-start.25 = (bf16[128,2816]{1,0:T(8,128)(2,1)}, bf16[128,2816]{1,0:T(8,128)(2,1)S(1)}, u32[]{:S(2)}, u32[]{:S(2)}) collective-permute-start(bf16[128,2816]{1,0:T(8,128)(2,1)} %copy-done.7), channel_id=1, source_target_pairs={{0,8},{8,16},{16,24},{24,28},{28,20},{20,12},{12,4},{4,0},{1,9},{9... | collective-permute-start | bytes 2162696 | tf_op jit(solution)/shard_map/ppermute | solution.py:342
  100.9 28.6 %collective-permute-start.26 = (bf16[128,2816]{1,0:T(8,128)(2,1)}, bf16[128,2816]{1,0:T(8,128)(2,1)S(1)}, u32[]{:S(2)}, u32[]{:S(2)}) collective-permute-start(bf16[128,2816]{1,0:T(8,128)(2,1)} %collective-permute-done.22.refs_10_), channel_id=1, source_target_pairs={{0,4},{8,0},{16,8},{24,16},{28,24},{20,28},{12,20},{4,12},{1,5},{9... | collective-permute-start | bytes 2162696 | tf_op jit(solution)/shard_map/ppermute | solution.py:342
  102.5 30.9 %collective-permute-start.16 = (bf16[128,2816]{1,0:T(8,128)(2,1)}, bf16[128,2816]{1,0:T(8,128)(2,1)S(1)}, u32[]{:S(2)}, u32[]{:S(2)}) collective-permute-start(bf16[128,2816]{1,0:T(8,128)(2,1)} %collective-permute-done.15.refs_4_), channel_id=1, source_target_pairs={{0,8},{8,16},{16,24},{24,28},{28,20},{20,12},{12,4},{4,0},{1,9},{9... | collective-permute-start | bytes 2162696 | tf_op jit(solution)/shard_map/ppermute | solution.py:342
  122.7 36.9 %collective-permute-start.32 = (bf16[128,2816]{1,0:T(8,128)(2,1)}, bf16[128,2816]{1,0:T(8,128)(2,1)S(1)}, u32[]{:S(2)}, u32[]{:S(2)}) collective-permute-start(bf16[128,2816]{1,0:T(8,128)(2,1)} %collective-permute-done.24.refs_16_), channel_id=1, source_target_pairs={{0,4},{8,0},{16,8},{24,16},{28,24},{20,28},{12,20},{4,12},{1,5},{9... | collective-permute-start | bytes 2162696 | tf_op jit(solution)/shard_map/ppermute | solution.py:342
  125.9 30.7 %collective-permute-start.29 = (bf16[128,2816]{1,0:T(8,128)(2,1)S(1)}, bf16[128,2816]{1,0:T(8,128)(2,1)S(1)}, u32[]{:S(2)}, u32[]{:S(2)}) collective-permute-start(bf16[128,2816]{1,0:T(8,128)(2,1)S(1)} %get-tuple-element.70), channel_id=1, source_target_pairs={{0,8},{8,16},{16,24},{24,28},{28,20},{20,12},{12,4},{4,0},{1,9},{9... | collective-permute-start | bytes 2162696 | tf_op jit(solution)/shard_map/ppermute | solution.py:342
  133.4 30.9 %collective-permute-start.23 = (bf16[128,2816]{1,0:T(8,128)(2,1)S(1)}, bf16[128,2816]{1,0:T(8,128)(2,1)S(1)}, u32[]{:S(2)}, u32[]{:S(2)}) collective-permute-start(bf16[128,2816]{1,0:T(8,128)(2,1)S(1)} %collective-permute-done.16.refs_5_), channel_id=1, source_target_pairs={{0,8},{8,16},{16,24},{24,28},{28,20},{20,12},{12,4},{4,0},{1,9},{9... | collective-permute-start | bytes 2162696 | tf_op jit(solution)/shard_map/ppermute | solution.py:342
  134.3 30.0 %collective-permute-start.33 = (bf16[128,2816]{1,0:T(8,128)(2,1)S(1)}, bf16[128,2816]{1,0:T(8,128)(2,1)S(1)}, u32[]{:S(2)}, u32[]{:S(2)}) collective-permute-start(bf16[128,2816]{1,0:T(8,128)(2,1)S(1)} %collective-permute-done.26.refs_9_), channel_id=1, source_target_pairs={{0,4},{8,0},{16,8},{24,16},{28,24},{20,28},{12,20},{4,12},{1,5},{9... | collective-permute-start | bytes 2162696 | tf_op jit(solution)/shard_map/ppermute | solution.py:342
  153.2 41.1 %collective-permute-start.28 = (bf16[128,2816]{1,0:T(8,128)(2,1)S(1)}, bf16[128,2816]{1,0:T(8,128)(2,1)S(1)}, u32[]{:S(2)}, u32[]{:S(2)}) collective-permute-start(bf16[128,2816]{1,0:T(8,128)(2,1)S(1)} %get-tuple-element.69), channel_id=1, source_target_pairs={{0,4},{8,0},{16,8},{24,16},{28,24},{20,28},{12,20},{4,12},{1,5},{9... | collective-permute-start | bytes 2162696 | tf_op jit(solution)/shard_map/ppermute | solution.py:342
  156.6 34.2 %collective-permute-start.31 = (bf16[128,2816]{1,0:T(8,128)(2,1)S(1)}, bf16[128,2816]{1,0:T(8,128)(2,1)S(1)}, u32[]{:S(2)}, u32[]{:S(2)}) collective-permute-start(bf16[128,2816]{1,0:T(8,128)(2,1)S(1)} %get-tuple-element.72), channel_id=1, source_target_pairs={{0,4},{8,0},{16,8},{24,16},{28,24},{20,28},{12,20},{4,12},{1,5},{9... | collective-permute-start | bytes 2162696 | tf_op jit(solution)/shard_map/ppermute | solution.py:342
  159.6 34.7 %collective-permute-start.30 = (bf16[128,2816]{1,0:T(8,128)(2,1)S(1)}, bf16[128,2816]{1,0:T(8,128)(2,1)S(1)}, u32[]{:S(2)}, u32[]{:S(2)}) collective-permute-start(bf16[128,2816]{1,0:T(8,128)(2,1)S(1)} %add_convert_fusion.15), channel_id=1, source_target_pairs={{0,8},{8,16},{16,24},{24,28},{28,20},{20,12},{12,4},{4,0},{1,9},{9... | collective-permute-start | bytes 2162696 | tf_op jit(solution)/shard_map/ppermute | solution.py:342
  164.3 34.8 %collective-permute-start.27 = (bf16[128,2816]{1,0:T(8,128)(2,1)S(1)}, bf16[128,2816]{1,0:T(8,128)(2,1)S(1)}, u32[]{:S(2)}, u32[]{:S(2)}) collective-permute-start(bf16[128,2816]{1,0:T(8,128)(2,1)S(1)} %collective-permute-done.23.refs_6_), channel_id=1, source_target_pairs={{0,8},{8,16},{16,24},{24,28},{28,20},{20,12},{12,4},{4,0},{1,9},{9... | collective-permute-start | bytes 2162696 | tf_op jit(solution)/shard_map/ppermute | solution.py:342
  192.2 33.1 %collective-permute-start.37 = (bf16[128,2816]{1,0:T(8,128)(2,1)S(1)}, bf16[128,2816]{1,0:T(8,128)(2,1)S(1)}, u32[]{:S(2)}, u32[]{:S(2)}) collective-permute-start(bf16[128,2816]{1,0:T(8,128)(2,1)S(1)} %add_convert_fusion.12), channel_id=1, source_target_pairs={{0,4},{8,0},{16,8},{24,16},{28,24},{20,28},{12,20},{4,12},{1,5},{9... | collective-permute-start | bytes 2162696 | tf_op jit(solution)/shard_map/ppermute | solution.py:342
  193.8 31.5 %collective-permute-start.36 = (bf16[128,2816]{1,0:T(8,128)(2,1)S(1)}, bf16[128,2816]{1,0:T(8,128)(2,1)S(1)}, u32[]{:S(2)}, u32[]{:S(2)}) collective-permute-start(bf16[128,2816]{1,0:T(8,128)(2,1)S(1)} %get-tuple-element.79), channel_id=1, source_target_pairs={{0,8},{8,16},{16,24},{24,28},{28,20},{20,12},{12,4},{4,0},{1,9},{9... | collective-permute-start | bytes 2162696 | tf_op jit(solution)/shard_map/ppermute | solution.py:342
  197.1 29.7 %collective-permute-start.34 = (bf16[128,2816]{1,0:T(8,128)(2,1)}, bf16[128,2816]{1,0:T(8,128)(2,1)S(1)}, u32[]{:S(2)}, u32[]{:S(2)}) collective-permute-start(bf16[128,2816]{1,0:T(8,128)(2,1)} %get-tuple-element.77), channel_id=1, source_target_pairs={{0,8},{8,16},{16,24},{24,28},{28,20},{20,12},{12,4},{4,0},{1,9},{9... | collective-permute-start | bytes 2162696 | tf_op jit(solution)/shard_map/ppermute | solution.py:342
  198.3 29.3 %collective-permute-start.35 = (bf16[128,2816]{1,0:T(8,128)(2,1)}, bf16[128,2816]{1,0:T(8,128)(2,1)}, u32[]{:S(2)}, u32[]{:S(2)}) collective-permute-start(bf16[128,2816]{1,0:T(8,128)(2,1)} %get-tuple-element.78), channel_id=1, source_target_pairs={{0,4},{8,0},{16,8},{24,16},{28,24},{20,28},{12,20},{4,12},{1,5},{9... | collective-permute-start | bytes 2162696 | tf_op jit(solution)/shard_map/ppermute | solution.py:342
  233.3 32.2 %collective-permute-start.48 = (bf16[128,2816]{1,0:T(8,128)(2,1)S(1)}, bf16[128,2816]{1,0:T(8,128)(2,1)S(1)}, u32[]{:S(2)}, u32[]{:S(2)}) collective-permute-start(bf16[128,2816]{1,0:T(8,128)(2,1)S(1)} %get-tuple-element.92), channel_id=1, source_target_pairs={{0,8},{8,16},{16,24},{24,28},{28,20},{20,12},{12,4},{4,0},{1,9},{9... | collective-permute-start | bytes 2162696 | tf_op jit(solution)/shard_map/ppermute | solution.py:342
  233.9 31.5 %collective-permute-start.46 = (bf16[128,2816]{1,0:T(8,128)(2,1)S(1)}, bf16[128,2816]{1,0:T(8,128)(2,1)S(1)}, u32[]{:S(2)}, u32[]{:S(2)}) collective-permute-start(bf16[128,2816]{1,0:T(8,128)(2,1)S(1)} %get-tuple-element.90), channel_id=1, source_target_pairs={{0,4},{8,0},{16,8},{24,16},{28,24},{20,28},{12,20},{4,12},{1,5},{9... | collective-permute-start | bytes 2162696 | tf_op jit(solution)/shard_map/ppermute | solution.py:342
  265.8 28.2 %collective-permute-start.49 = (bf16[128,2816]{1,0:T(8,128)(2,1)S(1)}, bf16[128,2816]{1,0:T(8,128)(2,1)S(1)}, u32[]{:S(2)}, u32[]{:S(2)}) collective-permute-start(bf16[128,2816]{1,0:T(8,128)(2,1)S(1)} %get-tuple-element.93), channel_id=1, source_target_pairs={{0,8},{8,16},{16,24},{24,28},{28,20},{20,12},{12,4},{4,0},{1,9},{9... | collective-permute-start | bytes 2162696 | tf_op jit(solution)/shard_map/ppermute | solution.py:342
  267.4 26.6 %collective-permute-start.47 = (bf16[128,2816]{1,0:T(8,128)(2,1)S(1)}, bf16[128,2816]{1,0:T(8,128)(2,1)S(1)}, u32[]{:S(2)}, u32[]{:S(2)}) collective-permute-start(bf16[128,2816]{1,0:T(8,128)(2,1)S(1)} %get-tuple-element.91), channel_id=1, source_target_pairs={{0,4},{8,0},{16,8},{24,16},{28,24},{20,28},{12,20},{4,12},{1,5},{9... | collective-permute-start | bytes 2162696 | tf_op jit(solution)/shard_map/ppermute | solution.py:342
  272.0 24.1 %collective-permute-start.42 = (bf16[256,2048]{1,0:T(8,128)(2,1)S(1)}, bf16[256,2048]{1,0:T(8,128)(2,1)S(1)}, u32[]{:S(2)}, u32[]{:S(2)}) collective-permute-start(bf16[256,2048]{1,0:T(8,128)(2,1)S(1)} %slice.147), channel_id=1, source_target_pairs={{0,2},{1,3},{2,0},{3,1},{4,6},{5,7},{6,4},{7,5},{8,10},{9,11},{10,... | collective-permute-start | bytes 3145736 | tf_op jit(solution)/shard_map/ppermute | solution.py:347
  (66 other events, 805.0 us)

commit v5 on v4

--- a/solution.py
+++ b/solution.py
@@ -191,8 +191,8 @@
 def forward_kernel(counts, bits, row_block, has_sum, group_ref, order_ref, scales_ref, *refs):
     total_blocks = sum(counts)
     blocks, codes_ref = refs[:total_blocks], refs[total_blocks]
-    sum_ref = refs[total_blocks + 1] if has_sum else None
-    out_ref, rows_ref, weight_ref, sems = refs[-4:]
+    rows_ref, weight_ref, sems, sum_tile_ref, sum_sem = refs[-5:]
+    out_refs = refs[total_blocks + 1 + has_sum : -5]
     tile = codes_ref.shape[1]
     per = max(1, counts[0] >> bits)
     step = pl.program_id(0)
@@ -210,11 +210,18 @@
                 yield pltpu.make_async_copy(blocks[i], place, sems.at[i])
             column += blocks[part * count].shape[1]
 
+    def sum_copy():
+        columns = pl.ds(pl.multiple_of(step * tile, tile), tile)
+        sum_ref = refs[total_blocks + 1]
+        return pltpu.make_async_copy(sum_ref.at[:, columns], sum_tile_ref, sum_sem)
+
     @pl.when(step == 0)
     def _():
         for copy in copies():
             copy.start()
 
+    if has_sum:
+        sum_copy().start()
     dequantize_into(weight_ref, codes_ref, scales_ref, row_block, step * (tile // BLOCK))
 
     @pl.when(step == 0)
@@ -224,36 +231,42 @@
 
     total = jnp.dot(rows_ref[...], weight_ref[...], preferred_element_type=F32)
     if has_sum:
-        total = total + sum_ref[...]
-    out_ref[...] = total.astype(out_ref.dtype)
-
-
-def forward_product(parts, bits, group, order, codes, scales, start, running, out_dtype):
+        sum_copy().wait()
+        total = total + sum_tile_ref[...]
+    size = total.shape[0] // len(out_refs)
+    for i, out_ref in enumerate(out_refs):
+        out_ref[...] = total[i * size : (i + 1) * size].astype(out_ref.dtype)
+
+
+def forward_product(parts, bits, group, order, codes, scales, start, running, final):
     size, count = parts[0][0].shape[0], len(parts[0])
     depth = sum(blocks[0].shape[1] for blocks in parts)
     tokens, width = size * count, codes.shape[1]
-    tile = min(512, width)
+    tile = min(256, width)
     sums = [] if running is None else [running]
-    sliced = pl.BlockSpec((tokens, tile), lambda i: (0, i))
+    halves = 2 if final else 1
+    made = jax.ShapeDtypeStruct((tokens // halves, width), BF16 if final else F32)
     return pl.pallas_call(
         lambda *refs: forward_kernel(
-            [count] * len(parts), bits, start // BLOCK, bool(sums), *refs
+            [count] * len(parts), bits, start // BLOCK, len(sums), *refs
         ),
         grid=(width // tile,),
-        out_shape=pltpu.HBM((tokens, width), out_dtype),
+        out_shape=[pltpu.HBM(made.shape, made.dtype)] * halves,
         in_specs=[
             spec_smem(),
             spec_smem(),
             spec_smem(),
             *[pl.BlockSpec(memory_space=pltpu.HBM)] * (count * len(parts)),
             pl.BlockSpec((pl.Element(depth), pl.Element(tile)), lambda i: (start, i * tile)),
-            *[sliced] * len(sums),
+            *[pl.BlockSpec(memory_space=pltpu.HBM)] * len(sums),
         ],
-        out_specs=sliced,
+        out_specs=[pl.BlockSpec((made.shape[0], tile), lambda i: (0, i))] * halves,
         scratch_shapes=[
             pltpu.VMEM((tokens, depth), BF16),
             pltpu.VMEM((depth, tile), BF16),
             pltpu.SemaphoreType.DMA((count * len(parts),)),
+            pltpu.VMEM((tokens, tile), F32),
+            pltpu.SemaphoreType.DMA,
         ],
         compiler_params=params(),
         cost_estimate=cost(
@@ -396,7 +409,7 @@
     held = {0: own, 1 << bits[0]: partner(own, bits[0])}
     _, ring_a, ring_b = gathers
 
-    running, partials = [None], []
+    running, partials = [[None]], []
 
     def forward(which, *tokens):
         running.append(
@@ -408,11 +421,11 @@
                 down_codes,
                 down_scales,
                 ahead_streams[which[0]][0],
-                running[-1],
-                BF16 if which[-1] == len(gathers) - 1 else F32,
+                running[-1][0],
+                which[-1] == len(gathers) - 1,
             )
         )
-        return running[-1]
+        return running[-1][0]
 
     def backward(k, *tokens):
         start, cols = back_streams[k]
@@ -443,17 +456,21 @@
     level([(ring_b, 1), (sum_a, -1), (sum_a, 1), (sum_b, -1)], (forward, (0, 1)))
     both = [(sum_a, 1), (sum_a, -1), (sum_b, 1), (sum_b, -1)]
     level(both, (forward, (2,)))
-    layer_output = running[-1]
-    def halved(value, bit, *tokens):
+    halves = running[-1]
+    def halves_of(value):
         kept = value.shape[0] // 2
-        other = partner(after(lax.slice_in_dim(value, kept, 2 * kept, axis=0), *tokens), bit)
-        own = lax.slice_in_dim(value, 0, kept, axis=0)
+        return [lax.slice_in_dim(value, at, at + kept, axis=0) for at in (0, kept)]
+
+    def halved(halves, bit, *tokens):
+        own, sent = halves
+        other = partner(after(sent, *tokens), bit)
         return (own.astype(F32) + other.astype(F32)).astype(BF16)
 
     before = [*done["hops"], *done["work"]]
     for bit in reversed(bits[1:]):
-        layer_output = halved(layer_output, bit, *before)
-    done["hops"].append(layer_output)
+        summed = halved(halves, bit, *before)
+        halves = halves_of(summed)
+    done["hops"].append(summed)
     level(both, (backward, 2))
     for _ in range(4, last):
         level(both)
@@ -462,7 +479,7 @@
     small_both = [(small_sum, 1), (small_sum, -1)]
     level([(small_sum, 1), (sum_b, 1), (sum_b, -1)])
     first = exchanged(sum_a.total(partials[2]), [])
-    layer_output = halved(layer_output, bits[0], first[2])
+    layer_output = halved(halves, bits[0], first[2])
     for _ in range(2, last):
         level(small_both)
     total = sum_b.total()

time: 328 us -> 328 us (level)
  Pallas kernels: 100 us -> 106 us
    pallas_call x2, Pallas kernels: 45.9 us -> 51.1 us  [forward_product(): pl.pallas_call(lambda *refs: forward_kernel([count] * len(parts), bits, s...]
    ppermute x42, waiting for transfers between devices: 96 us -> 92.6 us  [send(): lax.ppermute(value, 'dp', [(cycle[i], cycle[(i + step) % ring]) for i in...]
  transfers between devices with their start and end apart: 59 -> 59, of which waited for: 31 -> 29; matrix products, arithmetic and copies ran while one was open for 8% -> 7% of each run, Pallas kernels for 30% -> 32%
where the time goes in v5:
time: 328 us; the launch traced here: 327 us
  waiting for transfers between devices  131 us (40%)
  Pallas kernels  106 us (32%)
  starting transfers between devices  59.9 us (18%)
  other arithmetic  19.7 us (6%)
  local copies, waits for them, and re-layouts  9.48 us (3%)
    ppermute x42, waiting for transfers between devices, send(): lax.ppermute(value, 'dp', [(cycle[i], cycle[(i + step) % ring]) for i in...  92.6 us
    pallas_call x2, Pallas kernels, forward_product(): pl.pallas_call(lambda *refs: forward_kernel([count] * len(parts), bits, s...  51.1 us
    ppermute x42, starting transfers between devices, send(): lax.ppermute(value, 'dp', [(cycle[i], cycle[(i + step) % ring]) for i in...  45.4 us
    pallas_call x3, Pallas kernels, backward_product(): pl.pallas_call(lambda *refs: backward_kernel(start // BLOCK, *refs), grid...  43.6 us
    ppermute x17, waiting for transfers between devices, partner(): lax.ppermute(value, 'tensor', [(i, i ^ 1 << bit) for i in range(groups)])  38.3 us
    ppermute x17, starting transfers between devices, partner(): lax.ppermute(value, 'tensor', [(i, i ^ 1 << bit) for i in range(groups)])  14.6 us
    convert_element_type x9, other arithmetic, outgoing(): return (self.sums[step].astype(F32) + term.astype(F32)).astype(BF16)  11.1 us
    pallas_call x3, Pallas kernels, local_grads(): pl.pallas_call(lambda *refs: grads_kernel(scale, tile, *refs), grid=(cols...  7.12 us
  transfers between devices with their start and end apart: 59, of which 29 were waited for; matrix products, arithmetic and copies ran while one was open for 7% of the time, Pallas kernels for 32%

profile of v5, /device:TPU:0, one launch (start us, length us, event | category | flops | bytes accessed | tf_op | source)
XLA Modules:
  0.0 326.6 jit_solution(16616042954072967951)
XLA Ops:
  1.8 3.0 collective-permute-start
  4.9 3.5 %fusion.8 = (bf16[128,2816]{1,0:T(8,128)(2,1)S(1)}, bf16[128,2816]{1,0:T(8,128)(2,1)}) fusion(bf16[128,6656]{1,0:T(8,128)(2,1)} %refs_5_.5, bf16[128,6656]{1,0:T(8,128)(2,1)} %refs_4_.5), kind=kLoop, calls=%fused_computation.30 | loop fusion | flops 5767168 | bytes 4325376 | tf_op jit(solution)/shard_map/convert_element_type | solution.py:376
  17.0 6.3 %collective-permute-done.5.refs_10_ = bf16[128,1024]{1,0:T(8,128)(2,1)S(1)} collective-permute-done((bf16[128,1024]{1,0:T(8,128)(2,1)S(1)}, bf16[128,1024]{1,0:T(8,128)(2,1)S(1)}, u32[]{:S(2)}, u32[]{:S(2)}) %collective-permute-start.5) | collective-permute-done | bytes 262176 | tf_op jit(solution)/shard_map/ppermute | solution.py:355
  24.5 4.0 %collective-permute-done.1 = bf16[128,2816]{1,0:T(8,128)(2,1)S(1)} collective-permute-done((bf16[128,2816]{1,0:T(8,128)(2,1)S(1)}, bf16[128,2816]{1,0:T(8,128)(2,1)S(1)}, u32[]{:S(2)}, u32[]{:S(2)}) %collective-permute-start.1) | collective-permute-done | bytes 720928 | tf_op jit(solution)/shard_map/ppermute | solution.py:360
  30.9 6.6 %collective-permute-done.6.refs_9_ = bf16[128,1024]{1,0:T(8,128)(2,1)S(1)} collective-permute-done((bf16[128,1024]{1,0:T(8,128)(2,1)S(1)}, bf16[128,1024]{1,0:T(8,128)(2,1)S(1)}, u32[]{:S(2)}, u32[]{:S(2)}) %collective-permute-start.6) | collective-permute-done | bytes 262176 | tf_op jit(solution)/shard_map/ppermute | solution.py:355
  42.9 5.2 %collective-permute-done.9.refs_6_ = bf16[128,1024]{1,0:T(8,128)(2,1)S(1)} collective-permute-done((bf16[128,1024]{1,0:T(8,128)(2,1)S(1)}, bf16[128,1024]{1,0:T(8,128)(2,1)S(1)}, u32[]{:S(2)}, u32[]{:S(2)}) %collective-permute-start.9) | collective-permute-done | bytes 262176 | tf_op jit(solution)/shard_map/ppermute | solution.py:355
  50.9 5.1 %collective-permute-done.7 = bf16[128,2816]{1,0:T(8,128)(2,1)S(1)} collective-permute-done((bf16[128,2816]{1,0:T(8,128)(2,1)S(1)}, bf16[128,2816]{1,0:T(8,128)(2,1)S(1)}, u32[]{:S(2)}, u32[]{:S(2)}) %collective-permute-start.7) | collective-permute-done | bytes 720928 | tf_op jit(solution)/shard_map/ppermute | solution.py:360
  58.6 6.5 %collective-permute-done.14.refs_18_ = bf16[128,2816]{1,0:T(8,128)(2,1)S(1)} collective-permute-done((bf16[128,2816]{1,0:T(8,128)(2,1)S(1)}, bf16[128,2816]{1,0:T(8,128)(2,1)S(1)}, u32[]{:S(2)}, u32[]{:S(2)}) %collective-permute-start.14) | collective-permute-done | bytes 720928 | tf_op jit(solution)/shard_map/ppermute | solution.py:355
  66.3 3.6 %collective-permute-done.13.refs_12_ = bf16[128,2816]{1,0:T(8,128)(2,1)S(1)} collective-permute-done((bf16[128,2816]{1,0:T(8,128)(2,1)S(1)}, bf16[128,2816]{1,0:T(8,128)(2,1)S(1)}, u32[]{:S(2)}, u32[]{:S(2)}) %collective-permute-start.13) | collective-permute-done | bytes 720928 | tf_op jit(solution)/shard_map/ppermute | solution.py:355
  71.6 8.0 %collective-permute-done.18.refs_4_ = bf16[256,2048]{1,0:T(8,128)(2,1)} collective-permute-done((bf16[256,2048]{1,0:T(8,128)(2,1)S(1)}, bf16[256,2048]{1,0:T(8,128)(2,1)}, u32[]{:S(2)}, u32[]{:S(2)}) %collective-permute-start.18) | collective-permute-done | bytes 1048608 | tf_op jit(solution)/shard_map/ppermute | solution.py:360
  82.1 4.5 %collective-permute-done.21.refs_13_ = bf16[128,2816]{1,0:T(8,128)(2,1)S(1)} collective-permute-done((bf16[128,2816]{1,0:T(8,128)(2,1)S(1)}, bf16[128,2816]{1,0:T(8,128)(2,1)S(1)}, u32[]{:S(2)}, u32[]{:S(2)}) %collective-permute-start.21) | collective-permute-done | bytes 720928 | tf_op jit(solution)/shard_map/ppermute | solution.py:355
  89.8 8.9 %collective-permute-done.22.refs_10_ = bf16[128,2816]{1,0:T(8,128)(2,1)} collective-permute-done((bf16[128,2816]{1,0:T(8,128)(2,1)S(1)}, bf16[128,2816]{1,0:T(8,128)(2,1)}, u32[]{:S(2)}, u32[]{:S(2)}) %collective-permute-start.22) | collective-permute-done | bytes 720928 | tf_op jit(solution)/shard_map/ppermute | solution.py:355
  105.1 17.7 %backward_product.3 = bf16[1024,2816]{1,0:T(8,128)(2,1)} custom-call(f32[52,16]{1,0:T(8,128)S(1)} %copy.14.refs_0_.refs_2_, bf16[1024,2048]{1,0:T(8,128)(2,1)S(1)} %arrange_rows.1.refs_1_, bf16[6656,2048]{1,0:T(8,128)(2,1)} %refs_2_.8), custom_call_target="tpu_custom_call" | custom-call | flops 738197504 | bytes 1343488 | tf_op jit(solution)/shard_map/backward_product/pallas_call | solution.py:172
  129.5 3.9 %collective-permute-done.16.refs_5_ = bf16[128,2816]{1,0:T(8,128)(2,1)S(1)} collective-permute-done((bf16[128,2816]{1,0:T(8,128)(2,1)}, bf16[128,2816]{1,0:T(8,128)(2,1)S(1)}, u32[]{:S(2)}, u32[]{:S(2)}) %collective-permute-start.16) | collective-permute-done | bytes 720928 | tf_op jit(solution)/shard_map/ppermute | solution.py:355
  135.4 17.8 %backward_product.4 = bf16[1024,2816]{1,0:T(8,128)(2,1)} custom-call(f32[52,16]{1,0:T(8,128)S(1)} %copy.14.refs_0_.refs_2_, bf16[1024,2048]{1,0:T(8,128)(2,1)S(1)} %arrange_rows.1.refs_1_, bf16[6656,2048]{1,0:T(8,128)(2,1)} %refs_2_.8), custom_call_target="tpu_custom_call" | custom-call | flops 738197504 | bytes 1343488 | tf_op jit(solution)/shard_map/backward_product/pallas_call | solution.py:172
  160.2 4.1 %collective-permute-done.23.refs_6_ = bf16[128,2816]{1,0:T(8,128)(2,1)S(1)} collective-permute-done((bf16[128,2816]{1,0:T(8,128)(2,1)S(1)}, bf16[128,2816]{1,0:T(8,128)(2,1)S(1)}, u32[]{:S(2)}, u32[]{:S(2)}) %collective-permute-start.23) | collective-permute-done | bytes 720928 | tf_op jit(solution)/shard_map/ppermute | solution.py:355
  165.3 25.5 %forward_product.2.refs_12_ = f32[1024,2048]{1,0:T(8,128)} custom-call(s32[1]{0:T(128)} %bitcast.refs_0_, s32[16]{0:T(128)S(1)} %dynamic-slice_bitcast_fusion.refs_1_, f32[52,16]{1,0:T(8,128)S(1)} %copy.14.refs_0_.refs_2_, bf16[128,1024]{1,0:T(8,128)(2,1)S(1)} %local_mix.3.refs_3_, bf16[128,1024]{1,0:T(8,128)(2,1)S(1)} %copy-done.12, ...), custom_call_target="tpu_custom_call" | custom-call | flops 1006632960 | bytes 2523136 | tf_op jit(solution)/shard_map/forward_product/pallas_call | solution.py:249
  199.1 3.4 %copy-done = f32[1024,2048]{1,0:T(8,128)S(1)} copy-done((f32[1024,2048]{1,0:T(8,128)S(1)}, f32[1024,2048]{1,0:T(8,128)}, u32[]{:S(2)}) %copy-start) | copy-done | bytes 8388632
  202.5 25.6 %forward_product.3 = (bf16[512,2048]{1,0:T(8,128)(2,1)}, bf16[512,2048]{1,0:T(8,128)(2,1)}) custom-call(s32[1]{0:T(128)} %bitcast.refs_0_, s32[16]{0:T(128)S(1)} %dynamic-slice_bitcast_fusion.refs_1_, f32[52,16]{1,0:T(8,128)S(1)} %copy.14.refs_0_.refs_2_, bf16[128,2816]{1,0:T(8,128)(2,1)S(1)} %local_mix.5.refs_3_, ...), custom_call_target="tpu_custom_call" | custom-call | flops 738197504 | bytes 2129920 | tf_op jit(solution)/shard_map/forward_product/pallas_call | solution.py:249
  236.7 8.2 %backward_product.5 = bf16[1024,1024]{1,0:T(8,128)(2,1)} custom-call(f32[52,16]{1,0:T(8,128)S(1)} %copy.14.refs_0_.refs_2_, bf16[1024,2048]{1,0:T(8,128)(2,1)S(1)} %arrange_rows.1.refs_1_, bf16[6656,2048]{1,0:T(8,128)(2,1)} %refs_2_.8), custom_call_target="tpu_custom_call" | custom-call | flops 268435456 | bytes 655360 | tf_op jit(solution)/shard_map/backward_product/pallas_call | solution.py:172
  244.9 5.8 %collective-permute-done.40 = bf16[128,2816]{1,0:T(8,128)(2,1)S(1)} collective-permute-done((bf16[128,2816]{1,0:T(8,128)(2,1)S(1)}, bf16[128,2816]{1,0:T(8,128)(2,1)S(1)}, u32[]{:S(2)}, u32[]{:S(2)}) %collective-permute-start.40) | collective-permute-done | bytes 720928 | tf_op jit(solution)/shard_map/ppermute | solution.py:355
  254.2 10.3 %collective-permute-done.48 = bf16[128,2816]{1,0:T(8,128)(2,1)S(1)} collective-permute-done((bf16[128,2816]{1,0:T(8,128)(2,1)S(1)}, bf16[128,2816]{1,0:T(8,128)(2,1)S(1)}, u32[]{:S(2)}, u32[]{:S(2)}) %collective-permute-start.48) | collective-permute-done | bytes 720928 | tf_op jit(solution)/shard_map/ppermute | solution.py:355
  273.5 18.0 %collective-permute-done.51 = bf16[128,1024]{1,0:T(8,128)(2,1)S(1)} collective-permute-done((bf16[128,1024]{1,0:T(8,128)(2,1)S(1)}, bf16[128,1024]{1,0:T(8,128)(2,1)S(1)}, u32[]{:S(2)}, u32[]{:S(2)}) %collective-permute-start.51) | collective-permute-done | bytes 262176 | tf_op jit(solution)/shard_map/ppermute | solution.py:355
  302.5 11.1 %collective-permute-done.54 = bf16[128,2816]{1,0:T(8,128)(2,1)S(1)} collective-permute-done((bf16[128,2816]{1,0:T(8,128)(2,1)S(1)}, bf16[128,2816]{1,0:T(8,128)(2,1)S(1)}, u32[]{:S(2)}, u32[]{:S(2)}) %collective-permute-start.54) | collective-permute-done | bytes 720928 | tf_op jit(solution)/shard_map/ppermute | solution.py:360
  (188 shorter events, 108.8 us)
Async XLA Ops:
  56.1 23.6 %collective-permute-start.18 = (bf16[256,2048]{1,0:T(8,128)(2,1)S(1)}, bf16[256,2048]{1,0:T(8,128)(2,1)}, u32[]{:S(2)}, u32[]{:S(2)}) collective-permute-start(bf16[256,2048]{1,0:T(8,128)(2,1)S(1)} %copy-done.4), channel_id=1, source_target_pairs={{0,2},{1,3},{2,0},{3,1},{4,6},{5,7},{6,4},{7,5},{8,10},{9,11},{10,... | collective-permute-start | bytes 3145736 | tf_op jit(solution)/shard_map/ppermute | solution.py:360
  71.5 31.0 %collective-permute-start.17 = (bf16[256,2048]{1,0:T(8,128)(2,1)S(1)}, bf16[256,2048]{1,0:T(8,128)(2,1)}, u32[]{:S(2)}, u32[]{:S(2)}) collective-permute-start(bf16[256,2048]{1,0:T(8,128)(2,1)S(1)} %copy-done.4), channel_id=1, source_target_pairs={{0,1},{1,0},{2,3},{3,2},{4,5},{5,4},{6,7},{7,6},{8,9},{9,8},{10,11... | collective-permute-start | bytes 3145736 | tf_op jit(solution)/shard_map/ppermute | solution.py:360
  79.6 23.3 %collective-permute-start.19 = (bf16[256,2048]{1,0:T(8,128)(2,1)}, bf16[256,2048]{1,0:T(8,128)(2,1)}, u32[]{:S(2)}, u32[]{:S(2)}) collective-permute-start(bf16[256,2048]{1,0:T(8,128)(2,1)} %collective-permute-done.18.refs_4_), channel_id=1, source_target_pairs={{0,1},{1,0},{2,3},{3,2},{4,5},{5,4},{6,7},{7,6},{8,9},{9,8},{10,11... | collective-permute-start | bytes 3145736 | tf_op jit(solution)/shard_map/ppermute | solution.py:360
  87.5 35.3 %collective-permute-start.24 = (bf16[128,2816]{1,0:T(8,128)(2,1)}, bf16[128,2816]{1,0:T(8,128)(2,1)}, u32[]{:S(2)}, u32[]{:S(2)}) collective-permute-start(bf16[128,2816]{1,0:T(8,128)(2,1)} %collective-permute-done.20.refs_17_), channel_id=1, source_target_pairs={{0,4},{8,0},{16,8},{24,16},{28,24},{20,28},{12,20},{4,12},{1,5},{9... | collective-permute-start | bytes 2162696 | tf_op jit(solution)/shard_map/ppermute | solution.py:355
  98.7 30.8 %collective-permute-start.25 = (bf16[128,2816]{1,0:T(8,128)(2,1)}, bf16[128,2816]{1,0:T(8,128)(2,1)S(1)}, u32[]{:S(2)}, u32[]{:S(2)}) collective-permute-start(bf16[128,2816]{1,0:T(8,128)(2,1)} %copy-done.7), channel_id=1, source_target_pairs={{0,8},{8,16},{16,24},{24,28},{28,20},{20,12},{12,4},{4,0},{1,9},{9... | collective-permute-start | bytes 2162696 | tf_op jit(solution)/shard_map/ppermute | solution.py:355
  100.9 28.6 %collective-permute-start.26 = (bf16[128,2816]{1,0:T(8,128)(2,1)}, bf16[128,2816]{1,0:T(8,128)(2,1)S(1)}, u32[]{:S(2)}, u32[]{:S(2)}) collective-permute-start(bf16[128,2816]{1,0:T(8,128)(2,1)} %collective-permute-done.22.refs_10_), channel_id=1, source_target_pairs={{0,4},{8,0},{16,8},{24,16},{28,24},{20,28},{12,20},{4,12},{1,5},{9... | collective-permute-start | bytes 2162696 | tf_op jit(solution)/shard_map/ppermute | solution.py:355
  102.5 30.9 %collective-permute-start.16 = (bf16[128,2816]{1,0:T(8,128)(2,1)}, bf16[128,2816]{1,0:T(8,128)(2,1)S(1)}, u32[]{:S(2)}, u32[]{:S(2)}) collective-permute-start(bf16[128,2816]{1,0:T(8,128)(2,1)} %collective-permute-done.15.refs_4_), channel_id=1, source_target_pairs={{0,8},{8,16},{16,24},{24,28},{28,20},{20,12},{12,4},{4,0},{1,9},{9... | collective-permute-start | bytes 2162696 | tf_op jit(solution)/shard_map/ppermute | solution.py:355
  122.8 36.9 %collective-permute-start.32 = (bf16[128,2816]{1,0:T(8,128)(2,1)}, bf16[128,2816]{1,0:T(8,128)(2,1)S(1)}, u32[]{:S(2)}, u32[]{:S(2)}) collective-permute-start(bf16[128,2816]{1,0:T(8,128)(2,1)} %collective-permute-done.24.refs_16_), channel_id=1, source_target_pairs={{0,4},{8,0},{16,8},{24,16},{28,24},{20,28},{12,20},{4,12},{1,5},{9... | collective-permute-start | bytes 2162696 | tf_op jit(solution)/shard_map/ppermute | solution.py:355
  126.0 30.7 %collective-permute-start.29 = (bf16[128,2816]{1,0:T(8,128)(2,1)S(1)}, bf16[128,2816]{1,0:T(8,128)(2,1)S(1)}, u32[]{:S(2)}, u32[]{:S(2)}) collective-permute-start(bf16[128,2816]{1,0:T(8,128)(2,1)S(1)} %get-tuple-element.72), channel_id=1, source_target_pairs={{0,8},{8,16},{16,24},{24,28},{28,20},{20,12},{12,4},{4,0},{1,9},{9... | collective-permute-start | bytes 2162696 | tf_op jit(solution)/shard_map/ppermute | solution.py:355
  133.4 30.9 %collective-permute-start.23 = (bf16[128,2816]{1,0:T(8,128)(2,1)S(1)}, bf16[128,2816]{1,0:T(8,128)(2,1)S(1)}, u32[]{:S(2)}, u32[]{:S(2)}) collective-permute-start(bf16[128,2816]{1,0:T(8,128)(2,1)S(1)} %collective-permute-done.16.refs_5_), channel_id=1, source_target_pairs={{0,8},{8,16},{16,24},{24,28},{28,20},{20,12},{12,4},{4,0},{1,9},{9... | collective-permute-start | bytes 2162696 | tf_op jit(solution)/shard_map/ppermute | solution.py:355
  134.3 30.0 %collective-permute-start.33 = (bf16[128,2816]{1,0:T(8,128)(2,1)S(1)}, bf16[128,2816]{1,0:T(8,128)(2,1)S(1)}, u32[]{:S(2)}, u32[]{:S(2)}) collective-permute-start(bf16[128,2816]{1,0:T(8,128)(2,1)S(1)} %collective-permute-done.26.refs_9_), channel_id=1, source_target_pairs={{0,4},{8,0},{16,8},{24,16},{28,24},{20,28},{12,20},{4,12},{1,5},{9... | collective-permute-start | bytes 2162696 | tf_op jit(solution)/shard_map/ppermute | solution.py:355
  153.3 41.0 %collective-permute-start.28 = (bf16[128,2816]{1,0:T(8,128)(2,1)S(1)}, bf16[128,2816]{1,0:T(8,128)(2,1)S(1)}, u32[]{:S(2)}, u32[]{:S(2)}) collective-permute-start(bf16[128,2816]{1,0:T(8,128)(2,1)S(1)} %get-tuple-element.71), channel_id=1, source_target_pairs={{0,4},{8,0},{16,8},{24,16},{28,24},{20,28},{12,20},{4,12},{1,5},{9... | collective-permute-start | bytes 2162696 | tf_op jit(solution)/shard_map/ppermute | solution.py:355
  156.7 34.2 %collective-permute-start.31 = (bf16[128,2816]{1,0:T(8,128)(2,1)S(1)}, bf16[128,2816]{1,0:T(8,128)(2,1)S(1)}, u32[]{:S(2)}, u32[]{:S(2)}) collective-permute-start(bf16[128,2816]{1,0:T(8,128)(2,1)S(1)} %get-tuple-element.74), channel_id=1, source_target_pairs={{0,4},{8,0},{16,8},{24,16},{28,24},{20,28},{12,20},{4,12},{1,5},{9... | collective-permute-start | bytes 2162696 | tf_op jit(solution)/shard_map/ppermute | solution.py:355
  159.7 34.6 %collective-permute-start.30 = (bf16[128,2816]{1,0:T(8,128)(2,1)S(1)}, bf16[128,2816]{1,0:T(8,128)(2,1)S(1)}, u32[]{:S(2)}, u32[]{:S(2)}) collective-permute-start(bf16[128,2816]{1,0:T(8,128)(2,1)S(1)} %add_convert_fusion.15), channel_id=1, source_target_pairs={{0,8},{8,16},{16,24},{24,28},{28,20},{20,12},{12,4},{4,0},{1,9},{9... | collective-permute-start | bytes 2162696 | tf_op jit(solution)/shard_map/ppermute | solution.py:355
  164.3 34.8 %collective-permute-start.27 = (bf16[128,2816]{1,0:T(8,128)(2,1)S(1)}, bf16[128,2816]{1,0:T(8,128)(2,1)S(1)}, u32[]{:S(2)}, u32[]{:S(2)}) collective-permute-start(bf16[128,2816]{1,0:T(8,128)(2,1)S(1)} %collective-permute-done.23.refs_6_), channel_id=1, source_target_pairs={{0,8},{8,16},{16,24},{24,28},{28,20},{20,12},{12,4},{4,0},{1,9},{9... | collective-permute-start | bytes 2162696 | tf_op jit(solution)/shard_map/ppermute | solution.py:355
  192.2 35.9 %collective-permute-start.37 = (bf16[128,2816]{1,0:T(8,128)(2,1)S(1)}, bf16[128,2816]{1,0:T(8,128)(2,1)S(1)}, u32[]{:S(2)}, u32[]{:S(2)}) collective-permute-start(bf16[128,2816]{1,0:T(8,128)(2,1)S(1)} %add_convert_fusion.12), channel_id=1, source_target_pairs={{0,4},{8,0},{16,8},{24,16},{28,24},{20,28},{12,20},{4,12},{1,5},{9... | collective-permute-start | bytes 2162696 | tf_op jit(solution)/shard_map/ppermute | solution.py:355
  193.9 34.3 %collective-permute-start.36 = (bf16[128,2816]{1,0:T(8,128)(2,1)S(1)}, bf16[128,2816]{1,0:T(8,128)(2,1)S(1)}, u32[]{:S(2)}, u32[]{:S(2)}) collective-permute-start(bf16[128,2816]{1,0:T(8,128)(2,1)S(1)} %get-tuple-element.83), channel_id=1, source_target_pairs={{0,8},{8,16},{16,24},{24,28},{28,20},{20,12},{12,4},{4,0},{1,9},{9... | collective-permute-start | bytes 2162696 | tf_op jit(solution)/shard_map/ppermute | solution.py:355
  197.1 31.1 %collective-permute-start.34 = (bf16[128,2816]{1,0:T(8,128)(2,1)}, bf16[128,2816]{1,0:T(8,128)(2,1)S(1)}, u32[]{:S(2)}, u32[]{:S(2)}) collective-permute-start(bf16[128,2816]{1,0:T(8,128)(2,1)} %get-tuple-element.81), channel_id=1, source_target_pairs={{0,8},{8,16},{16,24},{24,28},{28,20},{20,12},{12,4},{4,0},{1,9},{9... | collective-permute-start | bytes 2162696 | tf_op jit(solution)/shard_map/ppermute | solution.py:355
  198.7 29.5 %collective-permute-start.35 = (bf16[128,2816]{1,0:T(8,128)(2,1)}, bf16[128,2816]{1,0:T(8,128)(2,1)S(1)}, u32[]{:S(2)}, u32[]{:S(2)}) collective-permute-start(bf16[128,2816]{1,0:T(8,128)(2,1)} %get-tuple-element.82), channel_id=1, source_target_pairs={{0,4},{8,0},{16,8},{24,16},{28,24},{20,28},{12,20},{4,12},{1,5},{9... | collective-permute-start | bytes 2162696 | tf_op jit(solution)/shard_map/ppermute | solution.py:355
  233.8 30.6 %collective-permute-start.48 = (bf16[128,2816]{1,0:T(8,128)(2,1)S(1)}, bf16[128,2816]{1,0:T(8,128)(2,1)S(1)}, u32[]{:S(2)}, u32[]{:S(2)}) collective-permute-start(bf16[128,2816]{1,0:T(8,128)(2,1)S(1)} %get-tuple-element.96), channel_id=1, source_target_pairs={{0,8},{8,16},{16,24},{24,28},{28,20},{20,12},{12,4},{4,0},{1,9},{9... | collective-permute-start | bytes 2162696 | tf_op jit(solution)/shard_map/ppermute | solution.py:355
  235.5 29.9 %collective-permute-start.46 = (bf16[128,2816]{1,0:T(8,128)(2,1)S(1)}, bf16[128,2816]{1,0:T(8,128)(2,1)S(1)}, u32[]{:S(2)}, u32[]{:S(2)}) collective-permute-start(bf16[128,2816]{1,0:T(8,128)(2,1)S(1)} %get-tuple-element.94), channel_id=1, source_target_pairs={{0,4},{8,0},{16,8},{24,16},{28,24},{20,28},{12,20},{4,12},{1,5},{9... | collective-permute-start | bytes 2162696 | tf_op jit(solution)/shard_map/ppermute | solution.py:355
  267.1 26.7 %collective-permute-start.49 = (bf16[128,2816]{1,0:T(8,128)(2,1)S(1)}, bf16[128,2816]{1,0:T(8,128)(2,1)S(1)}, u32[]{:S(2)}, u32[]{:S(2)}) collective-permute-start(bf16[128,2816]{1,0:T(8,128)(2,1)S(1)} %get-tuple-element.97), channel_id=1, source_target_pairs={{0,8},{8,16},{16,24},{24,28},{28,20},{20,12},{12,4},{4,0},{1,9},{9... | collective-permute-start | bytes 2162696 | tf_op jit(solution)/shard_map/ppermute | solution.py:355
  268.7 25.1 %collective-permute-start.47 = (bf16[128,2816]{1,0:T(8,128)(2,1)S(1)}, bf16[128,2816]{1,0:T(8,128)(2,1)S(1)}, u32[]{:S(2)}, u32[]{:S(2)}) collective-permute-start(bf16[128,2816]{1,0:T(8,128)(2,1)S(1)} %get-tuple-element.95), channel_id=1, source_target_pairs={{0,4},{8,0},{16,8},{24,16},{28,24},{20,28},{12,20},{4,12},{1,5},{9... | collective-permute-start | bytes 2162696 | tf_op jit(solution)/shard_map/ppermute | solution.py:355
  271.9 24.2 %collective-permute-start.42 = (bf16[256,2048]{1,0:T(8,128)(2,1)S(1)}, bf16[256,2048]{1,0:T(8,128)(2,1)S(1)}, u32[]{:S(2)}, u32[]{:S(2)}) collective-permute-start(bf16[256,2048]{1,0:T(8,128)(2,1)S(1)} %slice.137), channel_id=1, source_target_pairs={{0,2},{1,3},{2,0},{3,1},{4,6},{5,7},{6,4},{7,5},{8,10},{9,11},{10,... | collective-permute-start | bytes 3145736 | tf_op jit(solution)/shard_map/ppermute | solution.py:360
  (62 other events, 795.1 us)

commit v6 on v4

--- a/solution.py
+++ b/solution.py
@@ -9,7 +9,7 @@
 from jax.sharding import PartitionSpec as P
 
 BLOCK = 128
-AHEAD = (4, 11, 11)
+AHEAD = (5, 10, 11)
 BACK = (11, 11, 4)
 VMEM_LIMIT = 40 * 1024 * 1024
 F32, BF16 = jnp.float32, jnp.bfloat16
@@ -197,7 +197,7 @@
     per = max(1, counts[0] >> bits)
     step = pl.program_id(0)
 
-    def copies():
+    def places():
         column = 0
         for part, count in enumerate(counts):
             for r in range(count):
@@ -206,21 +206,29 @@
                 offset = order_ref[r] // per ^ group_ref[0]
                 turned = sum((offset >> k & 1) << bits - 1 - k for k in range(bits))
                 start = pl.multiple_of((turned * per + order_ref[r] % per) * size, size)
-                place = rows_ref.at[pl.ds(start, size), pl.ds(column, width)]
-                yield pltpu.make_async_copy(blocks[i], place, sems.at[i])
+                yield i, rows_ref.at[pl.ds(start, size), pl.ds(column, width)]
             column += blocks[part * count].shape[1]
+
+    def copies():
+        return [pltpu.make_async_copy(blocks[i], place, sems.at[i]) for i, place in places()]
 
     @pl.when(step == 0)
     def _():
-        for copy in copies():
-            copy.start()
+        if len(counts) == 1:
+            for i, place in places():
+                place[...] = blocks[i][...]
+        else:
+            for copy in copies():
+                copy.start()
 
     dequantize_into(weight_ref, codes_ref, scales_ref, row_block, step * (tile // BLOCK))
 
-    @pl.when(step == 0)
-    def _():
-        for copy in copies():
-            copy.wait()
+    if len(counts) > 1:
+
+        @pl.when(step == 0)
+        def _():
+            for copy in copies():
+                copy.wait()
 
     total = jnp.dot(rows_ref[...], weight_ref[...], preferred_element_type=F32)
     if has_sum:
@@ -232,7 +240,11 @@
     size, count = parts[0][0].shape[0], len(parts[0])
     depth = sum(blocks[0].shape[1] for blocks in parts)
     tokens, width = size * count, codes.shape[1]
-    tile = min(512, width)
+    tile = min(512 if len(parts) > 1 else 256, width)
+    if len(parts) > 1:
+        block = pl.BlockSpec(memory_space=pltpu.HBM)
+    else:
+        block = pl.BlockSpec((size, depth), lambda i: (0, 0), pipeline_mode=pl.Buffered(1))
     sums = [] if running is None else [running]
     sliced = pl.BlockSpec((tokens, tile), lambda i: (0, i))
     return pl.pallas_call(
@@ -245,7 +257,7 @@
             spec_smem(),
             spec_smem(),
             spec_smem(),
-            *[pl.BlockSpec(memory_space=pltpu.HBM)] * (count * len(parts)),
+            *[block] * (count * len(parts)),
             pl.BlockSpec((pl.Element(depth), pl.Element(tile)), lambda i: (start, i * tile)),
             *[sliced] * len(sums),
         ],

time: 328 us -> 325 us (level)
  starting transfers between devices: 59.9 us -> 51.5 us
  other arithmetic: 19.9 us -> 25 us
  local copies, waits for them, and re-layouts: 12.3 us -> 16.7 us
  waiting for transfers between devices: 133 us -> 129 us
    ppermute x17, starting transfers between devices: 14.6 us -> 8.43 us  [partner(): lax.ppermute(value, 'tensor', [(i, i ^ 1 << bit) for i in range(groups)])]
    convert_element_type x9, other arithmetic: 9.85 us -> 14.1 us  [outgoing(): return (self.sums[step].astype(F32) + term.astype(F32)).astype(BF16)]
    unnamed x63 -> x73, local copies, waits for them, and re-layouts: 6.04 us -> 9.29 us
  transfers between devices with their start and end apart: 59 -> 59, of which waited for: 31 -> 29; matrix products, arithmetic and copies ran while one was open for 8% -> 10% of each run, Pallas kernels for 30% -> 30%
where the time goes in v6:
time: 325 us; the launch traced here: 323 us
  waiting for transfers between devices  129 us (40%)
  Pallas kernels  99.6 us (31%)
  starting transfers between devices  51.5 us (16%)
  other arithmetic  25 us (8%)
  local copies, waits for them, and re-layouts  16.7 us (5%)
    ppermute x42, waiting for transfers between devices, send(): lax.ppermute(value, 'dp', [(cycle[i], cycle[(i + step) % ring]) for i in...  93.9 us
    pallas_call x2, Pallas kernels, forward_product(): pl.pallas_call(lambda *refs: forward_kernel([count] * len(parts), bits, s...  44.2 us
    pallas_call x3, Pallas kernels, backward_product(): pl.pallas_call(lambda *refs: backward_kernel(start // BLOCK, *refs), grid...  43.6 us
    ppermute x42, starting transfers between devices, send(): lax.ppermute(value, 'dp', [(cycle[i], cycle[(i + step) % ring]) for i in...  43 us
    ppermute x17, waiting for transfers between devices, partner(): lax.ppermute(value, 'tensor', [(i, i ^ 1 << bit) for i in range(groups)])  35.6 us
    convert_element_type x9, other arithmetic, outgoing(): return (self.sums[step].astype(F32) + term.astype(F32)).astype(BF16)  14.1 us
    unnamed x73, local copies, waits for them, and re-layouts  9.29 us
    ppermute x17, starting transfers between devices, partner(): lax.ppermute(value, 'tensor', [(i, i ^ 1 << bit) for i in range(groups)])  8.43 us
  transfers between devices with their start and end apart: 59, of which 29 were waited for; matrix products, arithmetic and copies ran while one was open for 10% of the time, Pallas kernels for 30%

profile of v6, /device:TPU:0, one launch (start us, length us, event | category | flops | bytes accessed | tf_op | source)
XLA Modules:
  0.0 323.5 jit_solution(16299071520189522557)
XLA Ops:
  2.0 3.0 collective-permute-start
  5.1 7.7 %collective-permute-done = bf16[128,1280]{1,0:T(8,128)(2,1)S(1)} collective-permute-done((bf16[128,1280]{1,0:T(8,128)(2,1)S(1)}, bf16[128,1280]{1,0:T(8,128)(2,1)S(1)}, u32[]{:S(2)}, u32[]{:S(2)}) %collective-permute-start) | collective-permute-done | bytes 327712 | tf_op jit(solution)/shard_map/ppermute | solution.py:359
  22.2 7.8 %collective-permute-done.5.refs_10_ = bf16[128,1280]{1,0:T(8,128)(2,1)S(1)} collective-permute-done((bf16[128,1280]{1,0:T(8,128)(2,1)S(1)}, bf16[128,1280]{1,0:T(8,128)(2,1)S(1)}, u32[]{:S(2)}, u32[]{:S(2)}) %collective-permute-start.5) | collective-permute-done | bytes 327712 | tf_op jit(solution)/shard_map/ppermute | solution.py:354
  34.8 4.3 %collective-permute-done.6.refs_9_ = bf16[128,1280]{1,0:T(8,128)(2,1)S(1)} collective-permute-done((bf16[128,1280]{1,0:T(8,128)(2,1)S(1)}, bf16[128,1280]{1,0:T(8,128)(2,1)S(1)}, u32[]{:S(2)}, u32[]{:S(2)}) %collective-permute-start.6) | collective-permute-done | bytes 327712 | tf_op jit(solution)/shard_map/ppermute | solution.py:354
  43.4 5.9 %collective-permute-done.9.refs_6_ = bf16[128,1280]{1,0:T(8,128)(2,1)S(1)} collective-permute-done((bf16[128,1280]{1,0:T(8,128)(2,1)S(1)}, bf16[128,1280]{1,0:T(8,128)(2,1)S(1)}, u32[]{:S(2)}, u32[]{:S(2)}) %collective-permute-start.9) | collective-permute-done | bytes 327712 | tf_op jit(solution)/shard_map/ppermute | solution.py:354
  52.5 4.1 %collective-permute-done.7 = bf16[128,2816]{1,0:T(8,128)(2,1)S(1)} collective-permute-done((bf16[128,2816]{1,0:T(8,128)(2,1)S(1)}, bf16[128,2816]{1,0:T(8,128)(2,1)S(1)}, u32[]{:S(2)}, u32[]{:S(2)}) %collective-permute-start.7) | collective-permute-done | bytes 720928 | tf_op jit(solution)/shard_map/ppermute | solution.py:359
  60.9 3.3 %collective-permute-done.14.refs_18_ = bf16[128,2560]{1,0:T(8,128)(2,1)S(1)} collective-permute-done((bf16[128,2560]{1,0:T(8,128)(2,1)S(1)}, bf16[128,2560]{1,0:T(8,128)(2,1)S(1)}, u32[]{:S(2)}, u32[]{:S(2)}) %collective-permute-start.14) | collective-permute-done | bytes 655392 | tf_op jit(solution)/shard_map/ppermute | solution.py:354
  65.1 5.9 %collective-permute-done.13.refs_12_ = bf16[128,2560]{1,0:T(8,128)(2,1)S(1)} collective-permute-done((bf16[128,2560]{1,0:T(8,128)(2,1)S(1)}, bf16[128,2560]{1,0:T(8,128)(2,1)S(1)}, u32[]{:S(2)}, u32[]{:S(2)}) %collective-permute-start.13) | collective-permute-done | bytes 655392 | tf_op jit(solution)/shard_map/ppermute | solution.py:354
  72.9 6.3 %collective-permute-done.18.refs_4_ = bf16[256,2048]{1,0:T(8,128)(2,1)} collective-permute-done((bf16[256,2048]{1,0:T(8,128)(2,1)}, bf16[256,2048]{1,0:T(8,128)(2,1)}, u32[]{:S(2)}, u32[]{:S(2)}) %collective-permute-start.18) | collective-permute-done | bytes 1048608 | tf_op jit(solution)/shard_map/ppermute | solution.py:359
  87.4 11.1 %collective-permute-done.22.refs_10_ = bf16[128,2816]{1,0:T(8,128)(2,1)} collective-permute-done((bf16[128,2816]{1,0:T(8,128)(2,1)}, bf16[128,2816]{1,0:T(8,128)(2,1)}, u32[]{:S(2)}, u32[]{:S(2)}) %collective-permute-start.22) | collective-permute-done | bytes 720928 | tf_op jit(solution)/shard_map/ppermute | solution.py:354
  104.1 17.6 %backward_product.3 = bf16[1024,2816]{1,0:T(8,128)(2,1)} custom-call(f32[52,16]{1,0:T(8,128)S(1)} %copy.14.refs_0_.refs_2_, bf16[1024,2048]{1,0:T(8,128)(2,1)S(1)} %arrange_rows.1.refs_1_, bf16[6656,2048]{1,0:T(8,128)(2,1)} %refs_2_.8), custom_call_target="tpu_custom_call" | custom-call | flops 738197504 | bytes 1343488 | tf_op jit(solution)/shard_map/backward_product/pallas_call | solution.py:172
  127.9 3.9 %collective-permute-done.16.refs_5_ = bf16[128,2816]{1,0:T(8,128)(2,1)S(1)} collective-permute-done((bf16[128,2816]{1,0:T(8,128)(2,1)}, bf16[128,2816]{1,0:T(8,128)(2,1)S(1)}, u32[]{:S(2)}, u32[]{:S(2)}) %collective-permute-start.16) | collective-permute-done | bytes 720928 | tf_op jit(solution)/shard_map/ppermute | solution.py:354
  133.9 17.8 %backward_product.4 = bf16[1024,2816]{1,0:T(8,128)(2,1)} custom-call(f32[52,16]{1,0:T(8,128)S(1)} %copy.14.refs_0_.refs_2_, bf16[1024,2048]{1,0:T(8,128)(2,1)S(1)} %arrange_rows.1.refs_1_, bf16[6656,2048]{1,0:T(8,128)(2,1)} %refs_2_.8), custom_call_target="tpu_custom_call" | custom-call | flops 738197504 | bytes 1343488 | tf_op jit(solution)/shard_map/backward_product/pallas_call | solution.py:172
  159.7 3.0 collective-permute-done.23.refs_6_
  163.7 25.0 %forward_product.2.refs_12_ = f32[1024,2048]{1,0:T(8,128)} custom-call(s32[1]{0:T(128)} %bitcast.refs_0_, s32[16]{0:T(128)S(1)} %dynamic-slice_bitcast_fusion.refs_1_, f32[52,16]{1,0:T(8,128)S(1)} %copy.14.refs_0_.refs_2_, bf16[128,1280]{1,0:T(8,128)(2,1)S(1)} %copy-done.6, bf16[128,1280]{1,0:T(8,128)(2,1)S(1)} %copy-done.19, ...), custom_call_target="tpu_custom_call" | custom-call | flops 1006632960 | bytes 2523136 | tf_op jit(solution)/shard_map/forward_product/pallas_call | solution.py:250
  197.7 3.4 %copy-done = f32[1024,2048]{1,0:T(8,128)S(1)} copy-done((f32[1024,2048]{1,0:T(8,128)S(1)}, f32[1024,2048]{1,0:T(8,128)}, u32[]{:S(2)}) %copy-start) | copy-done | bytes 8388632
  201.1 19.2 %forward_product.3 = bf16[1024,2048]{1,0:T(8,128)(2,1)} custom-call(s32[1]{0:T(128)} %bitcast.refs_0_, s32[16]{0:T(128)S(1)} %dynamic-slice_bitcast_fusion.refs_1_, f32[52,16]{1,0:T(8,128)S(1)} %copy.14.refs_0_.refs_2_, bf16[128,2816]{1,0:T(8,128)(2,1)} %local_mix.5.refs_3_, bf16[128,2816]{1,0:T(8,128)(2,1)} %collective-permute-done.15.refs_4_, ...), custom_call_target="tpu_custom_call" | custom-call | flops 738197504 | bytes 2129920 | tf_op jit(solution)/shard_map/forward_product/pallas_call | solution.py:250
  224.9 2.9 add_convert_fusion.11
  235.5 8.2 %backward_product.5 = bf16[1024,1024]{1,0:T(8,128)(2,1)} custom-call(f32[52,16]{1,0:T(8,128)S(1)} %copy.14.refs_0_.refs_2_, bf16[1024,2048]{1,0:T(8,128)(2,1)S(1)} %arrange_rows.1.refs_1_, bf16[6656,2048]{1,0:T(8,128)(2,1)} %refs_2_.8), custom_call_target="tpu_custom_call" | custom-call | flops 268435456 | bytes 655360 | tf_op jit(solution)/shard_map/backward_product/pallas_call | solution.py:172
  243.7 3.9 %collective-permute-done.40 = bf16[128,2816]{1,0:T(8,128)(2,1)} collective-permute-done((bf16[128,2816]{1,0:T(8,128)(2,1)}, bf16[128,2816]{1,0:T(8,128)(2,1)}, u32[]{:S(2)}, u32[]{:S(2)}) %collective-permute-start.40) | collective-permute-done | bytes 720928 | tf_op jit(solution)/shard_map/ppermute | solution.py:354
  251.1 11.2 %collective-permute-done.48 = bf16[128,2816]{1,0:T(8,128)(2,1)} collective-permute-done((bf16[128,2816]{1,0:T(8,128)(2,1)}, bf16[128,2816]{1,0:T(8,128)(2,1)}, u32[]{:S(2)}, u32[]{:S(2)}) %collective-permute-start.48) | collective-permute-done | bytes 720928 | tf_op jit(solution)/shard_map/ppermute | solution.py:354
  269.3 18.4 %collective-permute-done.51 = bf16[128,1024]{1,0:T(8,128)(2,1)S(1)} collective-permute-done((bf16[128,1024]{1,0:T(8,128)(2,1)S(1)}, bf16[128,1024]{1,0:T(8,128)(2,1)S(1)}, u32[]{:S(2)}, u32[]{:S(2)}) %collective-permute-start.51) | collective-permute-done | bytes 262176 | tf_op jit(solution)/shard_map/ppermute | solution.py:354
  300.3 10.2 %collective-permute-done.54 = bf16[128,2816]{1,0:T(8,128)(2,1)S(1)} collective-permute-done((bf16[128,2816]{1,0:T(8,128)(2,1)S(1)}, bf16[128,2816]{1,0:T(8,128)(2,1)S(1)}, u32[]{:S(2)}, u32[]{:S(2)}) %collective-permute-start.54) | collective-permute-done | bytes 720928 | tf_op jit(solution)/shard_map/ppermute | solution.py:359
  316.5 3.2 collective-permute-done.55
  (208 shorter events, 115.1 us)
Async XLA Ops:
  56.6 22.7 %collective-permute-start.18 = (bf16[256,2048]{1,0:T(8,128)(2,1)}, bf16[256,2048]{1,0:T(8,128)(2,1)}, u32[]{:S(2)}, u32[]{:S(2)}) collective-permute-start(bf16[256,2048]{1,0:T(8,128)(2,1)} %refs_2_.5), channel_id=1, source_target_pairs={{0,2},{1,3},{2,0},{3,1},{4,6},{5,7},{6,4},{7,5},{8,10},{9,11},{10,... | collective-permute-start | bytes 3145736 | tf_op jit(solution)/shard_map/ppermute | solution.py:359
  72.9 28.3 %collective-permute-start.17 = (bf16[256,2048]{1,0:T(8,128)(2,1)}, bf16[256,2048]{1,0:T(8,128)(2,1)}, u32[]{:S(2)}, u32[]{:S(2)}) collective-permute-start(bf16[256,2048]{1,0:T(8,128)(2,1)} %refs_2_.5), channel_id=1, source_target_pairs={{0,1},{1,0},{2,3},{3,2},{4,5},{5,4},{6,7},{7,6},{8,9},{9,8},{10,11... | collective-permute-start | bytes 3145736 | tf_op jit(solution)/shard_map/ppermute | solution.py:359
  79.3 22.4 %collective-permute-start.19 = (bf16[256,2048]{1,0:T(8,128)(2,1)}, bf16[256,2048]{1,0:T(8,128)(2,1)}, u32[]{:S(2)}, u32[]{:S(2)}) collective-permute-start(bf16[256,2048]{1,0:T(8,128)(2,1)} %collective-permute-done.18.refs_4_), channel_id=1, source_target_pairs={{0,1},{1,0},{2,3},{3,2},{4,5},{5,4},{6,7},{7,6},{8,9},{9,8},{10,11... | collective-permute-start | bytes 3145736 | tf_op jit(solution)/shard_map/ppermute | solution.py:359
  85.0 36.7 %collective-permute-start.24 = (bf16[128,2560]{1,0:T(8,128)(2,1)}, bf16[128,2560]{1,0:T(8,128)(2,1)}, u32[]{:S(2)}, u32[]{:S(2)}) collective-permute-start(bf16[128,2560]{1,0:T(8,128)(2,1)} %collective-permute-done.20.refs_17_), channel_id=1, source_target_pairs={{0,4},{8,0},{16,8},{24,16},{28,24},{20,28},{12,20},{4,12},{1,5},{9... | collective-permute-start | bytes 1966088 | tf_op jit(solution)/shard_map/ppermute | solution.py:354
  98.5 29.4 %collective-permute-start.25 = (bf16[128,2560]{1,0:T(8,128)(2,1)}, bf16[128,2560]{1,0:T(8,128)(2,1)S(1)}, u32[]{:S(2)}, u32[]{:S(2)}) collective-permute-start(bf16[128,2560]{1,0:T(8,128)(2,1)} %copy-done.14), channel_id=1, source_target_pairs={{0,8},{8,16},{16,24},{24,28},{28,20},{20,12},{12,4},{4,0},{1,9},{9... | collective-permute-start | bytes 1966088 | tf_op jit(solution)/shard_map/ppermute | solution.py:354
  99.6 28.3 %collective-permute-start.26 = (bf16[128,2816]{1,0:T(8,128)(2,1)}, bf16[128,2816]{1,0:T(8,128)(2,1)S(1)}, u32[]{:S(2)}, u32[]{:S(2)}) collective-permute-start(bf16[128,2816]{1,0:T(8,128)(2,1)} %collective-permute-done.22.refs_10_), channel_id=1, source_target_pairs={{0,4},{8,0},{16,8},{24,16},{28,24},{20,28},{12,20},{4,12},{1,5},{9... | collective-permute-start | bytes 2162696 | tf_op jit(solution)/shard_map/ppermute | solution.py:354
  101.2 30.6 %collective-permute-start.16 = (bf16[128,2816]{1,0:T(8,128)(2,1)}, bf16[128,2816]{1,0:T(8,128)(2,1)S(1)}, u32[]{:S(2)}, u32[]{:S(2)}) collective-permute-start(bf16[128,2816]{1,0:T(8,128)(2,1)} %collective-permute-done.15.refs_4_), channel_id=1, source_target_pairs={{0,8},{8,16},{16,24},{24,28},{28,20},{20,12},{12,4},{4,0},{1,9},{9... | collective-permute-start | bytes 2162696 | tf_op jit(solution)/shard_map/ppermute | solution.py:354
  121.7 37.5 %collective-permute-start.32 = (bf16[128,2560]{1,0:T(8,128)(2,1)}, bf16[128,2560]{1,0:T(8,128)(2,1)S(1)}, u32[]{:S(2)}, u32[]{:S(2)}) collective-permute-start(bf16[128,2560]{1,0:T(8,128)(2,1)} %collective-permute-done.24.refs_16_), channel_id=1, source_target_pairs={{0,4},{8,0},{16,8},{24,16},{28,24},{20,28},{12,20},{4,12},{1,5},{9... | collective-permute-start | bytes 1966088 | tf_op jit(solution)/shard_map/ppermute | solution.py:354
  125.0 31.2 %collective-permute-start.29 = (bf16[128,2816]{1,0:T(8,128)(2,1)S(1)}, bf16[128,2816]{1,0:T(8,128)(2,1)S(1)}, u32[]{:S(2)}, u32[]{:S(2)}) collective-permute-start(bf16[128,2816]{1,0:T(8,128)(2,1)S(1)} %get-tuple-element.70), channel_id=1, source_target_pairs={{0,8},{8,16},{16,24},{24,28},{28,20},{20,12},{12,4},{4,0},{1,9},{9... | collective-permute-start | bytes 2162696 | tf_op jit(solution)/shard_map/ppermute | solution.py:354
  131.8 30.9 %collective-permute-start.23 = (bf16[128,2816]{1,0:T(8,128)(2,1)S(1)}, bf16[128,2816]{1,0:T(8,128)(2,1)S(1)}, u32[]{:S(2)}, u32[]{:S(2)}) collective-permute-start(bf16[128,2816]{1,0:T(8,128)(2,1)S(1)} %collective-permute-done.16.refs_5_), channel_id=1, source_target_pairs={{0,8},{8,16},{16,24},{24,28},{28,20},{20,12},{12,4},{4,0},{1,9},{9... | collective-permute-start | bytes 2162696 | tf_op jit(solution)/shard_map/ppermute | solution.py:354
  132.7 30.0 %collective-permute-start.33 = (bf16[128,2816]{1,0:T(8,128)(2,1)S(1)}, bf16[128,2816]{1,0:T(8,128)(2,1)S(1)}, u32[]{:S(2)}, u32[]{:S(2)}) collective-permute-start(bf16[128,2816]{1,0:T(8,128)(2,1)S(1)} %collective-permute-done.26.refs_9_), channel_id=1, source_target_pairs={{0,4},{8,0},{16,8},{24,16},{28,24},{20,28},{12,20},{4,12},{1,5},{9... | collective-permute-start | bytes 2162696 | tf_op jit(solution)/shard_map/ppermute | solution.py:354
  151.7 41.3 %collective-permute-start.28 = (bf16[128,2816]{1,0:T(8,128)(2,1)S(1)}, bf16[128,2816]{1,0:T(8,128)(2,1)S(1)}, u32[]{:S(2)}, u32[]{:S(2)}) collective-permute-start(bf16[128,2816]{1,0:T(8,128)(2,1)S(1)} %get-tuple-element.69), channel_id=1, source_target_pairs={{0,4},{8,0},{16,8},{24,16},{28,24},{20,28},{12,20},{4,12},{1,5},{9... | collective-permute-start | bytes 2162696 | tf_op jit(solution)/shard_map/ppermute | solution.py:354
  156.3 32.5 %collective-permute-start.31 = (bf16[128,2816]{1,0:T(8,128)(2,1)}, bf16[128,2816]{1,0:T(8,128)(2,1)S(1)}, u32[]{:S(2)}, u32[]{:S(2)}) collective-permute-start(bf16[128,2816]{1,0:T(8,128)(2,1)} %get-tuple-element.72), channel_id=1, source_target_pairs={{0,4},{8,0},{16,8},{24,16},{28,24},{20,28},{12,20},{4,12},{1,5},{9... | collective-permute-start | bytes 2162696 | tf_op jit(solution)/shard_map/ppermute | solution.py:354
  159.3 33.7 %collective-permute-start.30 = (bf16[128,2816]{1,0:T(8,128)(2,1)S(1)}, bf16[128,2816]{1,0:T(8,128)(2,1)S(1)}, u32[]{:S(2)}, u32[]{:S(2)}) collective-permute-start(bf16[128,2816]{1,0:T(8,128)(2,1)S(1)} %add_convert_fusion.15), channel_id=1, source_target_pairs={{0,8},{8,16},{16,24},{24,28},{28,20},{20,12},{12,4},{4,0},{1,9},{9... | collective-permute-start | bytes 2162696 | tf_op jit(solution)/shard_map/ppermute | solution.py:354
  162.7 35.0 %collective-permute-start.27 = (bf16[128,2816]{1,0:T(8,128)(2,1)S(1)}, bf16[128,2816]{1,0:T(8,128)(2,1)S(1)}, u32[]{:S(2)}, u32[]{:S(2)}) collective-permute-start(bf16[128,2816]{1,0:T(8,128)(2,1)S(1)} %collective-permute-done.23.refs_6_), channel_id=1, source_target_pairs={{0,8},{8,16},{16,24},{24,28},{28,20},{20,12},{12,4},{4,0},{1,9},{9... | collective-permute-start | bytes 2162696 | tf_op jit(solution)/shard_map/ppermute | solution.py:354
  190.9 31.5 %collective-permute-start.37 = (bf16[128,2816]{1,0:T(8,128)(2,1)}, bf16[128,2816]{1,0:T(8,128)(2,1)}, u32[]{:S(2)}, u32[]{:S(2)}) collective-permute-start(bf16[128,2816]{1,0:T(8,128)(2,1)} %add_convert_fusion.12), channel_id=1, source_target_pairs={{0,4},{8,0},{16,8},{24,16},{28,24},{20,28},{12,20},{4,12},{1,5},{9... | collective-permute-start | bytes 2162696 | tf_op jit(solution)/shard_map/ppermute | solution.py:354
  192.0 30.3 %collective-permute-start.36 = (bf16[128,2816]{1,0:T(8,128)(2,1)}, bf16[128,2816]{1,0:T(8,128)(2,1)}, u32[]{:S(2)}, u32[]{:S(2)}) collective-permute-start(bf16[128,2816]{1,0:T(8,128)(2,1)} %get-tuple-element.79), channel_id=1, source_target_pairs={{0,8},{8,16},{16,24},{24,28},{28,20},{20,12},{12,4},{4,0},{1,9},{9... | collective-permute-start | bytes 2162696 | tf_op jit(solution)/shard_map/ppermute | solution.py:354
  195.7 29.2 %collective-permute-start.34 = (bf16[128,2816]{1,0:T(8,128)(2,1)}, bf16[128,2816]{1,0:T(8,128)(2,1)}, u32[]{:S(2)}, u32[]{:S(2)}) collective-permute-start(bf16[128,2816]{1,0:T(8,128)(2,1)} %get-tuple-element.77), channel_id=1, source_target_pairs={{0,8},{8,16},{16,24},{24,28},{28,20},{20,12},{12,4},{4,0},{1,9},{9... | collective-permute-start | bytes 2162696 | tf_op jit(solution)/shard_map/ppermute | solution.py:354
  197.3 27.6 %collective-permute-start.35 = (bf16[128,2816]{1,0:T(8,128)(2,1)}, bf16[128,2816]{1,0:T(8,128)(2,1)}, u32[]{:S(2)}, u32[]{:S(2)}) collective-permute-start(bf16[128,2816]{1,0:T(8,128)(2,1)} %get-tuple-element.78), channel_id=1, source_target_pairs={{0,4},{8,0},{16,8},{24,16},{28,24},{20,28},{12,20},{4,12},{1,5},{9... | collective-permute-start | bytes 2162696 | tf_op jit(solution)/shard_map/ppermute | solution.py:354
  232.6 29.7 %collective-permute-start.48 = (bf16[128,2816]{1,0:T(8,128)(2,1)}, bf16[128,2816]{1,0:T(8,128)(2,1)}, u32[]{:S(2)}, u32[]{:S(2)}) collective-permute-start(bf16[128,2816]{1,0:T(8,128)(2,1)} %get-tuple-element.92), channel_id=1, source_target_pairs={{0,8},{8,16},{16,24},{24,28},{28,20},{20,12},{12,4},{4,0},{1,9},{9... | collective-permute-start | bytes 2162696 | tf_op jit(solution)/shard_map/ppermute | solution.py:354
  233.1 29.3 %collective-permute-start.46 = (bf16[128,2816]{1,0:T(8,128)(2,1)}, bf16[128,2816]{1,0:T(8,128)(2,1)}, u32[]{:S(2)}, u32[]{:S(2)}) collective-permute-start(bf16[128,2816]{1,0:T(8,128)(2,1)} %get-tuple-element.90), channel_id=1, source_target_pairs={{0,4},{8,0},{16,8},{24,16},{28,24},{20,28},{12,20},{4,12},{1,5},{9... | collective-permute-start | bytes 2162696 | tf_op jit(solution)/shard_map/ppermute | solution.py:354
  264.0 26.8 %collective-permute-start.49 = (bf16[128,2816]{1,0:T(8,128)(2,1)S(1)}, bf16[128,2816]{1,0:T(8,128)(2,1)S(1)}, u32[]{:S(2)}, u32[]{:S(2)}) collective-permute-start(bf16[128,2816]{1,0:T(8,128)(2,1)S(1)} %get-tuple-element.93), channel_id=1, source_target_pairs={{0,8},{8,16},{16,24},{24,28},{28,20},{20,12},{12,4},{4,0},{1,9},{9... | collective-permute-start | bytes 2162696 | tf_op jit(solution)/shard_map/ppermute | solution.py:354
  264.9 25.9 %collective-permute-start.47 = (bf16[128,2816]{1,0:T(8,128)(2,1)S(1)}, bf16[128,2816]{1,0:T(8,128)(2,1)S(1)}, u32[]{:S(2)}, u32[]{:S(2)}) collective-permute-start(bf16[128,2816]{1,0:T(8,128)(2,1)S(1)} %get-tuple-element.91), channel_id=1, source_target_pairs={{0,4},{8,0},{16,8},{24,16},{28,24},{20,28},{12,20},{4,12},{1,5},{9... | collective-permute-start | bytes 2162696 | tf_op jit(solution)/shard_map/ppermute | solution.py:354
  268.7 24.2 %collective-permute-start.42 = (bf16[256,2048]{1,0:T(8,128)(2,1)S(1)}, bf16[256,2048]{1,0:T(8,128)(2,1)S(1)}, u32[]{:S(2)}, u32[]{:S(2)}) collective-permute-start(bf16[256,2048]{1,0:T(8,128)(2,1)S(1)} %slice.147), channel_id=1, source_target_pairs={{0,2},{1,3},{2,0},{3,1},{4,6},{5,7},{6,4},{7,5},{8,10},{9,11},{10,... | collective-permute-start | bytes 3145736 | tf_op jit(solution)/shard_map/ppermute | solution.py:359
  (71 other events, 769.6 us)

commit v7 on v6

--- a/solution.py
+++ b/solution.py
@@ -12,6 +12,7 @@
 AHEAD = (5, 10, 11)
 BACK = (11, 11, 4)
 VMEM_LIMIT = 40 * 1024 * 1024
+SUM_LIMIT = 52 * 1024 * 1024
 F32, BF16 = jnp.float32, jnp.bfloat16
 
 
@@ -38,8 +39,8 @@
     return np.concatenate([behind, ahead], axis=1).astype(np.int32)
 
 
-def params():
-    return pltpu.CompilerParams(vmem_limit_bytes=VMEM_LIMIT)
+def params(limit=VMEM_LIMIT):
+    return pltpu.CompilerParams(vmem_limit_bytes=limit)
 
 
 def cost(operations, moved):
@@ -267,7 +268,7 @@
             pltpu.VMEM((depth, tile), BF16),
             pltpu.SemaphoreType.DMA((count * len(parts),)),
         ],
-        compiler_params=params(),
+        compiler_params=params(SUM_LIMIT if sums else VMEM_LIMIT),
         cost_estimate=cost(
             2 * tokens * depth * width, 2 * (tokens + width) * depth + 8 * tokens * width
         ),

time: 325 us -> 323 us (level)
  other arithmetic: 25 us -> 20.9 us
    unnamed x73 -> x85, local copies, waits for them, and re-layouts: 9.29 us -> 6.74 us
  transfers between devices with their start and end apart: 59 -> 59, of which waited for: 29 -> 29; matrix products, arithmetic and copies ran while one was open for 10% -> 9% of each run, Pallas kernels for 30% -> 31%
where the time goes in v7:
time: 323 us; the launch traced here: 322 us
  waiting for transfers between devices  132 us (41%)
  Pallas kernels  101 us (31%)
  starting transfers between devices  51.7 us (16%)
  other arithmetic  20.9 us (6%)
  local copies, waits for them, and re-layouts  14.9 us (5%)
    ppermute x42, waiting for transfers between devices, send(): lax.ppermute(value, 'dp', [(cycle[i], cycle[(i + step) % ring]) for i in...  96.7 us
    pallas_call x2, Pallas kernels, forward_product(): pl.pallas_call(lambda *refs: forward_kernel([count] * len(parts), bits, s...  45.2 us
    pallas_call x3, Pallas kernels, backward_product(): pl.pallas_call(lambda *refs: backward_kernel(start // BLOCK, *refs), grid...  43.6 us
    ppermute x42, starting transfers between devices, send(): lax.ppermute(value, 'dp', [(cycle[i], cycle[(i + step) % ring]) for i in...  43.3 us
    ppermute x17, waiting for transfers between devices, partner(): lax.ppermute(value, 'tensor', [(i, i ^ 1 << bit) for i in range(groups)])  35.6 us
    convert_element_type x9, other arithmetic, outgoing(): return (self.sums[step].astype(F32) + term.astype(F32)).astype(BF16)  11.4 us
    ppermute x17, starting transfers between devices, partner(): lax.ppermute(value, 'tensor', [(i, i ^ 1 << bit) for i in range(groups)])  8.43 us
    pallas_call x3, Pallas kernels, local_grads(): pl.pallas_call(lambda *refs: grads_kernel(scale, tile, *refs), grid=(cols...  7.1 us
  transfers between devices with their start and end apart: 59, of which 29 were waited for; matrix products, arithmetic and copies ran while one was open for 9% of the time, Pallas kernels for 31%

profile of v7, /device:TPU:0, one launch (start us, length us, event | category | flops | bytes accessed | tf_op | source)
XLA Modules:
  0.0 321.7 jit_solution(8476857383367106149)
XLA Ops:
  2.0 3.0 collective-permute-start
  5.1 7.7 %collective-permute-done = bf16[128,1280]{1,0:T(8,128)(2,1)S(1)} collective-permute-done((bf16[128,1280]{1,0:T(8,128)(2,1)S(1)}, bf16[128,1280]{1,0:T(8,128)(2,1)S(1)}, u32[]{:S(2)}, u32[]{:S(2)}) %collective-permute-start) | collective-permute-done | bytes 327712 | tf_op jit(solution)/shard_map/ppermute | solution.py:360
  22.2 7.8 %collective-permute-done.5.refs_10_ = bf16[128,1280]{1,0:T(8,128)(2,1)S(1)} collective-permute-done((bf16[128,1280]{1,0:T(8,128)(2,1)S(1)}, bf16[128,1280]{1,0:T(8,128)(2,1)S(1)}, u32[]{:S(2)}, u32[]{:S(2)}) %collective-permute-start.5) | collective-permute-done | bytes 327712 | tf_op jit(solution)/shard_map/ppermute | solution.py:355
  34.8 4.3 %collective-permute-done.6.refs_9_ = bf16[128,1280]{1,0:T(8,128)(2,1)S(1)} collective-permute-done((bf16[128,1280]{1,0:T(8,128)(2,1)S(1)}, bf16[128,1280]{1,0:T(8,128)(2,1)S(1)}, u32[]{:S(2)}, u32[]{:S(2)}) %collective-permute-start.6) | collective-permute-done | bytes 327712 | tf_op jit(solution)/shard_map/ppermute | solution.py:355
  43.4 5.9 %collective-permute-done.9.refs_6_ = bf16[128,1280]{1,0:T(8,128)(2,1)S(1)} collective-permute-done((bf16[128,1280]{1,0:T(8,128)(2,1)S(1)}, bf16[128,1280]{1,0:T(8,128)(2,1)S(1)}, u32[]{:S(2)}, u32[]{:S(2)}) %collective-permute-start.9) | collective-permute-done | bytes 327712 | tf_op jit(solution)/shard_map/ppermute | solution.py:355
  52.5 4.1 %collective-permute-done.7 = bf16[128,2816]{1,0:T(8,128)(2,1)S(1)} collective-permute-done((bf16[128,2816]{1,0:T(8,128)(2,1)S(1)}, bf16[128,2816]{1,0:T(8,128)(2,1)S(1)}, u32[]{:S(2)}, u32[]{:S(2)}) %collective-permute-start.7) | collective-permute-done | bytes 720928 | tf_op jit(solution)/shard_map/ppermute | solution.py:360
  60.9 3.2 collective-permute-done.14.refs_18_
  65.1 5.9 %collective-permute-done.13.refs_12_ = bf16[128,2560]{1,0:T(8,128)(2,1)S(1)} collective-permute-done((bf16[128,2560]{1,0:T(8,128)(2,1)S(1)}, bf16[128,2560]{1,0:T(8,128)(2,1)S(1)}, u32[]{:S(2)}, u32[]{:S(2)}) %collective-permute-start.13) | collective-permute-done | bytes 655392 | tf_op jit(solution)/shard_map/ppermute | solution.py:355
  72.9 6.3 %collective-permute-done.18.refs_4_ = bf16[256,2048]{1,0:T(8,128)(2,1)} collective-permute-done((bf16[256,2048]{1,0:T(8,128)(2,1)}, bf16[256,2048]{1,0:T(8,128)(2,1)}, u32[]{:S(2)}, u32[]{:S(2)}) %collective-permute-start.18) | collective-permute-done | bytes 1048608 | tf_op jit(solution)/shard_map/ppermute | solution.py:360
  87.5 11.1 %collective-permute-done.22.refs_10_ = bf16[128,2816]{1,0:T(8,128)(2,1)} collective-permute-done((bf16[128,2816]{1,0:T(8,128)(2,1)}, bf16[128,2816]{1,0:T(8,128)(2,1)}, u32[]{:S(2)}, u32[]{:S(2)}) %collective-permute-start.22) | collective-permute-done | bytes 720928 | tf_op jit(solution)/shard_map/ppermute | solution.py:355
  104.1 17.6 %backward_product.3 = bf16[1024,2816]{1,0:T(8,128)(2,1)} custom-call(f32[52,16]{1,0:T(8,128)S(1)} %copy.14.refs_0_.refs_2_, bf16[1024,2048]{1,0:T(8,128)(2,1)S(1)} %arrange_rows.1.refs_1_, bf16[6656,2048]{1,0:T(8,128)(2,1)} %refs_2_.8), custom_call_target="tpu_custom_call" | custom-call | flops 738197504 | bytes 1343488 | tf_op jit(solution)/shard_map/backward_product/pallas_call | solution.py:173
  127.9 3.9 %collective-permute-done.16.refs_5_ = bf16[128,2816]{1,0:T(8,128)(2,1)S(1)} collective-permute-done((bf16[128,2816]{1,0:T(8,128)(2,1)}, bf16[128,2816]{1,0:T(8,128)(2,1)S(1)}, u32[]{:S(2)}, u32[]{:S(2)}) %collective-permute-start.16) | collective-permute-done | bytes 720928 | tf_op jit(solution)/shard_map/ppermute | solution.py:355
  133.9 17.8 %backward_product.4 = bf16[1024,2816]{1,0:T(8,128)(2,1)} custom-call(f32[52,16]{1,0:T(8,128)S(1)} %copy.14.refs_0_.refs_2_, bf16[1024,2048]{1,0:T(8,128)(2,1)S(1)} %arrange_rows.1.refs_1_, bf16[6656,2048]{1,0:T(8,128)(2,1)} %refs_2_.8), custom_call_target="tpu_custom_call" | custom-call | flops 738197504 | bytes 1343488 | tf_op jit(solution)/shard_map/backward_product/pallas_call | solution.py:173
  153.3 2.9 fusion.15
  159.7 3.1 collective-permute-done.23.refs_6_
  164.0 25.0 %forward_product.2.refs_12_ = f32[1024,2048]{1,0:T(8,128)} custom-call(s32[1]{0:T(128)} %bitcast.refs_0_, s32[16]{0:T(128)S(1)} %dynamic-slice_bitcast_fusion.refs_1_, f32[52,16]{1,0:T(8,128)S(1)} %copy.14.refs_0_.refs_2_, bf16[128,1280]{1,0:T(8,128)(2,1)S(1)} %copy-done.5, bf16[128,1280]{1,0:T(8,128)(2,1)S(1)} %copy-done.18, ...), custom_call_target="tpu_custom_call" | custom-call | flops 1006632960 | bytes 2523136 | tf_op jit(solution)/shard_map/forward_product/pallas_call | solution.py:251
  197.2 20.2 %forward_product.3 = bf16[1024,2048]{1,0:T(8,128)(2,1)} custom-call(s32[1]{0:T(128)} %bitcast.refs_0_, s32[16]{0:T(128)S(1)} %dynamic-slice_bitcast_fusion.refs_1_, f32[52,16]{1,0:T(8,128)S(1)} %copy.14.refs_0_.refs_2_, bf16[128,2816]{1,0:T(8,128)(2,1)} %local_mix.5.refs_3_, bf16[128,2816]{1,0:T(8,128)(2,1)} %collective-permute-done.15.refs_4_, ...), custom_call_target="tpu_custom_call" | custom-call | flops 738197504 | bytes 2129920 | tf_op jit(solution)/shard_map/forward_product/pallas_call | solution.py:251
  219.3 4.8 %collective-permute-done.34 = bf16[128,2816]{1,0:T(8,128)(2,1)S(1)} collective-permute-done((bf16[128,2816]{1,0:T(8,128)(2,1)}, bf16[128,2816]{1,0:T(8,128)(2,1)S(1)}, u32[]{:S(2)}, u32[]{:S(2)}) %collective-permute-start.34) | collective-permute-done | bytes 720928 | tf_op jit(solution)/shard_map/ppermute | solution.py:355
  233.2 8.2 %backward_product.5 = bf16[1024,1024]{1,0:T(8,128)(2,1)} custom-call(f32[52,16]{1,0:T(8,128)S(1)} %copy.14.refs_0_.refs_2_, bf16[1024,2048]{1,0:T(8,128)(2,1)S(1)} %arrange_rows.1.refs_1_, bf16[6656,2048]{1,0:T(8,128)(2,1)} %refs_2_.8), custom_call_target="tpu_custom_call" | custom-call | flops 268435456 | bytes 655360 | tf_op jit(solution)/shard_map/backward_product/pallas_call | solution.py:173
  241.4 4.1 %collective-permute-done.40 = bf16[128,2816]{1,0:T(8,128)(2,1)S(1)} collective-permute-done((bf16[128,2816]{1,0:T(8,128)(2,1)S(1)}, bf16[128,2816]{1,0:T(8,128)(2,1)S(1)}, u32[]{:S(2)}, u32[]{:S(2)}) %collective-permute-start.40) | collective-permute-done | bytes 720928 | tf_op jit(solution)/shard_map/ppermute | solution.py:355
  248.1 12.4 %collective-permute-done.48 = bf16[128,2816]{1,0:T(8,128)(2,1)S(1)} collective-permute-done((bf16[128,2816]{1,0:T(8,128)(2,1)S(1)}, bf16[128,2816]{1,0:T(8,128)(2,1)S(1)}, u32[]{:S(2)}, u32[]{:S(2)}) %collective-permute-start.48) | collective-permute-done | bytes 720928 | tf_op jit(solution)/shard_map/ppermute | solution.py:355
  267.6 18.1 %collective-permute-done.51 = bf16[128,1024]{1,0:T(8,128)(2,1)S(1)} collective-permute-done((bf16[128,1024]{1,0:T(8,128)(2,1)S(1)}, bf16[128,1024]{1,0:T(8,128)(2,1)S(1)}, u32[]{:S(2)}, u32[]{:S(2)}) %collective-permute-start.51) | collective-permute-done | bytes 262176 | tf_op jit(solution)/shard_map/ppermute | solution.py:355
  298.5 10.2 %collective-permute-done.54 = bf16[128,2816]{1,0:T(8,128)(2,1)S(1)} collective-permute-done((bf16[128,2816]{1,0:T(8,128)(2,1)S(1)}, bf16[128,2816]{1,0:T(8,128)(2,1)S(1)}, u32[]{:S(2)}, u32[]{:S(2)}) %collective-permute-start.54) | collective-permute-done | bytes 720928 | tf_op jit(solution)/shard_map/ppermute | solution.py:360
  314.8 3.2 collective-permute-done.55
  (220 shorter events, 109.8 us)
Async XLA Ops:
  56.6 22.7 %collective-permute-start.18 = (bf16[256,2048]{1,0:T(8,128)(2,1)}, bf16[256,2048]{1,0:T(8,128)(2,1)}, u32[]{:S(2)}, u32[]{:S(2)}) collective-permute-start(bf16[256,2048]{1,0:T(8,128)(2,1)} %refs_2_.5), channel_id=1, source_target_pairs={{0,2},{1,3},{2,0},{3,1},{4,6},{5,7},{6,4},{7,5},{8,10},{9,11},{10,... | collective-permute-start | bytes 3145736 | tf_op jit(solution)/shard_map/ppermute | solution.py:360
  72.9 28.3 %collective-permute-start.17 = (bf16[256,2048]{1,0:T(8,128)(2,1)}, bf16[256,2048]{1,0:T(8,128)(2,1)}, u32[]{:S(2)}, u32[]{:S(2)}) collective-permute-start(bf16[256,2048]{1,0:T(8,128)(2,1)} %refs_2_.5), channel_id=1, source_target_pairs={{0,1},{1,0},{2,3},{3,2},{4,5},{5,4},{6,7},{7,6},{8,9},{9,8},{10,11... | collective-permute-start | bytes 3145736 | tf_op jit(solution)/shard_map/ppermute | solution.py:360
  79.3 22.4 %collective-permute-start.19 = (bf16[256,2048]{1,0:T(8,128)(2,1)}, bf16[256,2048]{1,0:T(8,128)(2,1)}, u32[]{:S(2)}, u32[]{:S(2)}) collective-permute-start(bf16[256,2048]{1,0:T(8,128)(2,1)} %collective-permute-done.18.refs_4_), channel_id=1, source_target_pairs={{0,1},{1,0},{2,3},{3,2},{4,5},{5,4},{6,7},{7,6},{8,9},{9,8},{10,11... | collective-permute-start | bytes 3145736 | tf_op jit(solution)/shard_map/ppermute | solution.py:360
  85.1 36.6 %collective-permute-start.24 = (bf16[128,2560]{1,0:T(8,128)(2,1)}, bf16[128,2560]{1,0:T(8,128)(2,1)}, u32[]{:S(2)}, u32[]{:S(2)}) collective-permute-start(bf16[128,2560]{1,0:T(8,128)(2,1)} %collective-permute-done.20.refs_17_), channel_id=1, source_target_pairs={{0,4},{8,0},{16,8},{24,16},{28,24},{20,28},{12,20},{4,12},{1,5},{9... | collective-permute-start | bytes 1966088 | tf_op jit(solution)/shard_map/ppermute | solution.py:355
  98.5 29.4 %collective-permute-start.25 = (bf16[128,2560]{1,0:T(8,128)(2,1)}, bf16[128,2560]{1,0:T(8,128)(2,1)S(1)}, u32[]{:S(2)}, u32[]{:S(2)}) collective-permute-start(bf16[128,2560]{1,0:T(8,128)(2,1)} %copy-done.13), channel_id=1, source_target_pairs={{0,8},{8,16},{16,24},{24,28},{28,20},{20,12},{12,4},{4,0},{1,9},{9... | collective-permute-start | bytes 1966088 | tf_op jit(solution)/shard_map/ppermute | solution.py:355
  99.6 28.3 %collective-permute-start.26 = (bf16[128,2816]{1,0:T(8,128)(2,1)}, bf16[128,2816]{1,0:T(8,128)(2,1)S(1)}, u32[]{:S(2)}, u32[]{:S(2)}) collective-permute-start(bf16[128,2816]{1,0:T(8,128)(2,1)} %collective-permute-done.22.refs_10_), channel_id=1, source_target_pairs={{0,4},{8,0},{16,8},{24,16},{28,24},{20,28},{12,20},{4,12},{1,5},{9... | collective-permute-start | bytes 2162696 | tf_op jit(solution)/shard_map/ppermute | solution.py:355
  101.2 30.6 %collective-permute-start.16 = (bf16[128,2816]{1,0:T(8,128)(2,1)}, bf16[128,2816]{1,0:T(8,128)(2,1)S(1)}, u32[]{:S(2)}, u32[]{:S(2)}) collective-permute-start(bf16[128,2816]{1,0:T(8,128)(2,1)} %collective-permute-done.15.refs_4_), channel_id=1, source_target_pairs={{0,8},{8,16},{16,24},{24,28},{28,20},{20,12},{12,4},{4,0},{1,9},{9... | collective-permute-start | bytes 2162696 | tf_op jit(solution)/shard_map/ppermute | solution.py:355
  121.7 37.5 %collective-permute-start.32 = (bf16[128,2560]{1,0:T(8,128)(2,1)}, bf16[128,2560]{1,0:T(8,128)(2,1)S(1)}, u32[]{:S(2)}, u32[]{:S(2)}) collective-permute-start(bf16[128,2560]{1,0:T(8,128)(2,1)} %collective-permute-done.24.refs_16_), channel_id=1, source_target_pairs={{0,4},{8,0},{16,8},{24,16},{28,24},{20,28},{12,20},{4,12},{1,5},{9... | collective-permute-start | bytes 1966088 | tf_op jit(solution)/shard_map/ppermute | solution.py:355
  125.9 30.4 %collective-permute-start.29 = (bf16[128,2816]{1,0:T(8,128)(2,1)S(1)}, bf16[128,2816]{1,0:T(8,128)(2,1)S(1)}, u32[]{:S(2)}, u32[]{:S(2)}) collective-permute-start(bf16[128,2816]{1,0:T(8,128)(2,1)S(1)} %get-tuple-element.70), channel_id=1, source_target_pairs={{0,8},{8,16},{16,24},{24,28},{28,20},{20,12},{12,4},{4,0},{1,9},{9... | collective-permute-start | bytes 2162696 | tf_op jit(solution)/shard_map/ppermute | solution.py:355
  131.8 30.9 %collective-permute-start.23 = (bf16[128,2816]{1,0:T(8,128)(2,1)S(1)}, bf16[128,2816]{1,0:T(8,128)(2,1)S(1)}, u32[]{:S(2)}, u32[]{:S(2)}) collective-permute-start(bf16[128,2816]{1,0:T(8,128)(2,1)S(1)} %collective-permute-done.16.refs_5_), channel_id=1, source_target_pairs={{0,8},{8,16},{16,24},{24,28},{28,20},{20,12},{12,4},{4,0},{1,9},{9... | collective-permute-start | bytes 2162696 | tf_op jit(solution)/shard_map/ppermute | solution.py:355
  132.7 30.0 %collective-permute-start.33 = (bf16[128,2816]{1,0:T(8,128)(2,1)S(1)}, bf16[128,2816]{1,0:T(8,128)(2,1)S(1)}, u32[]{:S(2)}, u32[]{:S(2)}) collective-permute-start(bf16[128,2816]{1,0:T(8,128)(2,1)S(1)} %collective-permute-done.26.refs_9_), channel_id=1, source_target_pairs={{0,4},{8,0},{16,8},{24,16},{28,24},{20,28},{12,20},{4,12},{1,5},{9... | collective-permute-start | bytes 2162696 | tf_op jit(solution)/shard_map/ppermute | solution.py:355
  151.7 40.7 %collective-permute-start.28 = (bf16[128,2816]{1,0:T(8,128)(2,1)S(1)}, bf16[128,2816]{1,0:T(8,128)(2,1)S(1)}, u32[]{:S(2)}, u32[]{:S(2)}) collective-permute-start(bf16[128,2816]{1,0:T(8,128)(2,1)S(1)} %get-tuple-element.69), channel_id=1, source_target_pairs={{0,4},{8,0},{16,8},{24,16},{28,24},{20,28},{12,20},{4,12},{1,5},{9... | collective-permute-start | bytes 2162696 | tf_op jit(solution)/shard_map/ppermute | solution.py:355
  156.2 32.7 %collective-permute-start.31 = (bf16[128,2816]{1,0:T(8,128)(2,1)S(1)}, bf16[128,2816]{1,0:T(8,128)(2,1)S(1)}, u32[]{:S(2)}, u32[]{:S(2)}) collective-permute-start(bf16[128,2816]{1,0:T(8,128)(2,1)S(1)} %get-tuple-element.72), channel_id=1, source_target_pairs={{0,4},{8,0},{16,8},{24,16},{28,24},{20,28},{12,20},{4,12},{1,5},{9... | collective-permute-start | bytes 2162696 | tf_op jit(solution)/shard_map/ppermute | solution.py:355
  159.2 33.2 %collective-permute-start.30 = (bf16[128,2816]{1,0:T(8,128)(2,1)S(1)}, bf16[128,2816]{1,0:T(8,128)(2,1)S(1)}, u32[]{:S(2)}, u32[]{:S(2)}) collective-permute-start(bf16[128,2816]{1,0:T(8,128)(2,1)S(1)} %add_convert_fusion.15), channel_id=1, source_target_pairs={{0,8},{8,16},{16,24},{24,28},{28,20},{20,12},{12,4},{4,0},{1,9},{9... | collective-permute-start | bytes 2162696 | tf_op jit(solution)/shard_map/ppermute | solution.py:355
  162.7 34.4 %collective-permute-start.27 = (bf16[128,2816]{1,0:T(8,128)(2,1)S(1)}, bf16[128,2816]{1,0:T(8,128)(2,1)}, u32[]{:S(2)}, u32[]{:S(2)}) collective-permute-start(bf16[128,2816]{1,0:T(8,128)(2,1)S(1)} %collective-permute-done.23.refs_6_), channel_id=1, source_target_pairs={{0,8},{8,16},{16,24},{24,28},{28,20},{20,12},{12,4},{4,0},{1,9},{9... | collective-permute-start | bytes 2162696 | tf_op jit(solution)/shard_map/ppermute | solution.py:355
  190.3 29.0 %collective-permute-start.37 = (bf16[128,2816]{1,0:T(8,128)(2,1)S(1)}, bf16[128,2816]{1,0:T(8,128)(2,1)S(1)}, u32[]{:S(2)}, u32[]{:S(2)}) collective-permute-start(bf16[128,2816]{1,0:T(8,128)(2,1)S(1)} %add_convert_fusion.12), channel_id=1, source_target_pairs={{0,4},{8,0},{16,8},{24,16},{28,24},{20,28},{12,20},{4,12},{1,5},{9... | collective-permute-start | bytes 2162696 | tf_op jit(solution)/shard_map/ppermute | solution.py:355
  191.5 27.8 %collective-permute-start.36 = (bf16[128,2816]{1,0:T(8,128)(2,1)}, bf16[128,2816]{1,0:T(8,128)(2,1)S(1)}, u32[]{:S(2)}, u32[]{:S(2)}) collective-permute-start(bf16[128,2816]{1,0:T(8,128)(2,1)} %get-tuple-element.79), channel_id=1, source_target_pairs={{0,8},{8,16},{16,24},{24,28},{28,20},{20,12},{12,4},{4,0},{1,9},{9... | collective-permute-start | bytes 2162696 | tf_op jit(solution)/shard_map/ppermute | solution.py:355
  195.1 28.9 %collective-permute-start.34 = (bf16[128,2816]{1,0:T(8,128)(2,1)}, bf16[128,2816]{1,0:T(8,128)(2,1)S(1)}, u32[]{:S(2)}, u32[]{:S(2)}) collective-permute-start(bf16[128,2816]{1,0:T(8,128)(2,1)} %get-tuple-element.77), channel_id=1, source_target_pairs={{0,8},{8,16},{16,24},{24,28},{28,20},{20,12},{12,4},{4,0},{1,9},{9... | collective-permute-start | bytes 2162696 | tf_op jit(solution)/shard_map/ppermute | solution.py:355
  196.7 27.4 %collective-permute-start.35 = (bf16[128,2816]{1,0:T(8,128)(2,1)}, bf16[128,2816]{1,0:T(8,128)(2,1)}, u32[]{:S(2)}, u32[]{:S(2)}) collective-permute-start(bf16[128,2816]{1,0:T(8,128)(2,1)} %get-tuple-element.78), channel_id=1, source_target_pairs={{0,4},{8,0},{16,8},{24,16},{28,24},{20,28},{12,20},{4,12},{1,5},{9... | collective-permute-start | bytes 2162696 | tf_op jit(solution)/shard_map/ppermute | solution.py:355
  230.2 30.3 %collective-permute-start.48 = (bf16[128,2816]{1,0:T(8,128)(2,1)S(1)}, bf16[128,2816]{1,0:T(8,128)(2,1)S(1)}, u32[]{:S(2)}, u32[]{:S(2)}) collective-permute-start(bf16[128,2816]{1,0:T(8,128)(2,1)S(1)} %get-tuple-element.92), channel_id=1, source_target_pairs={{0,8},{8,16},{16,24},{24,28},{28,20},{20,12},{12,4},{4,0},{1,9},{9... | collective-permute-start | bytes 2162696 | tf_op jit(solution)/shard_map/ppermute | solution.py:355
  230.7 29.8 %collective-permute-start.46 = (bf16[128,2816]{1,0:T(8,128)(2,1)S(1)}, bf16[128,2816]{1,0:T(8,128)(2,1)S(1)}, u32[]{:S(2)}, u32[]{:S(2)}) collective-permute-start(bf16[128,2816]{1,0:T(8,128)(2,1)S(1)} %get-tuple-element.90), channel_id=1, source_target_pairs={{0,4},{8,0},{16,8},{24,16},{28,24},{20,28},{12,20},{4,12},{1,5},{9... | collective-permute-start | bytes 2162696 | tf_op jit(solution)/shard_map/ppermute | solution.py:355
  262.1 26.9 %collective-permute-start.49 = (bf16[128,2816]{1,0:T(8,128)(2,1)S(1)}, bf16[128,2816]{1,0:T(8,128)(2,1)S(1)}, u32[]{:S(2)}, u32[]{:S(2)}) collective-permute-start(bf16[128,2816]{1,0:T(8,128)(2,1)S(1)} %get-tuple-element.93), channel_id=1, source_target_pairs={{0,8},{8,16},{16,24},{24,28},{28,20},{20,12},{12,4},{4,0},{1,9},{9... | collective-permute-start | bytes 2162696 | tf_op jit(solution)/shard_map/ppermute | solution.py:355
  262.8 26.2 %collective-permute-start.47 = (bf16[128,2816]{1,0:T(8,128)(2,1)S(1)}, bf16[128,2816]{1,0:T(8,128)(2,1)S(1)}, u32[]{:S(2)}, u32[]{:S(2)}) collective-permute-start(bf16[128,2816]{1,0:T(8,128)(2,1)S(1)} %get-tuple-element.91), channel_id=1, source_target_pairs={{0,4},{8,0},{16,8},{24,16},{28,24},{20,28},{12,20},{4,12},{1,5},{9... | collective-permute-start | bytes 2162696 | tf_op jit(solution)/shard_map/ppermute | solution.py:355
  267.0 24.2 %collective-permute-start.42 = (bf16[256,2048]{1,0:T(8,128)(2,1)S(1)}, bf16[256,2048]{1,0:T(8,128)(2,1)S(1)}, u32[]{:S(2)}, u32[]{:S(2)}) collective-permute-start(bf16[256,2048]{1,0:T(8,128)(2,1)S(1)} %slice.147), channel_id=1, source_target_pairs={{0,2},{1,3},{2,0},{3,1},{4,6},{5,7},{6,4},{7,5},{8,10},{9,11},{10,... | collective-permute-start | bytes 3145736 | tf_op jit(solution)/shard_map/ppermute | solution.py:360
  (77 other events, 903.7 us)
